TPU v7x, 1024 devices: a whole 8x8x8 slice. The times are simulated.
1024 devices in a mesh: dp: 16 (over x, core), loss: 16 (over z_lo, y), mp: 4 (over z_hi).
Axes of the slice: x: 8, y: 8, z: 8 (z_hi: 4, z_lo: 2; z = z_hi * 2 + z_lo), core: 2. Of those that a mesh axis runs over, the one named last changes fastest.
Arguments:
- patches: bfloat16 [81920, 1152], P(('dp', 'loss'))
- layer_norm_gain: float32 [1152], replicated, may hold values from 0.5 to 1.5
- layer_norm_bias: float32 [1152], replicated, may hold values from -1.75 to 1.75
- fc1_weight: bfloat16 [1152, 4304], P(None, 'mp'), may hold values from -0.1875 to 0.1875
- fc1_bias: float32 [4304], P('mp'), may hold values from -1.75 to 1.75
- fc2_weight: bfloat16 [4304, 1152], P('mp'), may hold values from -0.09375 to 0.09375
- counts: int32 [16, 8], P('loss'), may hold values from 256 to 1024, as said below
- owners: int32 [16, 16, 16], P('loss'), may hold values from 0 to 15, each once within a row
- text_embed: bfloat16 [128, 1152], P('loss'), may hold values from -0.1875 to 0.1875
- labels: int32 [128], replicated, may hold values from 0 to 127, each once
- logit_scale: float32 [1], replicated, may hold values from 5 to 20
- logit_bias: float32 [1], replicated, may hold values from -6 to -3
Outputs:
- grad_rows: float32 [81920, 1152], P(('dp', 'loss', 'mp'))
- grad_text: float32 [128, 1152], P('loss')
- loss: float32 [], replicated
Inputs may be any that keep to these rules, and one draw needn't show every extreme that they name: In each pair group the counts add up to 5120; one image of every group has exactly 1024 patches and one exactly 256. For each group and source, the owners of the 16 blocks are all different. `labels`: each text matches exactly one image.
All inputs are finite; a program needn't handle non-finite values.
Results may differ from a plain program's by a relative error of at most 0.015.
Values may be sent and summed in bfloat16 or wider, within the bound.
No kernel may reach another device: no remote copies, remote signals or barrier semaphores. Data moves between devices by JAX's collectives and lax.ppermute only.
A program may use at most 32 MiB of HBM per device.

v0:
```python
import jax
import jax.numpy as jnp
from jax import lax
from jax.sharding import PartitionSpec as P

eps = 1e-06
grad_scale = 262144.0
gelu_coef = 0.7978845608028654


def gelu_tanh(values):
    inner = gelu_coef * (values + 0.044715 * values * values * values)
    return 0.5 * values * (1.0 + jnp.tanh(inner))


def gelu_slope(values):
    inner = gelu_coef * (values + 0.044715 * values * values * values)
    tanh_part = jnp.tanh(inner)
    return 0.5 * (1.0 + tanh_part) + 0.5 * values * (1.0 - tanh_part * tanh_part) * gelu_coef * (
        1.0 + 0.134145 * values * values
    )


def layer_statistics(rows_in):
    floats = rows_in.astype(jnp.float32)
    center = floats - jnp.mean(floats, axis=-1, keepdims=True)
    spread = jnp.mean(center * center, axis=-1, keepdims=True)
    inverse_deviation = lax.rsqrt(spread + eps)
    return (center * inverse_deviation, inverse_deviation)


def reduce_rows(term, shared_rows):
    return lax.psum_scatter(
        term(jnp.int32(0), shared_rows * lax.axis_size("mp")).astype(jnp.bfloat16),
        "mp",
        scatter_dimension=0,
        tiled=True,
    ).astype(jnp.float32)


def shards(
    patches,
    layer_norm_gain,
    layer_norm_bias,
    fc1_weight,
    fc1_bias,
    fc2_weight,
    counts,
    owners,
    text_embed,
    labels,
    logit_scale,
    logit_bias,
):
    dp_size = lax.axis_size("dp")
    mp_size = lax.axis_size("mp")
    dp_index = lax.axis_index("dp")
    mp_index = lax.axis_index("mp")
    row_count, feat_width = patches.shape
    block_rows = row_count // dp_size
    plan = owners[0]
    outgoing = patches.reshape(dp_size, block_rows, feat_width)[jnp.argsort(plan[dp_index])]
    incoming = lax.all_to_all(outgoing, "dp", split_axis=0, concat_axis=0, tiled=True)
    local_rows = incoming.reshape(row_count, feat_width)
    slots = jnp.arange(dp_size, dtype=jnp.int32)
    source_block = jnp.sum(jnp.where(plan == dp_index, slots[None, :], 0), axis=1)
    position = (
        slots[:, None] * row_count
        + source_block[:, None] * block_rows
        + jnp.arange(block_rows, dtype=jnp.int32)[None, :]
    ).reshape(row_count)
    count_row = counts[0]
    ends = jnp.cumsum(count_row)
    starts = ends - count_row
    member = ((position[:, None] >= starts[None, :]) & (position[:, None] < ends[None, :])).astype(
        jnp.float32
    )
    count_float = count_row.astype(jnp.float32)[:, None]
    normalized_input, inverse_deviation = layer_statistics(local_rows)
    normalized_rows = (normalized_input * layer_norm_gain + layer_norm_bias).astype(jnp.bfloat16)
    pre = jnp.dot(normalized_rows, fc1_weight, preferred_element_type=jnp.float32) + fc1_bias
    act = gelu_tanh(pre).astype(jnp.bfloat16)

    def forward_term(first_row, many):
        return jnp.dot(act, fc2_weight, preferred_element_type=jnp.float32)

    shared_rows = row_count // mp_size
    first_index = mp_index * shared_rows
    mixed = reduce_rows(forward_term, shared_rows)
    output_share = (
        lax.dynamic_slice_in_dim(local_rows, first_index, shared_rows, 0).astype(jnp.float32)
        + mixed
    )
    member_share = lax.dynamic_slice_in_dim(member, first_index, shared_rows, 0)
    partial_sums = jnp.dot(member_share.T, output_share, precision=lax.Precision.HIGHEST)
    image_sums = lax.psum(partial_sums, ("dp", "mp"))
    embeds = image_sums / count_float
    all_embeds, all_texts = (
        lax.all_gather(embeds.astype(jnp.bfloat16), "loss", axis=0, tiled=True).astype(
            embeds.dtype
        ),
        lax.all_gather(
            text_embed.astype(jnp.float32).astype(jnp.bfloat16), "loss", axis=0, tiled=True
        ).astype(jnp.float32),
    )
    total_images = all_embeds.shape[0]
    group_images = embeds.shape[0]
    norm_e = jnp.sqrt(jnp.sum(all_embeds * all_embeds, axis=-1, keepdims=True) + eps)
    unit_e = all_embeds / norm_e
    norm_t = jnp.sqrt(jnp.sum(all_texts * all_texts, axis=-1, keepdims=True) + eps)
    unit_t = all_texts / norm_t
    score = (
        logit_scale[0] * jnp.dot(unit_e, unit_t.T, precision=lax.Precision.HIGHEST) + logit_bias[0]
    )
    sign = jnp.where(
        labels[:, None] == jnp.arange(total_images, dtype=jnp.int32)[None, :], 1.0, -1.0
    ).astype(jnp.float32)
    loss = -jnp.sum(jax.nn.log_sigmoid(sign * score)) / total_images
    dscore = -sign * jax.nn.sigmoid(-sign * score) / total_images
    d_unit_e = logit_scale[0] * jnp.dot(dscore, unit_t, precision=lax.Precision.HIGHEST)
    d_unit_t = logit_scale[0] * jnp.dot(dscore.T, unit_e, precision=lax.Precision.HIGHEST)
    dembed = (d_unit_e - unit_e * jnp.sum(unit_e * d_unit_e, axis=-1, keepdims=True)) / norm_e
    text_grads = (d_unit_t - unit_t * jnp.sum(unit_t * d_unit_t, axis=-1, keepdims=True)) / norm_t
    group_first = lax.axis_index("loss") * group_images
    dembed_group = lax.dynamic_slice_in_dim(dembed, group_first, group_images, 0)
    grad_text = lax.dynamic_slice_in_dim(text_grads, group_first, group_images, 0)
    upstream = grad_scale * jnp.dot(
        member, dembed_group / count_float, precision=lax.Precision.HIGHEST
    )
    upstream_b = upstream.astype(jnp.bfloat16)
    d_act = jnp.dot(upstream_b, fc2_weight.T, preferred_element_type=jnp.float32)
    d_pre = (d_act * gelu_slope(pre)).astype(jnp.bfloat16)

    def backward_term(first_row, many):
        return jnp.dot(d_pre, fc1_weight.T, preferred_element_type=jnp.float32)

    backward_pass = reduce_rows(backward_term, shared_rows)
    normalized_share = lax.dynamic_slice_in_dim(normalized_input, first_index, shared_rows, 0)
    inv_share = lax.dynamic_slice_in_dim(inverse_deviation, first_index, shared_rows, 0)
    normalized_gradient = backward_pass * layer_norm_gain
    row_gradients = inv_share * (
        normalized_gradient
        - jnp.mean(normalized_gradient, axis=-1, keepdims=True)
        - normalized_share
        * jnp.mean(normalized_gradient * normalized_share, axis=-1, keepdims=True)
    )
    grad_rows = row_gradients + lax.dynamic_slice_in_dim(upstream, first_index, shared_rows, 0)
    return (grad_rows, grad_text, loss)


def solution(mesh):
    placed = (
        P(("dp", "loss"), None),
        P(),
        P(),
        P(None, "mp"),
        P("mp"),
        P("mp", None),
        P("loss", None),
        P("loss", None, None),
        P("loss", None),
        P(),
        P(),
        P(),
    )
    return jax.shard_map(
        shards,
        mesh=mesh,
        in_specs=placed,
        out_specs=(P(("dp", "loss", "mp"), None), P("loss", None), P()),
        check_vma=False,
    )
```

profile of v0, /device:TPU:1, one launch (start us, length us, event | category | flops | bytes accessed | tf_op | source)
XLA Modules:
  0.0 465.8 jit_solution(8114804956205594707)
XLA Ops:
  7.2 0.0 copy-start
  7.2 0.8 fusion.45
  8.0 1.2 sort.17
  9.3 1.3 reshape.130
  10.6 1.6 gather_fusion
  12.1 17.6 %all-to-all-start = ((bf16[16,20,1152]{2,1,0:T(8,128)(2,1)}), bf16[16,20,1152]{2,1,0:T(8,128)(2,1)S(1)}, u32[]{:S(2)}, u32[]{:S(2)}) async-start(bf16[16,20,1152]{2,1,0:T(8,128)(2,1)} %gather_fusion), calls=%async_computation | async-start | bytes 1769472 | tf_op jit(solution)/shard_map/all_to_all | solution.py:63
  29.7 0.0 reduce-scatter.3.cloned.1.call-start
  29.8 24.6 %all-to-all-done = bf16[16,20,1152]{2,1,0:T(8,128)(2,1)S(1)} async-done(((bf16[16,20,1152]{2,1,0:T(8,128)(2,1)}), bf16[16,20,1152]{2,1,0:T(8,128)(2,1)S(1)}, u32[]{:S(2)}, u32[]{:S(2)}) %all-to-all-start) | async-done | bytes 737312 | tf_op jit(solution)/shard_map/all_to_all | solution.py:63
  54.4 0.2 convert_reduce_fusion
  54.6 0.0 copy-start.4
  54.6 0.0 copy-start.10
  54.6 0.0 copy-start.11
  54.6 0.1 div.70
  54.7 0.4 fusion.2
  55.1 0.1 rsqrt.20
  55.2 1.0 reshape.133
  56.3 3.3 convolution_add_fusion
  59.5 0.0 copy-start.16
  59.6 1.1 copy-done.16
  60.7 2.3 convolution_convert_fusion.1
  63.0 0.0 reduce-scatter.3.cloned.1.call-update
  63.0 0.0 reduce-scatter.5.cloned.1.call-start
  63.1 0.1 select_reduce_fusion
  63.2 0.1 iota_add_fusion
  63.3 0.1 add.143
  63.4 0.0 copy-done.9
  63.4 0.2 reduce-window.4
  64.9 25.6 %all_gather.7 = bf16[128,1152]{1,0:T(8,128)(2,1)S(1)} all-gather(bf16[8,1152]{1,0:T(8,128)(2,1)} %param.20), channel_id=1, replica_groups=mesh['dp'=16,'loss'=16,'mp'=4] {'loss'}, dimensions={0}, use_global_device_ids=true | all-gather | bytes 313344 | tf_op jit(solution)/shard_map/all_gather | solution.py:102
  90.5 0.1 fusion.19
  90.6 0.6 add_sqrt_fusion
  91.2 1.2 convert_bitcast_fusion
  92.4 0.5 copy-done.7
  93.0 0.7 compare_and_fusion
  93.7 4.3 reduce-scatter.3.cloned.1.call-done
  98.0 0.0 copy-done.1
  98.0 1.8 fusion.21
  99.8 279.5 %psum.7 = f32[8,1152]{1,0:T(8,128)} all-reduce(f32[8,1152]{1,0:T(8,128)} %fusion.21), channel_id=1, replica_groups=mesh['dp'=16,'loss'=16,'mp'=4] {'dp','mp'}, use_global_device_ids=true, to_apply=%region_6.7 | all-reduce | flops 9216 | bytes 73728 | tf_op jit(solution)/shard_map/psum | solution.py:96
  379.3 0.8 divide_convert_fusion
  380.2 24.1 %all_gather.6 = bf16[128,1152]{1,0:T(8,128)(2,1)S(1)} all-gather(bf16[8,1152]{1,0:T(8,128)(2,1)S(1)} %divide_convert_fusion), channel_id=1, replica_groups=mesh['dp'=16,'loss'=16,'mp'=4] {'loss'}, dimensions={0}, use_global_device_ids=true | all-gather | bytes 313344 | tf_op jit(solution)/shard_map/all_gather | solution.py:99
  404.3 0.1 fusion.18
  404.5 0.1 dynamic-slice.2
  404.5 2.3 fusion.33
  406.8 0.0 copy-done.15
  406.8 0.0 copy-start.6
  406.8 0.0 copy-start.8
  406.8 0.9 multiply_reduce_fusion.1
  407.8 0.1 dynamic-slice.1
  407.8 0.0 copy-done.8
  407.8 1.9 convolution_multiply_fusion
  409.7 5.9 %convolution_convert_fusion = bf16[320,1152]{1,0:T(8,128)(2,1)} fusion(bf16[1152,1076]{0,1:T(8,128)(2,1)} %param.15, bf16[1076,1152]{1,0:T(8,128)(2,1)S(1)} %copy-done, f32[320,1076]{1,0:T(8,128)} %copy-done.16, f32[320,1152]{1,0:T(8,128)} %convolution_multiply_fusion), kind=kOutput, calls=%fused_computation.5 | convolution fusion | flops 1593905920 | bytes 8547328 | tf_op jit(solution)/shard_map/dot_general | solution.py:135
  415.6 0.0 reduce-scatter.5.cloned.1.call-update
  415.6 0.0 copy-done.14
  415.7 0.1 dynamic-slice.4
  415.7 0.1 rsqrt.19
  415.8 0.0 copy-start.3
  415.8 0.0 copy-start.18
  415.8 0.1 fusion.46
  415.9 1.4 subtract_multiply_fusion
  417.3 2.3 multiply_reduce_fusion
  419.6 0.1 dynamic-slice.3
  420.3 1.5 fusion.36
  421.8 32.7 %reduce-scatter.5.cloned.1.call-done = bf16[80,1152]{1,0:T(8,128)(2,1)} async-done(((bf16[320,1152]{1,0:T(8,128)(2,1)}), bf16[80,1152]{1,0:T(8,128)(2,1)}) %reduce-scatter.5.cloned.1.call-update) | async-done | bytes 184336 | tf_op jit(solution)/shard_map/reduce_scatter | solution.py:33
  454.5 1.2 fusion.20
  455.8 2.1 dynamic-slice_add_fusion
  (30 shorter events, 0.1 us)
Async XLA Ops:
  7.2 53.5 %copy-start = (bf16[1076,1152]{1,0:T(8,128)(2,1)S(1)}, bf16[1076,1152]{1,0:T(8,128)(2,1)}, u32[]{:S(2)}) copy-start(bf16[1076,1152]{1,0:T(8,128)(2,1)} %param.17) | copy-start | bytes 7437316
  12.1 42.3 %all-to-all-start = ((bf16[16,20,1152]{2,1,0:T(8,128)(2,1)}), bf16[16,20,1152]{2,1,0:T(8,128)(2,1)S(1)}, u32[]{:S(2)}, u32[]{:S(2)}) async-start(bf16[16,20,1152]{2,1,0:T(8,128)(2,1)} %gather_fusion), calls=%async_computation | async-start | bytes 1769472 | tf_op jit(solution)/shard_map/all_to_all | solution.py:63
  29.7 68.3 %reduce-scatter.3.cloned.1.call-start = ((), (), s32[]{:S(2)}) async-start(), calls=%async_computation.3 | async-start | bytes 921600 | tf_op jit(solution)/shard_map/reduce_scatter | solution.py:33
  54.6 1.7 copy-start.4
  54.6 1.7 copy-start.10
  54.6 1.7 copy-start.11
  59.5 1.1 copy-start.16
  60.7 2.4 copy-start.5
  60.7 2.7 copy-start.9
  63.0 35.0 %copy-start.1 = (bf16[320,1152]{1,0:T(8,128)(2,1)S(1)}, bf16[320,1152]{1,0:T(8,128)(2,1)}, u32[]{:S(2)}) copy-start(bf16[320,1152]{1,0:T(8,128)(2,1)} %reshape.133) | copy-start | bytes 2211844
  63.0 391.5 %reduce-scatter.5.cloned.1.call-start = ((), (), s32[]{:S(2)}) async-start(), calls=%async_computation.4 | async-start | bytes 921600 | tf_op jit(solution)/shard_map/reduce_scatter | solution.py:33
  92.4 0.5 copy-start.7
  404.3 2.5 copy-start.2
  404.5 2.3 copy-start.15
  404.5 2.3 copy-start.12
  404.5 2.3 copy-start.13
  406.8 0.9 copy-start.17
  406.8 1.0 copy-start.6
  406.8 1.0 copy-start.8
  409.7 5.9 %copy-start.14 = (f32[128]{0:T(128)S(1)}, f32[128]{0:T(128)}, u32[]{:S(2)}) copy-start(f32[128]{0:T(128)} %add_sqrt_fusion) | copy-start | bytes 1540
  415.8 1.5 copy-start.3
  415.8 1.5 copy-start.18
Sparse Core Ops, SparseCore 0:
  63.2 34.7 reduce-scatter.2
  415.8 38.7 reduce-scatter.4
where the time goes:
time: 467 us; the launch traced here: 466 us
  blocking collectives  329 us (70%)
  waiting for transfers between devices  61.7 us (13%)
  matrix products  20.6 us (4%)
  starting transfers between devices  17.6 us (4%)
  between operations  17.3 us (4%)
  other arithmetic  12.1 us (3%)
  local copies, waits for them, and re-layouts  7.2 us (2%)
    psum x1, blocking collectives, shards(): image_sums = lax.psum(partial_sums, ('dp', 'mp'))  280 us
    reduce_scatter x2, waiting for transfers between devices, reduce_rows(): lax.psum_scatter(term(jnp.int32(0), shared_rows * lax.axis_size('mp')).as...  37 us
    all_gather x1, blocking collectives, shards(): lax.all_gather(text_embed.astype(jnp.float32).astype(jnp.bfloat16), 'loss...  25.6 us
    all_to_all x1, waiting for transfers between devices, shards(): lax.all_to_all(outgoing, 'dp', split_axis=0, concat_axis=0, tiled=True)  24.6 us
    all_gather x1, blocking collectives, shards(): lax.all_gather(embeds.astype(jnp.bfloat16), 'loss', axis=0, tiled=True)  24.1 us
    all_to_all x1, starting transfers between devices, shards(): lax.all_to_all(outgoing, 'dp', split_axis=0, concat_axis=0, tiled=True)  17.6 us
  transfers between devices with their start and end apart: 3, of which 3 were waited for; matrix products, arithmetic and copies ran while one was open for 2% of the time, Pallas kernels for 0%

commit v1 on v0

v1 whole, which is shorter than its diff:
```python
import functools

import jax
import jax.numpy as jnp
from jax import lax
from jax.experimental import pallas as pl
from jax.experimental.pallas import tpu as pltpu
from jax.sharding import PartitionSpec as P

eps = 1e-06
grad_scale = 262144.0
gelu_coef = 0.7978845608028654
f32 = jnp.float32
bf16 = jnp.bfloat16
VMEM_LIMIT = 48 * 1024 * 1024
whole = pl.BlockSpec(memory_space=pltpu.VMEM)
scalars = pl.BlockSpec(memory_space=pltpu.SMEM)
NT = (((1,), (1,)), ((), ()))
TN = (((0,), (0,)), ((), ()))
HIGHEST = lax.Precision.HIGHEST


def column_chunks(width, step):
    return [(first, min(step, width - first)) for first in range(0, width, step)]


def layer_statistics(floats):
    center = floats - jnp.mean(floats, axis=-1, keepdims=True)
    spread = jnp.mean(center * center, axis=-1, keepdims=True)
    inverse_deviation = lax.rsqrt(spread + eps)
    return center * inverse_deviation, inverse_deviation


def split_bf16(values):
    high = values.astype(bf16)
    return high, (values - high.astype(f32)).astype(bf16)


def pool_kernel(dp_ref, counts_ref, x_ref, gain_ref, bias_ref, w1_ref, b1_ref, w2_ref, out_ref, *, share):
    rows = x_ref.shape[0]
    images = counts_ref.shape[1]
    position = dp_ref[0] * rows + lax.broadcasted_iota(jnp.int32, (images, rows), 1)
    image = lax.broadcasted_iota(jnp.int32, (images, rows), 0)
    member = jnp.zeros((images, rows), f32)
    start = jnp.int32(0)
    for j in range(images):
        end = start + counts_ref[0, j]
        inside = (image == j) & (position >= start) & (position < end)
        member = jnp.where(inside, 1.0, member)
        start = end
    member = member.astype(bf16)
    x = x_ref[...]
    xhat, _ = layer_statistics(x.astype(f32))
    normed = (xhat * gain_ref[...] + bias_ref[...]).astype(bf16)
    total = share * jnp.dot(member, x, preferred_element_type=f32)
    for first, many in column_chunks(w1_ref.shape[1], 256):
        cols = slice(first, first + many)
        pre = jnp.dot(normed, w1_ref[:, cols], preferred_element_type=f32) + b1_ref[:, cols]
        inner = gelu_coef * (pre + 0.044715 * pre * pre * pre)
        act = (0.5 * pre * (1.0 + jnp.tanh(inner))).astype(bf16)
        pooled = jnp.dot(member, act, preferred_element_type=f32)
        w2 = w2_ref[cols, :]
        for piece in split_bf16(pooled):
            total = total + jnp.dot(piece, w2, preferred_element_type=f32)
    out_ref[...] = total


def slope_kernel(x_ref, gain_ref, bias_ref, w1_ref, b1_ref, slope_ref):
    xhat, _ = layer_statistics(x_ref[...].astype(f32))
    normed = (xhat * gain_ref[...] + bias_ref[...]).astype(bf16)
    for first, many in column_chunks(w1_ref.shape[1], 256):
        cols = slice(first, first + many)
        pre = jnp.dot(normed, w1_ref[:, cols], preferred_element_type=f32) + b1_ref[:, cols]
        square = pre * pre
        tanh_part = jnp.tanh(gelu_coef * (pre + 0.044715 * square * pre))
        slope_ref[:, cols] = 0.5 * (1.0 + tanh_part) + 0.5 * pre * (
            1.0 - tanh_part * tanh_part
        ) * gelu_coef * (1.0 + 0.134145 * square)


def unit_rows(values):
    norm = jnp.sqrt(jnp.sum(values * values, axis=-1, keepdims=True) + eps)
    return values / norm, norm


def embed_kernel(pieces_ref, counts_ref, texts_ref, matches_ref, scale_ref, shift_ref, embed_ref, upstream_ref):
    total = pieces_ref[0]
    for k in range(1, pieces_ref.shape[0]):
        total = total + pieces_ref[k]
    counts = counts_ref[...]
    embed = total / counts
    embed_ref[...] = embed.astype(bf16)
    unit_e, norm_e = unit_rows(embed)
    unit_t, _ = unit_rows(texts_ref[...].astype(f32))
    images = unit_t.shape[0]
    scale = scale_ref[0]
    score = scale * lax.dot_general(unit_e, unit_t, NT, precision=HIGHEST, preferred_element_type=f32) + shift_ref[0]
    sign = 2.0 * matches_ref[...] - 1.0
    dscore = -sign * jax.nn.sigmoid(-sign * score) / images
    du = scale * jnp.dot(dscore, unit_t, precision=HIGHEST, preferred_element_type=f32)
    dembed = (du - unit_e * jnp.sum(unit_e * du, axis=-1, keepdims=True)) / norm_e
    upstream_ref[...] = grad_scale * (dembed / counts)


def back_kernel(upstream_ref, member_ref, slope_ref, w1_ref, w2_ref, out_ref):
    d_image = upstream_ref[...].astype(bf16)
    d_act = lax.dot_general(d_image, w2_ref[...], NT, preferred_element_type=f32)
    member = member_ref[...]
    high, low = split_bf16(d_act)
    d_rows = jnp.dot(member, high, preferred_element_type=f32) + jnp.dot(member, low, preferred_element_type=f32)
    d_pre = (d_rows * slope_ref[...]).astype(bf16)
    out_ref[...] = lax.dot_general(d_pre, w1_ref[...], NT, preferred_element_type=f32).astype(bf16)


def row_kernel(own_ref, first_ref, second_ref, third_ref, x_ref, gain_ref, member_ref, upstream_ref, out_ref):
    back = own_ref[...].astype(f32) + first_ref[...].astype(f32)
    back = back + second_ref[...].astype(f32) + third_ref[...].astype(f32)
    xhat, inverse_deviation = layer_statistics(x_ref[...].astype(f32))
    dxhat = back * gain_ref[...]
    dx = inverse_deviation * (
        dxhat
        - jnp.mean(dxhat, axis=-1, keepdims=True)
        - xhat * jnp.mean(dxhat * xhat, axis=-1, keepdims=True)
    )
    upstream = jnp.dot(member_ref[...], upstream_ref[...], precision=HIGHEST, preferred_element_type=f32)
    out_ref[...] = dx + upstream


def loss_kernel(embeds_ref, texts_ref, own_text_ref, labels_ref, matches_ref, scale_ref, shift_ref, grad_ref, loss_ref):
    unit_e, _ = unit_rows(embeds_ref[...].astype(f32))
    unit_t, _ = unit_rows(texts_ref[...].astype(f32))
    images = unit_e.shape[0]
    scale = scale_ref[0]
    score = scale * lax.dot_general(unit_e, unit_t, NT, precision=HIGHEST, preferred_element_type=f32) + shift_ref[0]
    text_index = lax.broadcasted_iota(jnp.int32, (images, images), 1)
    sign = jnp.where(labels_ref[...] == text_index, 1.0, -1.0)
    margin = sign * score
    log_sigmoid = jnp.minimum(margin, 0.0) - jnp.log1p(jnp.exp(-jnp.abs(margin)))
    row_sums = jnp.sum(log_sigmoid, axis=1, keepdims=True)
    loss_ref[...] = -jnp.sum(row_sums, axis=0, keepdims=True) / images
    unit_o, norm_o = unit_rows(own_text_ref[...].astype(f32))
    own_score = scale * lax.dot_general(unit_o, unit_e, NT, precision=HIGHEST, preferred_element_type=f32) + shift_ref[0]
    own_sign = 2.0 * matches_ref[...] - 1.0
    dscore = -own_sign * jax.nn.sigmoid(-own_sign * own_score) / images
    dv = scale * jnp.dot(dscore, unit_e, precision=HIGHEST, preferred_element_type=f32)
    grad_ref[...] = (dv - unit_o * jnp.sum(unit_o * dv, axis=-1, keepdims=True)) / norm_o


def call(kernel, outs, specs, operands, flops=0, read=0):
    return pl.pallas_call(
        kernel,
        out_shape=outs,
        in_specs=specs,
        out_specs=jax.tree.map(lambda _: whole, outs),
        compiler_params=pltpu.CompilerParams(vmem_limit_bytes=VMEM_LIMIT),
        cost_estimate=pl.CostEstimate(flops=flops, bytes_accessed=read, transcendentals=0),
    )(*operands)


def shape(dims, kind):
    return jax.ShapeDtypeStruct(dims, kind)


def gather_by_exchange(block, axis):
    copies = jnp.broadcast_to(block[None], (lax.axis_size(axis),) + block.shape)
    return lax.all_to_all(copies, axis, split_axis=0, concat_axis=0, tiled=True)


def shards(
    patches,
    layer_norm_gain,
    layer_norm_bias,
    fc1_weight,
    fc1_bias,
    fc2_weight,
    counts,
    owners,
    text_embed,
    labels,
    logit_scale,
    logit_bias,
):
    dp_size = lax.axis_size("dp")
    mp_size = lax.axis_size("mp")
    dp_index = lax.axis_index("dp")
    mp_index = lax.axis_index("mp")
    loss_index = lax.axis_index("loss")
    row_count, width = patches.shape
    hidden = fc1_weight.shape[1]
    block_rows = row_count // dp_size
    share_rows = row_count // mp_size
    group_images = counts.shape[1]
    total_images = labels.shape[0]
    gain = layer_norm_gain[None, :]
    bias = layer_norm_bias[None, :]
    fc1_offset = fc1_bias[None, :]
    plan = owners[0]
    slots = jnp.arange(dp_size, dtype=jnp.int32)

    all_texts = gather_by_exchange(text_embed, "loss").reshape(total_images, width)

    mine = lax.dynamic_index_in_dim(plan, dp_index, 0, keepdims=False)
    order = jnp.sum(jnp.where(mine[None, :] == slots[:, None], slots[None, :], 0), axis=1)
    outgoing = patches.reshape(dp_size, block_rows, width)[order]
    incoming = lax.all_to_all(outgoing, "dp", split_axis=0, concat_axis=0, tiled=True)

    matmul = 2 * row_count * width * hidden
    partial_sums = call(
        functools.partial(pool_kernel, share=1.0 / mp_size),
        shape((group_images, width), f32),
        [scalars, scalars] + [whole] * 6,
        (dp_index[None].astype(jnp.int32), counts, patches, gain, bias, fc1_weight, fc1_offset, fc2_weight),
        flops=matmul,
        read=4 * width * hidden,
    )
    slab_pieces = lax.all_gather(partial_sums, "mp", axis=0)
    slab_sums = jnp.sum(slab_pieces, axis=0)
    pieces = lax.all_gather(slab_sums, "dp", axis=0)

    local_rows = incoming.reshape(row_count, width)
    source_block = jnp.sum(jnp.where(plan == dp_index, slots[None, :], 0), axis=1)
    position = (
        slots[:, None] * row_count
        + source_block[:, None] * block_rows
        + jnp.arange(block_rows, dtype=jnp.int32)[None, :]
    ).reshape(row_count)
    ends = jnp.cumsum(counts[0])
    starts = ends - counts[0]
    member = ((position[:, None] >= starts[None, :]) & (position[:, None] < ends[None, :])).astype(bf16)
    first_row = mp_index * share_rows
    own_rows = lax.dynamic_slice_in_dim(local_rows, first_row, share_rows, 0)
    own_member = lax.dynamic_slice_in_dim(member, first_row, share_rows, 0).astype(f32)
    slope = call(
        slope_kernel,
        shape((row_count, hidden), f32),
        [whole] * 5,
        (local_rows, gain, bias, fc1_weight, fc1_offset),
        flops=matmul,
        read=4 * width * hidden,
    )

    own_first = loss_index * group_images
    text_index = jnp.arange(total_images, dtype=jnp.int32)
    own_labels = lax.dynamic_slice_in_dim(labels, own_first, group_images, 0)
    image_matches = (own_labels[:, None] == text_index[None, :]).astype(f32)
    own_texts = own_first + jnp.arange(group_images, dtype=jnp.int32)
    text_matches = (labels[None, :] == own_texts[:, None]).astype(f32)
    counts_column = counts[0].astype(f32)[:, None]
    embed, upstream = call(
        embed_kernel,
        (shape((group_images, width), bf16), shape((group_images, width), f32)),
        [whole] * 4 + [scalars] * 2,
        (pieces, counts_column, all_texts, image_matches, logit_scale, logit_bias),
    )
    back = call(
        back_kernel,
        shape((row_count, width), bf16),
        [whole] * 5,
        (upstream, member, slope, fc1_weight, fc2_weight),
        flops=matmul,
        read=4 * width * hidden,
    )
    received = []
    for step in (2, 1, 3):
        peer = (mp_index + step) % mp_size
        chunk = lax.dynamic_slice_in_dim(back, peer * share_rows, share_rows, 0)
        pairs = [(i, (i + step) % mp_size) for i in range(mp_size)]
        received.append(lax.ppermute(chunk, "mp", pairs))
    all_embeds = gather_by_exchange(embed, "loss").reshape(total_images, width)
    grad_text, loss = call(
        loss_kernel,
        (shape((group_images, width), f32), shape((1, 1), f32)),
        [whole] * 5 + [scalars] * 2,
        (all_embeds, all_texts, text_embed, labels[:, None], text_matches, logit_scale, logit_bias),
    )
    own_back = lax.dynamic_slice_in_dim(back, first_row, share_rows, 0)
    grad_rows = call(
        row_kernel,
        shape((share_rows, width), f32),
        [whole] * 8,
        (own_back, *received, own_rows, gain, own_member, upstream),
    )
    return (grad_rows, grad_text, loss[0, 0])


def solution(mesh):
    placed = (
        P(("dp", "loss"), None),
        P(),
        P(),
        P(None, "mp"),
        P("mp"),
        P("mp", None),
        P("loss", None),
        P("loss", None, None),
        P("loss", None),
        P(),
        P(),
        P(),
    )
    return jax.shard_map(
        shards,
        mesh=mesh,
        in_specs=placed,
        out_specs=(P(("dp", "loss", "mp"), None), P("loss", None), P()),
        check_vma=False,
    )
```

time: 467 us -> 161 us (0.34)
  blocking collectives: 329 us -> 42.8 us
  waiting for transfers between devices: 61.7 us -> 38.7 us
  matrix products: 20.6 us -> 0 us
  starting transfers between devices: 17.6 us -> 37.1 us
  Pallas kernels: 0 us -> 18.6 us
  between operations: 17.3 us -> 2.25 us
  local copies, waits for them, and re-layouts: 7.2 us -> 18.7 us
  other arithmetic: 12.1 us -> 0.8 us
    psum x1 -> x0, blocking collectives: 280 us -> none  [shards(): image_sums = lax.psum(partial_sums, ('dp', 'mp'))]
    reduce_scatter x2 -> x0, waiting for transfers between devices: 37 us -> none  [reduce_rows(): lax.psum_scatter(term(jnp.int32(0), shared_rows * lax.axis_size('mp')).as...]
    dot_general x8 -> x0, matrix products: 20.6 us -> none  [the longest x1 5.87 us: backward_term(): return jnp.dot(d_pre, fc1_weight.T, preferred_element_type=jnp.float32)]
    all_to_all x0 -> x2, starting transfers between devices: none -> 19 us  [gather_by_exchange(): return lax.all_to_all(copies, axis, split_axis=0, concat_axis=0, tiled=True)]
    pallas_call x0 -> x6, Pallas kernels: none -> 18.6 us  [call(): pl.pallas_call(kernel, out_shape=outs, in_specs=specs, out_specs=jax.tree...]
    ppermute x0 -> x3, waiting for transfers between devices: none -> 11.8 us  [shards(): received.append(lax.ppermute(chunk, 'mp', pairs))]
    ppermute x0 -> x3, starting transfers between devices: none -> 11.6 us  [shards(): received.append(lax.ppermute(chunk, 'mp', pairs))]
    all_to_all x1, starting transfers between devices: 17.6 us -> 6.51 us  [shards(): lax.all_to_all(outgoing, 'dp', split_axis=0, concat_axis=0, tiled=True)]
  transfers between devices with their start and end apart: 3 -> 6, of which waited for: 3 -> 4; matrix products, arithmetic and copies ran while one was open for 2% -> 7% of each run, Pallas kernels for 0% -> 5%
where the time goes in v1:
time: 161 us; the launch traced here: 159 us
  blocking collectives  42.8 us (27%)
  waiting for transfers between devices  38.7 us (24%)
  starting transfers between devices  37.1 us (23%)
  local copies, waits for them, and re-layouts  18.7 us (12%)
  Pallas kernels  18.6 us (12%)
  between operations  2.25 us (1%)
    all_gather x1, blocking collectives, shards(): pieces = lax.all_gather(slab_sums, 'dp', axis=0)  21.8 us
    all_gather x1, blocking collectives, shards(): slab_pieces = lax.all_gather(partial_sums, 'mp', axis=0)  21 us
    all_to_all x1, waiting for transfers between devices, shards(): lax.all_to_all(outgoing, 'dp', split_axis=0, concat_axis=0, tiled=True)  20.2 us
    all_to_all x2, starting transfers between devices, gather_by_exchange(): return lax.all_to_all(copies, axis, split_axis=0, concat_axis=0, tiled=True)  19 us
    pallas_call x6, Pallas kernels, call(): pl.pallas_call(kernel, out_shape=outs, in_specs=specs, out_specs=jax.tree...  18.6 us
    ppermute x3, waiting for transfers between devices, shards(): received.append(lax.ppermute(chunk, 'mp', pairs))  11.8 us
    ppermute x3, starting transfers between devices, shards(): received.append(lax.ppermute(chunk, 'mp', pairs))  11.6 us
    unnamed x29, local copies, waits for them, and re-layouts  8.86 us
  transfers between devices with their start and end apart: 6, of which 4 were waited for; matrix products, arithmetic and copies ran while one was open for 7% of the time, Pallas kernels for 5%

profile of v1, /device:TPU:1, one launch (start us, length us, event | category | flops | bytes accessed | tf_op | source)
XLA Modules:
  0.0 159.0 jit_solution(1628375196576824271)
XLA Ops:
  0.6 1.5 broadcast_in_dim.64
  2.1 11.0 %all-to-all-start = ((bf16[16,8,1152]{2,1,0:T(8,128)(2,1)}), bf16[16,8,1152]{2,1,0:T(8,128)(2,1)}, u32[]{:S(2)}, u32[]{:S(2)}) async-start(bf16[16,8,1152]{2,1,0:T(8,128)(2,1)} %broadcast_in_dim.64), calls=%async_computation | async-start | bytes 589824 | tf_op jit(solution)/shard_map/all_to_all | solution.py:166
  13.1 0.7 broadcast_in_dim.33.gain_ref
  13.8 0.0 copy-start.4
  13.8 0.7 broadcast_in_dim.34.bias_ref
  14.5 0.0 copy-start.7
  14.5 0.7 broadcast_in_dim.35.b1_ref
  15.2 0.0 copy-start.9
  15.2 0.0 copy-start.3
  15.2 4.2 %copy.25.w1_ref = bf16[1152,1076]{1,0:T(8,128)(2,1)S(1)} copy(bf16[1152,1076]{0,1:T(8,128)(2,1)} %param.15) | data formatting | bytes 4958208 | tf_op args[3]
  19.4 0.0 copy-start
  19.4 0.0 copy-done.4
  19.4 0.0 copy-done.7
  19.4 0.0 copy-done.9
  19.4 0.0 copy-done.3
  19.4 0.0 copy-done.11
  19.4 0.0 copy-start.1
  19.4 2.6 %copy-done.1 = bf16[1076,1152]{1,0:T(8,128)(2,1)S(1)} copy-done((bf16[1076,1152]{1,0:T(8,128)(2,1)S(1)}, bf16[1076,1152]{1,0:T(8,128)(2,1)}, u32[]{:S(2)}) %copy-start.1) | copy-done | bytes 2479128
  22.0 4.9 %shard_map.139 = f32[8,1152]{1,0:T(8,128)S(1)} custom-call(s32[1]{0:T(128)} %bitcast.dp_ref, s32[1,8]{1,0:T(1,128)S(1)} %copy-done.11, bf16[320,1152]{1,0:T(8,128)(2,1)S(1)} %copy-done.3, f32[1,1152]{1,0:T(1,128)S(1)} %broadcast_in_dim.33.gain_ref, f32[1,1152]{1,0:T(1,128)S(1)} %broadcast_in_dim.34.bias_ref, bf16[1152,1076]{1,0:T(8,128)(2,1)S(1)} %copy.25.w1_ref, ...), custom_call_target="tpu_custom_call" | custom-call | flops 793313280 | bytes 4958208 | tf_op jit(solution)/shard_map/pallas_call | solution.py:150
  27.0 0.0 copy-start.12
  27.0 21.0 %all-gather = f32[32,1152]{1,0:T(8,128)S(1)} all-gather(f32[8,1152]{1,0:T(8,128)S(1)} %shard_map.139), channel_id=2, replica_groups=mesh['dp'=16,'loss'=16,'mp'=4] {'mp'}, dimensions={0}, use_global_device_ids=true | all-gather | bytes 184320 | tf_op jit(solution)/shard_map/all_gather | solution.py:216
  48.0 1.1 reshape.88
  50.4 0.1 copy.26
  50.4 0.0 copy-done.13
  50.5 0.1 dynamic_slice.25
  50.5 0.1 fusion.matches_ref
  50.6 21.8 %all-gather.1 = f32[128,1152]{1,0:T(8,128)S(1)} all-gather(f32[8,1152]{1,0:T(8,128)S(1)} %bitcast_reduce_fusion), channel_id=3, replica_groups=mesh['dp'=16,'loss'=16,'mp'=4] {'dp'}, dimensions={0}, use_global_device_ids=true | all-gather | bytes 626688 | tf_op jit(solution)/shard_map/all_gather | solution.py:218
  72.4 0.0 all-to-all-done
  72.4 2.7 %shard_map.140 = (bf16[8,1152]{1,0:T(8,128)(2,1)S(1)}, f32[8,1152]{1,0:T(8,128)S(1)}) custom-call(f32[16,8,1152]{2,1,0:T(8,128)S(1)} %bitcast.24, f32[8,1]{1,0:T(8,128)S(1)} %convert_element_type.22.counts_ref, bf16[128,1152]{1,0:T(8,128)(2,1)} %bitcast.4.texts_ref, f32[8,128]{1,0:T(8,128)S(1)} %fusion.matches_ref, f32[1]{0:T(128)S(6)} %copy.32.scale_ref, ...), custom_call_target="tpu_custom_call" | custom-call | tf_op jit(solution)/shard_map/pallas_call | solution.py:150
  75.1 0.0 copy-start.6
  75.1 0.7 broadcast_in_dim.68
  75.9 8.0 %all-to-all-start.2 = ((bf16[16,8,1152]{2,1,0:T(8,128)(2,1)}), bf16[16,8,1152]{2,1,0:T(8,128)(2,1)S(1)}, u32[]{:S(2)}, u32[]{:S(2)}) async-start(bf16[16,8,1152]{2,1,0:T(8,128)(2,1)} %broadcast_in_dim.68), calls=%async_computation.2 | async-start | bytes 589824 | tf_op jit(solution)/shard_map/all_to_all | solution.py:166
  83.9 0.0 copy-done.12
  83.9 0.1 select_reduce_fusion
  84.0 2.7 %gather_fusion = bf16[16,20,1152]{2,1,0:T(8,128)(2,1)} fusion(bf16[16,20,1152]{2,1,0:T(8,128)(2,1)} %reshape.88, s32[1024]{0:T(1024)S(1)} %pad_clamp_fusion), kind=kCustom, calls=%fused_computation | custom fusion | bytes 1474624 | tf_op jit(solution)/shard_map/gather | solution.py:204
  86.8 6.7 %all-to-all-done.2 = bf16[16,8,1152]{2,1,0:T(8,128)(2,1)S(1)} async-done(((bf16[16,8,1152]{2,1,0:T(8,128)(2,1)}), bf16[16,8,1152]{2,1,0:T(8,128)(2,1)S(1)}, u32[]{:S(2)}, u32[]{:S(2)}) %all-to-all-start.2) | async-done | bytes 294944 | tf_op jit(solution)/shard_map/all_to_all | solution.py:166
  93.5 6.5 %all-to-all-start.1 = ((bf16[16,20,1152]{2,1,0:T(8,128)(2,1)}), bf16[16,20,1152]{2,1,0:T(8,128)(2,1)}, u32[]{:S(2)}, u32[]{:S(2)}) async-start(bf16[16,20,1152]{2,1,0:T(8,128)(2,1)} %gather_fusion), calls=%async_computation.1 | async-start | bytes 1769472 | tf_op jit(solution)/shard_map/all_to_all | solution.py:205
  100.0 0.1 select_reduce_fusion.1
  100.2 0.2 reduce-window.4
  100.3 0.1 iota_add_fusion
  100.4 0.1 add.93
  100.5 0.1 copy.31.labels_ref
  100.7 0.1 and_convert_fusion.member_ref
  100.8 0.1 compare_convert_fusion.matches_ref
  100.9 0.0 copy-done.6
  100.9 3.7 %shard_map.144 = (f32[8,1152]{1,0:T(8,128)}, f32[1,1]{1,0:T(1,128)}) custom-call(bf16[128,1152]{1,0:T(8,128)(2,1)S(1)} %bitcast.25, bf16[128,1152]{1,0:T(8,128)(2,1)} %bitcast.4.texts_ref, bf16[8,1152]{1,0:T(8,128)(2,1)S(1)} %copy-done.6, s32[128,1]{1,0:T(8,128)S(1)} %copy.31.labels_ref, f32[8,128]{1,0:T(8,128)S(1)} %compare_convert_fusion.matches_ref, ...), custom_call_target="tpu_custom_call" | custom-call | tf_op jit(solution)/shard_map/pallas_call | solution.py:150
  104.6 20.2 %all-to-all-done.1 = bf16[16,20,1152]{2,1,0:T(8,128)(2,1)} async-done(((bf16[16,20,1152]{2,1,0:T(8,128)(2,1)}), bf16[16,20,1152]{2,1,0:T(8,128)(2,1)}, u32[]{:S(2)}, u32[]{:S(2)}) %all-to-all-start.1) | async-done | bytes 737312 | tf_op jit(solution)/shard_map/all_to_all | solution.py:205
  124.8 1.3 reshape.89.x_ref
  126.0 0.0 copy-done
  126.1 0.0 copy-start.5
  126.1 0.7 copy-done.5
  126.7 0.7 copy-done.8
  127.4 0.7 copy-done.10
  128.1 1.9 %shard_map.141.slope_ref = f32[320,1076]{1,0:T(8,128)S(1)} custom-call(bf16[320,1152]{1,0:T(8,128)(2,1)S(1)} %reshape.89.x_ref, f32[1,1152]{1,0:T(1,128)S(1)} %copy-done.5, f32[1,1152]{1,0:T(1,128)S(1)} %copy-done.8, bf16[1152,1076]{1,0:T(8,128)(2,1)S(1)} %copy.25.w1_ref, f32[1,1076]{1,0:T(1,128)S(1)} %copy-done.10), custom_call_target="tpu_custom_call" | custom-call | flops 793313280 | bytes 4958208 | tf_op jit(solution)/shard_map/pallas_call | solution.py:150
  130.0 0.0 copy-done.2
  130.0 4.1 %shard_map.142 = bf16[320,1152]{1,0:T(8,128)(2,1)S(1)} custom-call(f32[8,1152]{1,0:T(8,128)S(1)} %get-tuple-element.7.upstream_ref, bf16[320,8]{1,0:T(8,128)(2,1)S(1)} %and_convert_fusion.member_ref, f32[320,1076]{1,0:T(8,128)S(1)} %shard_map.141.slope_ref, bf16[1152,1076]{1,0:T(8,128)(2,1)} %copy-done, bf16[1076,1152]{1,0:T(8,128)(2,1)S(1)} %copy-done.2), custom_call_target="tpu_custom_call" | custom-call | flops 793313280 | bytes 4958208 | tf_op jit(solution)/shard_map/pallas_call | solution.py:150
  134.2 0.1 constant_dynamic-slice_fusion.1
  134.3 5.7 %collective-permute-start.2 = (bf16[80,1152]{1,0:T(8,128)(2,1)S(1)}, bf16[80,1152]{1,0:T(8,128)(2,1)S(1)}, u32[]{:S(2)}, u32[]{:S(2)}) collective-permute-start(bf16[80,1152]{1,0:T(8,128)(2,1)S(1)} %get-tuple-element.11), channel_id=1, source_target_pairs={{0,3},{1,0},{2,1},{3,2},{4,7},{5,4},{6,5},{7,6},{8,11},{9,8},{10,9... | collective-permute-start | bytes 552968 | tf_op jit(solution)/shard_map/ppermute | solution.py:268
  140.0 1.9 %collective-permute-start.1 = (bf16[80,1152]{1,0:T(8,128)(2,1)S(1)}, bf16[80,1152]{1,0:T(8,128)(2,1)S(1)}, u32[]{:S(2)}, u32[]{:S(2)}) collective-permute-start(bf16[80,1152]{1,0:T(8,128)(2,1)S(1)} %get-tuple-element.12), channel_id=1, source_target_pairs={{0,1},{1,2},{2,3},{3,0},{4,5},{5,6},{6,7},{7,4},{8,9},{9,10},{10,1... | collective-permute-start | bytes 552968 | tf_op jit(solution)/shard_map/ppermute | solution.py:268
  141.9 4.0 %collective-permute-start = (bf16[80,1152]{1,0:T(8,128)(2,1)S(1)}, bf16[80,1152]{1,0:T(8,128)(2,1)S(1)}, u32[]{:S(2)}, u32[]{:S(2)}) collective-permute-start(bf16[80,1152]{1,0:T(8,128)(2,1)S(1)} %get-tuple-element.13), channel_id=1, source_target_pairs={{0,2},{1,3},{2,0},{3,1},{4,6},{5,7},{6,4},{7,5},{8,10},{9,11},{10,... | collective-permute-start | bytes 552968 | tf_op jit(solution)/shard_map/ppermute | solution.py:268
  145.9 0.3 collective-permute-done.2.third_ref
  146.2 11.5 %collective-permute-done.1.second_ref = bf16[80,1152]{1,0:T(8,128)(2,1)S(1)} collective-permute-done((bf16[80,1152]{1,0:T(8,128)(2,1)S(1)}, bf16[80,1152]{1,0:T(8,128)(2,1)S(1)}, u32[]{:S(2)}, u32[]{:S(2)}) %collective-permute-start.1) | collective-permute-done | bytes 184352 | tf_op jit(solution)/shard_map/ppermute | solution.py:268
  157.7 0.0 collective-permute-done.first_ref
  157.7 1.2 shard_map.143
  (15 shorter events, 0.1 us)
Async XLA Ops:
  2.1 70.3 %all-to-all-start = ((bf16[16,8,1152]{2,1,0:T(8,128)(2,1)}), bf16[16,8,1152]{2,1,0:T(8,128)(2,1)}, u32[]{:S(2)}, u32[]{:S(2)}) async-start(bf16[16,8,1152]{2,1,0:T(8,128)(2,1)} %broadcast_in_dim.64), calls=%async_computation | async-start | bytes 589824 | tf_op jit(solution)/shard_map/all_to_all | solution.py:166
  13.8 5.6 %copy-start.4 = (f32[1,1152]{1,0:T(1,128)}, f32[1,1152]{1,0:T(1,128)S(1)}, u32[]{:S(2)}) copy-start(f32[1,1152]{1,0:T(1,128)S(1)} %broadcast_in_dim.33.gain_ref) | copy-start | bytes 13828
  14.5 4.9 %copy-start.7 = (f32[1,1152]{1,0:T(1,128)}, f32[1,1152]{1,0:T(1,128)S(1)}, u32[]{:S(2)}) copy-start(f32[1,1152]{1,0:T(1,128)S(1)} %broadcast_in_dim.34.bias_ref) | copy-start | bytes 13828
  15.2 4.2 %copy-start.9 = (f32[1,1076]{1,0:T(1,128)}, f32[1,1076]{1,0:T(1,128)S(1)}, u32[]{:S(2)}) copy-start(f32[1,1076]{1,0:T(1,128)S(1)} %broadcast_in_dim.35.b1_ref) | copy-start | bytes 12916
  15.2 4.2 %copy-start.3 = (bf16[320,1152]{1,0:T(8,128)(2,1)S(1)}, bf16[320,1152]{1,0:T(8,128)(2,1)}, u32[]{:S(2)}) copy-start(bf16[320,1152]{1,0:T(8,128)(2,1)} %x_ref.1) | copy-start | bytes 2211844
  15.2 4.2 %copy-start.11 = (s32[1,8]{1,0:T(1,128)S(1)}, s32[1,8]{1,0:T(1,128)}, u32[]{:S(2)}) copy-start(s32[1,8]{1,0:T(1,128)} %counts_ref.1) | copy-start | bytes 100
  19.4 106.7 %copy-start = (bf16[1152,1076]{1,0:T(8,128)(2,1)}, bf16[1152,1076]{1,0:T(8,128)(2,1)S(1)}, u32[]{:S(2)}) copy-start(bf16[1152,1076]{1,0:T(8,128)(2,1)S(1)} %copy.25.w1_ref) | copy-start | bytes 7437316
  19.4 2.6 %copy-start.1 = (bf16[1076,1152]{1,0:T(8,128)(2,1)S(1)}, bf16[1076,1152]{1,0:T(8,128)(2,1)}, u32[]{:S(2)}) copy-start(bf16[1076,1152]{1,0:T(8,128)(2,1)} %w2_ref.3) | copy-start | bytes 7437316
  22.0 28.4 %copy-start.13 = (s32[128]{0:T(128)S(1)}, s32[128]{0:T(128)}, u32[]{:S(2)}) copy-start(s32[128]{0:T(128)} %param.21) | copy-start | bytes 1540
  27.0 56.9 %copy-start.12 = (s32[1,16,16]{2,1,0:T(8,128)S(1)}, s32[1,16,16]{2,1,0:T(8,128)}, u32[]{:S(2)}) copy-start(s32[1,16,16]{2,1,0:T(8,128)} %param.19) | copy-start | bytes 3076
  75.1 25.8 %copy-start.6 = (bf16[8,1152]{1,0:T(8,128)(2,1)S(1)}, bf16[8,1152]{1,0:T(8,128)(2,1)}, u32[]{:S(2)}) copy-start(bf16[8,1152]{1,0:T(8,128)(2,1)} %own_text_ref.1) | copy-start | bytes 55300
  75.9 17.6 %all-to-all-start.2 = ((bf16[16,8,1152]{2,1,0:T(8,128)(2,1)}), bf16[16,8,1152]{2,1,0:T(8,128)(2,1)S(1)}, u32[]{:S(2)}, u32[]{:S(2)}) async-start(bf16[16,8,1152]{2,1,0:T(8,128)(2,1)} %broadcast_in_dim.68), calls=%async_computation.2 | async-start | bytes 589824 | tf_op jit(solution)/shard_map/all_to_all | solution.py:166
  93.5 31.3 %all-to-all-start.1 = ((bf16[16,20,1152]{2,1,0:T(8,128)(2,1)}), bf16[16,20,1152]{2,1,0:T(8,128)(2,1)}, u32[]{:S(2)}, u32[]{:S(2)}) async-start(bf16[16,20,1152]{2,1,0:T(8,128)(2,1)} %gather_fusion), calls=%async_computation.1 | async-start | bytes 1769472 | tf_op jit(solution)/shard_map/all_to_all | solution.py:205
  126.1 0.7 copy-start.5
  126.7 0.7 copy-start.8
  127.4 0.7 copy-start.10
  128.1 1.9 %copy-start.2 = (bf16[1076,1152]{1,0:T(8,128)(2,1)S(1)}, bf16[1076,1152]{1,0:T(8,128)(2,1)}, u32[]{:S(2)}) copy-start(bf16[1076,1152]{1,0:T(8,128)(2,1)} %w2_ref.3) | copy-start | bytes 7437316
  134.3 11.9 %collective-permute-start.2 = (bf16[80,1152]{1,0:T(8,128)(2,1)S(1)}, bf16[80,1152]{1,0:T(8,128)(2,1)S(1)}, u32[]{:S(2)}, u32[]{:S(2)}) collective-permute-start(bf16[80,1152]{1,0:T(8,128)(2,1)S(1)} %get-tuple-element.11), channel_id=1, source_target_pairs={{0,3},{1,0},{2,1},{3,2},{4,7},{5,4},{6,5},{7,6},{8,11},{9,8},{10,9... | collective-permute-start | bytes 552968 | tf_op jit(solution)/shard_map/ppermute | solution.py:268
  140.0 17.8 %collective-permute-start.1 = (bf16[80,1152]{1,0:T(8,128)(2,1)S(1)}, bf16[80,1152]{1,0:T(8,128)(2,1)S(1)}, u32[]{:S(2)}, u32[]{:S(2)}) collective-permute-start(bf16[80,1152]{1,0:T(8,128)(2,1)S(1)} %get-tuple-element.12), channel_id=1, source_target_pairs={{0,1},{1,2},{2,3},{3,0},{4,5},{5,6},{6,7},{7,4},{8,9},{9,10},{10,1... | collective-permute-start | bytes 552968 | tf_op jit(solution)/shard_map/ppermute | solution.py:268
  141.9 15.8 %collective-permute-start = (bf16[80,1152]{1,0:T(8,128)(2,1)S(1)}, bf16[80,1152]{1,0:T(8,128)(2,1)S(1)}, u32[]{:S(2)}, u32[]{:S(2)}) collective-permute-start(bf16[80,1152]{1,0:T(8,128)(2,1)S(1)} %get-tuple-element.13), channel_id=1, source_target_pairs={{0,2},{1,3},{2,0},{3,1},{4,6},{5,7},{6,4},{7,5},{8,10},{9,11},{10,... | collective-permute-start | bytes 552968 | tf_op jit(solution)/shard_map/ppermute | solution.py:268

commit v2 on v1

v2 whole, which is shorter than its diff:
```python
import functools

import jax
import jax.numpy as jnp
from jax import lax
from jax.experimental import pallas as pl
from jax.experimental.pallas import tpu as pltpu
from jax.sharding import PartitionSpec as P

eps = 1e-06
grad_scale = 262144.0
gelu_coef = 0.7978845608028654
f32 = jnp.float32
bf16 = jnp.bfloat16
VMEM_LIMIT = 48 * 1024 * 1024
whole = pl.BlockSpec(memory_space=pltpu.VMEM)
scalars = pl.BlockSpec(memory_space=pltpu.SMEM)
NT = (((1,), (1,)), ((), ()))
TN = (((0,), (0,)), ((), ()))
LANES = 128
HIGHEST = lax.Precision.HIGHEST


def column_chunks(width, step):
    return [(first, min(step, width - first)) for first in range(0, width, step)]


def layer_statistics(floats):
    center = floats - jnp.mean(floats, axis=-1, keepdims=True)
    spread = jnp.mean(center * center, axis=-1, keepdims=True)
    inverse_deviation = lax.rsqrt(spread + eps)
    return center * inverse_deviation, inverse_deviation


def split_bf16(values):
    high = values.astype(bf16)
    return high, (values - high.astype(f32)).astype(bf16)


def split_three(values):
    high, rest = split_bf16(values)
    return high, rest, (values - high.astype(f32) - rest.astype(f32)).astype(bf16)


def quotient(values, by):
    return (values * (65536 // by + 1)) >> 16


def iota(dims, axis):
    return lax.broadcasted_iota(jnp.int32, dims, axis)


def one_hot(condition):
    return jnp.where(condition, 1.0, 0.0).astype(bf16)


def pack_kernel(dp_ref, owners_ref, x_ref, text_ref, out_ref, copies_ref, *, padded):
    rows = x_ref.shape[0]
    slots = owners_ref.shape[0]
    block_rows = rows // slots
    block = quotient(iota((1, rows), 1), block_rows)
    within = iota((1, rows), 1) - block * block_rows
    owner = jnp.zeros((1, rows), jnp.int32)
    for b in range(slots):
        owner = jnp.where(block == b, owners_ref[dp_ref[0], b], owner)
    target = owner * padded + within
    pick = one_hot(iota((slots * padded, rows), 0) == target)
    out_ref[...] = jnp.dot(pick, x_ref[...], preferred_element_type=f32).astype(bf16)
    text = text_ref[...].astype(f32)
    copies_ref[...] = jnp.concatenate([text] * (copies_ref.shape[0] // text.shape[0]), axis=0).astype(bf16)


def image_bounds(counts_ref, dims, axis):
    image = iota(dims, axis)
    starts = jnp.zeros(dims, jnp.int32)
    ends = jnp.zeros(dims, jnp.int32)
    first = jnp.int32(0)
    for j in range(counts_ref.shape[1]):
        last = first + counts_ref[0, j]
        starts = jnp.where(image == j, first, starts)
        ends = jnp.where(image == j, last, ends)
        first = last
    return starts, ends


def pool_kernel(dp_ref, counts_ref, x_ref, gain_ref, bias_ref, w1t_ref, b1_ref, w2_ref, out_ref, *, share):
    rows = x_ref.shape[0]
    images = counts_ref.shape[1]
    position = dp_ref[0] * rows + iota((images, rows), 1)
    starts, ends = image_bounds(counts_ref, (images, 1), 0)
    member = one_hot((position >= starts) & (position < ends))
    x = x_ref[...]
    xhat, _ = layer_statistics(x.astype(f32))
    normed = (xhat * gain_ref[...][None, :] + bias_ref[...][None, :]).astype(bf16)
    offset = b1_ref[...][None, :]
    total = share * jnp.dot(member, x, preferred_element_type=f32)
    for first, many in column_chunks(w1t_ref.shape[0], 256):
        cols = slice(first, first + many)
        pre = lax.dot_general(normed, w1t_ref[cols, :], NT, preferred_element_type=f32) + offset[:, cols]
        inner = gelu_coef * (pre + 0.044715 * pre * pre * pre)
        act = (0.5 * pre * (1.0 + jnp.tanh(inner))).astype(bf16)
        pooled = jnp.dot(member, act, preferred_element_type=f32)
        both = jnp.concatenate(split_bf16(pooled), axis=0)
        product = jnp.dot(both, w2_ref[cols, :], preferred_element_type=f32)
        total = total + product[:images] + product[images:]
    out_ref[...] = total


def slope_kernel(
    dp_ref, counts_ref, owners_ref, in_ref, gain_ref, bias_ref, w1t_ref, b1_ref, slope_ref, rows_ref, member_ref
):
    rows = rows_ref.shape[0]
    slots = owners_ref.shape[0]
    block_rows = rows // slots
    padded = in_ref.shape[0] // slots
    source = quotient(iota((rows, 1), 0), block_rows)
    within = iota((rows, 1), 0) - source * block_rows
    pick = one_hot(iota((rows, in_ref.shape[0]), 1) == source * padded + within)
    x = jnp.dot(pick, in_ref[...], preferred_element_type=f32)
    rows_ref[...] = x.astype(bf16)
    block = jnp.where(owners_ref[...] == dp_ref[0], iota((slots, slots), 1), 0)
    block = jnp.sum(block.astype(f32), axis=1, keepdims=True)
    by_source = one_hot(iota((rows, slots), 1) == source)
    block = jnp.dot(by_source, jnp.broadcast_to(block, (slots, LANES)).astype(bf16), preferred_element_type=f32)
    position = source * rows + block[:, :1].astype(jnp.int32) * block_rows + within
    starts, ends = image_bounds(counts_ref, (1, member_ref.shape[1]), 1)
    member_ref[...] = jnp.where((position >= starts) & (position < ends), 1.0, 0.0)
    xhat, _ = layer_statistics(x)
    normed = (xhat * gain_ref[...][None, :] + bias_ref[...][None, :]).astype(bf16)
    offset = b1_ref[...][None, :]
    for first, many in column_chunks(w1t_ref.shape[0], 256):
        cols = slice(first, first + many)
        pre = lax.dot_general(normed, w1t_ref[cols, :], NT, preferred_element_type=f32) + offset[:, cols]
        square = pre * pre
        tanh_part = jnp.tanh(gelu_coef * (pre + 0.044715 * square * pre))
        slope_ref[:, cols] = 0.5 * (1.0 + tanh_part) + 0.5 * pre * (
            1.0 - tanh_part * tanh_part
        ) * gelu_coef * (1.0 + 0.134145 * square)


def log_sigmoid(values):
    return jnp.minimum(values, 0.0) - jnp.log1p(jnp.exp(-jnp.abs(values)))


def embed_kernel(
    loss_ref, counts_ref, labels_ref, scale_ref, shift_ref, pieces_ref, texts_ref, upstream_ref, parts_ref
):
    total = pieces_ref[0]
    for k in range(1, pieces_ref.shape[0]):
        total = total + pieces_ref[k]
    images, width = total.shape
    texts = texts_ref[...]
    all_images = texts.shape[0]
    image = iota((images, 1), 0)
    count = jnp.zeros((images, 1), jnp.int32)
    label = jnp.zeros((images, 1), jnp.int32)
    for j in range(images):
        count = jnp.where(image == j, counts_ref[0, j], count)
        label = jnp.where(image == j, labels_ref[loss_ref[0] * images + j], label)
    count = count.astype(f32)
    embed = total / count
    norm_e = jnp.sqrt(jnp.sum(embed * embed, axis=-1, keepdims=True) + eps)
    unit_e = embed / norm_e
    wide = texts.astype(f32)
    norm_t = jnp.sqrt(jnp.sum(wide * wide, axis=-1, keepdims=True) + eps)
    inverse_t = (1.0 / norm_t).T
    scale = scale_ref[0]
    unit_parts = split_three(unit_e)
    raw = lax.dot_general(jnp.concatenate(unit_parts, axis=0), texts, NT, preferred_element_type=f32)
    raw = raw[:images] + raw[images : 2 * images] + raw[2 * images :]
    score = scale * (raw * inverse_t) + shift_ref[0]
    sign = jnp.where(iota((images, all_images), 1) == label, 1.0, -1.0)
    margin = sign * score
    dscore = -sign * jax.nn.sigmoid(-margin) / all_images
    du = jnp.dot(
        jnp.concatenate(split_three(dscore * inverse_t), axis=0), texts, preferred_element_type=f32
    )
    du = scale * (du[:images] + du[images : 2 * images] + du[2 * images :])
    dembed = (du - unit_e * jnp.sum(unit_e * du, axis=-1, keepdims=True)) / norm_e
    upstream_ref[...] = grad_scale * (dembed / count)
    high, low = split_bf16(scale * dscore)
    unit_high, unit_low = unit_parts[:2]
    parts = lax.dot_general(
        jnp.concatenate([high, high, low], axis=0),
        jnp.concatenate([unit_high, unit_low, unit_high], axis=0),
        TN,
        preferred_element_type=f32,
    )
    parts_ref[:, :width] = parts.astype(bf16)
    loss = jnp.sum(jnp.sum(log_sigmoid(margin), axis=1, keepdims=True), axis=0, keepdims=True) / -all_images
    loss_high, loss_low = split_bf16(loss)
    lane = iota((all_images, LANES), 1)
    loss_lanes = jnp.where(lane == 0, loss_high.astype(f32), jnp.where(lane == 1, loss_low.astype(f32), 0.0))
    parts_ref[:, width:] = loss_lanes.astype(bf16)


def back_kernel(
    mp_ref, upstream_ref, member_ref, slope_ref, w1t_ref, w2_ref, *refs, steps, ring
):
    outs, d_act_ref = refs[:-1], refs[-1]
    share = outs[0].shape[0]
    d_image = upstream_ref[...].astype(bf16)
    d_act = lax.dot_general(d_image, w2_ref[...], NT, preferred_element_type=f32)
    both = jnp.concatenate(split_bf16(d_act), axis=0)
    d_act_ref[...] = both
    for out_ref, step in zip(outs, steps):
        first = pl.multiple_of(lax.rem(mp_ref[0] + step, ring) * share, share)
        rows = pl.ds(first, share)
        out_ref[...] = back_rows(member_ref[rows, :], both, slope_ref[rows, :], w1t_ref[...]).astype(bf16)


def back_rows(member, both, slope, w1t):
    member = member.astype(bf16)
    d_rows = jnp.dot(jnp.concatenate([member, member], axis=1), both, preferred_element_type=f32)
    d_pre = (d_rows * slope).astype(bf16)
    return jnp.dot(d_pre, w1t, preferred_element_type=f32)


def own_kernel(d_act_ref, member_ref, slope_ref, w1t_ref, out_ref):
    out_ref[...] = back_rows(member_ref[...], d_act_ref[...], slope_ref[...], w1t_ref[...])


def row_kernel(own_ref, first_ref, second_ref, third_ref, x_ref, gain_ref, member_ref, upstream_ref, out_ref):
    back = own_ref[...] + first_ref[...].astype(f32)
    back = back + second_ref[...].astype(f32) + third_ref[...].astype(f32)
    xhat, inverse_deviation = layer_statistics(x_ref[...].astype(f32))
    dxhat = back * gain_ref[...][None, :]
    dx = inverse_deviation * (
        dxhat
        - jnp.mean(dxhat, axis=-1, keepdims=True)
        - xhat * jnp.mean(dxhat * xhat, axis=-1, keepdims=True)
    )
    upstream = jnp.dot(member_ref[...], upstream_ref[...], precision=HIGHEST, preferred_element_type=f32)
    out_ref[...] = dx + upstream


def text_kernel(parts_ref, text_ref, grad_ref, loss_ref):
    text = text_ref[...].astype(f32)
    width = text.shape[1]
    total = parts_ref[0].astype(f32)
    for k in range(1, parts_ref.shape[0]):
        total = total + parts_ref[k].astype(f32)
    norm = jnp.sqrt(jnp.sum(text * text, axis=-1, keepdims=True) + eps)
    unit = text / norm
    dv = total[:, :width]
    grad_ref[...] = (dv - unit * jnp.sum(unit * dv, axis=-1, keepdims=True)) / norm
    loss_ref[...] = jnp.sum(total[:1, width:], axis=1, keepdims=True)


def call(kernel, outs, specs, operands, flops=0, read=0):
    return pl.pallas_call(
        kernel,
        out_shape=outs,
        in_specs=specs,
        out_specs=jax.tree.map(lambda _: whole, outs),
        compiler_params=pltpu.CompilerParams(vmem_limit_bytes=VMEM_LIMIT),
        cost_estimate=pl.CostEstimate(flops=flops, bytes_accessed=read, transcendentals=0),
    )(*operands)


def shape(dims, kind):
    return jax.ShapeDtypeStruct(dims, kind)


def exchange(block, axis):
    return lax.all_to_all(block, axis, split_axis=0, concat_axis=0, tiled=True)


def shards(
    patches,
    layer_norm_gain,
    layer_norm_bias,
    fc1_weight,
    fc1_bias,
    fc2_weight,
    counts,
    owners,
    text_embed,
    labels,
    logit_scale,
    logit_bias,
):
    dp_size = lax.axis_size("dp")
    mp_size = lax.axis_size("mp")
    loss_size = lax.axis_size("loss")
    dp_index = lax.axis_index("dp").astype(jnp.int32)[None]
    mp_index = lax.axis_index("mp").astype(jnp.int32)[None]
    loss_index = lax.axis_index("loss").astype(jnp.int32)[None]
    row_count, width = patches.shape
    hidden = fc1_weight.shape[1]
    share_rows = row_count // mp_size
    images = counts.shape[1]
    all_images = labels.shape[0]
    padded = -(-row_count // dp_size // 8) * 8
    fc1_t = fc1_weight.T
    plan = owners[0]
    matmul = 2 * row_count * width * hidden
    weight_bytes = 2 * width * hidden

    outgoing, text_copies = call(
        functools.partial(pack_kernel, padded=padded),
        (shape((dp_size * padded, width), bf16), shape((all_images, width), bf16)),
        [scalars, scalars, whole, whole],
        (dp_index, plan, patches, text_embed),
    )
    incoming = exchange(outgoing, "dp")
    texts = exchange(text_copies, "loss")

    patches, outgoing = lax.optimization_barrier((patches, outgoing))
    partial_sums = call(
        functools.partial(pool_kernel, share=1.0 / mp_size),
        shape((images, width), f32),
        [scalars, scalars] + [whole] * 6,
        (dp_index, counts, patches, layer_norm_gain, layer_norm_bias, fc1_t, fc1_bias, fc2_weight),
        flops=matmul,
        read=2 * weight_bytes,
    )
    slab_sums = jnp.sum(lax.all_gather(partial_sums, "mp", axis=0), axis=0)
    slope, rows, member = call(
        slope_kernel,
        (shape((row_count, hidden), f32), shape((row_count, width), bf16), shape((row_count, images), f32)),
        [scalars, scalars] + [whole] * 6,
        (dp_index, counts, plan, incoming, layer_norm_gain, layer_norm_bias, fc1_t, fc1_bias),
        flops=matmul,
        read=2 * weight_bytes,
    )
    slab_sums, slope = lax.optimization_barrier((slab_sums, slope))
    pieces = lax.all_gather(slab_sums, "dp", axis=0)
    upstream, parts = call(
        embed_kernel,
        (shape((images, width), f32), shape((all_images, width + LANES), bf16)),
        [scalars] * 5 + [whole] * 2,
        (loss_index, counts, labels, logit_scale, logit_bias, pieces, texts),
    )
    steps = (2, 1, 3)
    *remote, d_act = call(
        functools.partial(back_kernel, steps=steps, ring=mp_size),
        [shape((share_rows, width), bf16)] * len(steps) + [shape((2 * images, hidden), bf16)],
        [scalars] + [whole] * 5,
        (mp_index, upstream, member, slope, fc1_t, fc2_weight),
        flops=matmul,
        read=2 * weight_bytes,
    )
    received = []
    for chunk, step in zip(remote, steps):
        pairs = [(i, (i + step) % mp_size) for i in range(mp_size)]
        received.append(lax.ppermute(chunk, "mp", pairs))
    first_row = mp_index[0] * share_rows
    own_rows = lax.dynamic_slice_in_dim(rows, first_row, share_rows, 0)
    own_member = lax.dynamic_slice_in_dim(member, first_row, share_rows, 0)
    own_slope = lax.dynamic_slice_in_dim(slope, first_row, share_rows, 0)
    own_back = call(
        own_kernel,
        shape((share_rows, width), f32),
        [whole] * 4,
        (d_act, own_member, own_slope, fc1_t),
        flops=matmul // mp_size,
        read=weight_bytes,
    )
    all_parts = exchange(parts, "loss").reshape(loss_size, images, width + LANES)
    grad_text, loss = call(
        text_kernel,
        (shape((images, width), f32), shape((1, 1), f32)),
        [whole] * 2,
        (all_parts, text_embed),
    )
    grad_rows = call(
        row_kernel,
        shape((share_rows, width), f32),
        [whole] * 8,
        (own_back, *received, own_rows, layer_norm_gain, own_member, upstream),
    )
    return (grad_rows, grad_text, loss[0, 0])


def solution(mesh):
    placed = (
        P(("dp", "loss"), None),
        P(),
        P(),
        P(None, "mp"),
        P("mp"),
        P("mp", None),
        P("loss", None),
        P("loss", None, None),
        P("loss", None),
        P(),
        P(),
        P(),
    )
    return jax.shard_map(
        shards,
        mesh=mesh,
        in_specs=placed,
        out_specs=(P(("dp", "loss", "mp"), None), P("loss", None), P()),
        check_vma=False,
    )
```

time: 161 us -> 150 us (0.932)
  blocking collectives: 42.8 us -> 35.7 us
  starting transfers between devices: 37.1 us -> 41.6 us
  local copies, waits for them, and re-layouts: 18.7 us -> 14.9 us
  waiting for transfers between devices: 38.7 us -> 36.4 us
    unnamed x29 -> x46, local copies, waits for them, and re-layouts: 8.86 us -> 13.9 us
    broadcast_in_dim x6 -> x0, local copies, waits for them, and re-layouts: 4.42 us -> none  [the longest x2 2.19 us: gather_by_exchange(): copies = jnp.broadcast_to(block[None], (lax.axis_size(axis),) + block.shape)]
    all_to_all x3, starting transfers between devices: 25.5 us -> 29.8 us  [exchange(): return lax.all_to_all(block, axis, split_axis=0, concat_axis=0, tiled=True)]
    all_gather x1, blocking collectives: 21.8 us -> 17.8 us  [shards(): pieces = lax.all_gather(slab_sums, 'dp', axis=0)]
    all_gather x1, blocking collectives: 21 us -> 17.9 us  [shards(): slab_sums = jnp.sum(lax.all_gather(partial_sums, 'mp', axis=0), axis=0)]
    gather x1 -> x0, local copies, waits for them, and re-layouts: 2.74 us -> none  [shards(): outgoing = patches.reshape(dp_size, block_rows, width)[order]]
    reshape x2 -> x0, local copies, waits for them, and re-layouts: 2.34 us -> none  [the longest x1 1.29 us: shards(): local_rows = incoming.reshape(row_count, width)]
    all_to_all x3, waiting for transfers between devices: 26.9 us -> 24.7 us  [exchange(): return lax.all_to_all(block, axis, split_axis=0, concat_axis=0, tiled=True)]
  transfers between devices with their start and end apart: 6 -> 6, of which waited for: 4 -> 3; matrix products, arithmetic and copies ran while one was open for 7% -> 1% of each run, Pallas kernels for 5% -> 9%
where the time goes in v2:
time: 150 us; the launch traced here: 149 us
  starting transfers between devices  41.6 us (28%)
  waiting for transfers between devices  36.4 us (24%)
  blocking collectives  35.7 us (24%)
  Pallas kernels  18.4 us (12%)
  local copies, waits for them, and re-layouts  14.9 us (10%)
  between operations  2.18 us (1%)
    all_to_all x3, starting transfers between devices, exchange(): return lax.all_to_all(block, axis, split_axis=0, concat_axis=0, tiled=True)  29.8 us
    all_to_all x3, waiting for transfers between devices, exchange(): return lax.all_to_all(block, axis, split_axis=0, concat_axis=0, tiled=True)  24.7 us
    pallas_call x8, Pallas kernels, call(): pl.pallas_call(kernel, out_shape=outs, in_specs=specs, out_specs=jax.tree...  18.4 us
    all_gather x1, blocking collectives, shards(): slab_sums = jnp.sum(lax.all_gather(partial_sums, 'mp', axis=0), axis=0)  17.9 us
    all_gather x1, blocking collectives, shards(): pieces = lax.all_gather(slab_sums, 'dp', axis=0)  17.8 us
    unnamed x46, local copies, waits for them, and re-layouts  13.9 us
    ppermute x3, starting transfers between devices, shards(): received.append(lax.ppermute(chunk, 'mp', pairs))  11.9 us
    ppermute x3, waiting for transfers between devices, shards(): received.append(lax.ppermute(chunk, 'mp', pairs))  11.7 us
  transfers between devices with their start and end apart: 6, of which 3 were waited for; matrix products, arithmetic and copies ran while one was open for 1% of the time, Pallas kernels for 9%

profile of v2, /device:TPU:1, one launch (start us, length us, event | category | flops | bytes accessed | tf_op | source)
XLA Modules:
  0.0 149.2 jit_solution(4834978386889471117)
XLA Ops:
  0.6 0.0 copy-start
  0.6 0.0 copy-start.2
  0.7 1.3 copy-done.2
  1.9 0.0 copy-start.11
  1.9 0.7 copy-done.11
  2.6 0.0 copy-start.17
  2.6 0.7 copy-done.17
  3.3 0.0 copy-start.10
  3.3 0.0 copy-start.14
  3.3 0.0 copy-start.15
  3.3 0.0 copy-start.19
  3.3 1.3 shard_map.139
  4.7 0.0 copy-start.6
  4.7 0.9 copy-done.6
  5.6 0.0 copy-start.7
  5.6 0.7 copy-done.7
  6.3 17.6 %all-to-all-start = ((bf16[16,24,1152]{2,1,0:T(8,128)(2,1)}), bf16[16,24,1152]{2,1,0:T(8,128)(2,1)S(1)}, u32[]{:S(2)}, u32[]{:S(2)}) async-start(bf16[16,24,1152]{2,1,0:T(8,128)(2,1)} %bitcast.20), calls=%async_computation | async-start | bytes 1769472 | tf_op jit(solution)/shard_map/all_to_all | solution.py:266
  23.9 24.7 %all-to-all-done = bf16[16,24,1152]{2,1,0:T(8,128)(2,1)S(1)} async-done(((bf16[16,24,1152]{2,1,0:T(8,128)(2,1)}), bf16[16,24,1152]{2,1,0:T(8,128)(2,1)S(1)}, u32[]{:S(2)}, u32[]{:S(2)}) %all-to-all-start) | async-done | bytes 884768 | tf_op jit(solution)/shard_map/all_to_all | solution.py:266
  48.6 4.2 %all-to-all-start.1 = ((bf16[16,8,1152]{2,1,0:T(8,128)(2,1)}), bf16[16,8,1152]{2,1,0:T(8,128)(2,1)}, u32[]{:S(2)}, u32[]{:S(2)}) async-start(bf16[16,8,1152]{2,1,0:T(8,128)(2,1)} %bitcast.21), calls=%async_computation.1 | async-start | bytes 589824 | tf_op jit(solution)/shard_map/all_to_all | solution.py:266
  52.8 0.0 copy-done
  52.8 0.0 copy-done.10
  52.8 0.0 copy-done.14
  52.8 0.0 copy-done.15
  52.8 0.0 copy-done.19
  52.8 0.0 copy-start.1
  52.8 1.7 %copy-done.1 = bf16[1076,1152]{1,0:T(8,128)(2,1)S(1)} copy-done((bf16[1076,1152]{1,0:T(8,128)(2,1)S(1)}, bf16[1076,1152]{1,0:T(8,128)(2,1)}, u32[]{:S(2)}) %copy-start.1) | copy-done | bytes 2479128
  54.5 0.0 copy-start.3
  54.5 1.1 copy-done.3
  55.6 4.6 %shard_map.140 = f32[8,1152]{1,0:T(8,128)S(1)} custom-call(s32[1]{0:T(128)} %bitcast.2.dp_ref, s32[1,8]{1,0:T(1,128)S(1)} %copy-done.19, bf16[320,1152]{1,0:T(8,128)(2,1)S(1)} %copy-done.3, f32[1152]{0:T(1024)S(1)} %copy-done.10, f32[1152]{0:T(1024)S(1)} %copy-done.14, bf16[1076,1152]{1,0:T(8,128)(2,1)S(1)} %bitcast.14, f32[1076]{0:T(1024)S(1)} %copy-done.15, ...), custom_call_target="tpu_custom_call" | custom-call | flops 793313280 | bytes 4958208 | tf_op jit(solution)/shard_map/pallas_call | solution.py:251
  61.6 17.9 %all-gather = f32[32,1152]{1,0:T(8,128)S(1)} all-gather(f32[8,1152]{1,0:T(8,128)S(1)} %shard_map.140), channel_id=2, replica_groups=mesh['dp'=16,'loss'=16,'mp'=4] {'mp'}, dimensions={0}, use_global_device_ids=true | all-gather | bytes 184320 | tf_op jit(solution)/shard_map/all_gather | solution.py:318
  79.5 0.0 copy-start.16
  79.5 0.7 copy-done.16
  80.2 0.0 copy-start.18
  80.2 0.7 copy-done.18
  80.9 0.7 copy-done.20
  81.5 3.1 %shard_map.141 = (f32[320,1076]{1,0:T(8,128)S(1)}, bf16[320,1152]{1,0:T(8,128)(2,1)S(1)}, f32[320,8]{1,0:T(8,128)S(1)}) custom-call(s32[1]{0:T(128)} %bitcast.2.dp_ref, s32[1,8]{1,0:T(1,128)S(1)} %copy-done.20, s32[16,16]{1,0:T(8,128)S(1)} %bitcast.23, bf16[384,1152]{1,0:T(8,128)(2,1)S(1)} %bitcast.18, f32[1152]{0:T(1024)S(1)} %copy-done.10, ...), custom_call_target="tpu_custom_call" | custom-call | flops 793313280 | bytes 4958208 | tf_op jit(solution)/shard_map/pallas_call | solution.py:251
  84.6 0.0 copy-start.4
  84.6 1.1 copy-done.4
  85.7 0.9 copy-done.13
  86.6 17.8 %all-gather.1 = f32[128,1152]{1,0:T(8,128)S(1)} all-gather(f32[8,1152]{1,0:T(8,128)S(1)} %bitcast_reduce_fusion), channel_id=3, replica_groups=mesh['dp'=16,'loss'=16,'mp'=4] {'dp'}, dimensions={0}, use_global_device_ids=true | all-gather | bytes 626688 | tf_op jit(solution)/shard_map/all_gather | solution.py:328
  104.4 0.0 all-to-all-done.1
  104.4 0.7 copy-done.21
  105.1 0.7 copy-done.22
  105.8 2.4 %shard_map.142 = (f32[8,1152]{1,0:T(8,128)S(1)}, bf16[128,1280]{1,0:T(8,128)(2,1)}) custom-call(s32[1]{0:T(128)} %bitcast.1.loss_ref, s32[1,8]{1,0:T(1,128)S(1)} %copy-done.21, s32[128]{0:T(128)S(1)} %copy-done.22, f32[1]{0:T(128)S(6)} %copy.15.scale_ref, f32[1]{0:T(128)S(6)} %copy.16.shift_ref, f32[16,8,1152]{2,1,0:T(8,128)S(1)} %bitcast.19, ...), custom_call_target="tpu_custom_call" | custom-call | tf_op jit(solution)/shard_map/pallas_call | solution.py:251
  108.1 8.0 %all-to-all-start.2 = ((bf16[16,8,1280]{2,1,0:T(8,128)(2,1)}), bf16[16,8,1280]{2,1,0:T(8,128)(2,1)S(1)}, u32[]{:S(2)}, u32[]{:S(2)}) async-start(bf16[16,8,1280]{2,1,0:T(8,128)(2,1)} %bitcast.11), calls=%async_computation.2 | async-start | bytes 655360 | tf_op jit(solution)/shard_map/all_to_all | solution.py:266
  116.1 0.0 copy-start.5
  116.1 1.4 copy-done.5
  117.5 4.2 %shard_map.143 = (bf16[80,1152]{1,0:T(8,128)(2,1)S(1)}, bf16[80,1152]{1,0:T(8,128)(2,1)S(1)}, bf16[80,1152]{1,0:T(8,128)(2,1)S(1)}, bf16[16,1076]{1,0:T(8,128)(2,1)S(1)}) custom-call(s32[1]{0:T(128)} %bitcast.mp_ref, f32[8,1152]{1,0:T(8,128)S(1)} %get-tuple-element.24.upstream_ref, f32[320,8]{1,0:T(8,128)S(1)} %get-tuple-element.25.member_ref, ...), custom_call_target="tpu_custom_call" | custom-call | flops 793313280 | bytes 4958208 | tf_op jit(solution)/shard_map/pallas_call | solution.py:251
  121.7 0.0 copy-done.8
  121.7 0.0 copy-start.9
  121.7 4.0 %collective-permute-start = (bf16[80,1152]{1,0:T(8,128)(2,1)S(1)}, bf16[80,1152]{1,0:T(8,128)(2,1)S(1)}, u32[]{:S(2)}, u32[]{:S(2)}) collective-permute-start(bf16[80,1152]{1,0:T(8,128)(2,1)S(1)} %get-tuple-element.28), channel_id=1, source_target_pairs={{0,2},{1,3},{2,0},{3,1},{4,6},{5,7},{6,4},{7,5},{8,10},{9,11},{10,... | collective-permute-start | bytes 552968 | tf_op jit(solution)/shard_map/ppermute | solution.py:347
  125.7 5.7 %collective-permute-start.1 = (bf16[80,1152]{1,0:T(8,128)(2,1)S(1)}, bf16[80,1152]{1,0:T(8,128)(2,1)S(1)}, u32[]{:S(2)}, u32[]{:S(2)}) collective-permute-start(bf16[80,1152]{1,0:T(8,128)(2,1)S(1)} %get-tuple-element.29), channel_id=1, source_target_pairs={{0,1},{1,2},{2,3},{3,0},{4,5},{5,6},{6,7},{7,4},{8,9},{9,10},{10,1... | collective-permute-start | bytes 552968 | tf_op jit(solution)/shard_map/ppermute | solution.py:347
  131.5 2.1 %collective-permute-start.2 = (bf16[80,1152]{1,0:T(8,128)(2,1)S(1)}, bf16[80,1152]{1,0:T(8,128)(2,1)S(1)}, u32[]{:S(2)}, u32[]{:S(2)}) collective-permute-start(bf16[80,1152]{1,0:T(8,128)(2,1)S(1)} %get-tuple-element.30), channel_id=1, source_target_pairs={{0,3},{1,0},{2,1},{3,2},{4,7},{5,4},{6,5},{7,6},{8,11},{9,8},{10,9... | collective-permute-start | bytes 552968 | tf_op jit(solution)/shard_map/ppermute | solution.py:347
  133.7 0.0 copy-start.12
  133.7 0.8 shard_map.144.own_ref
  134.5 0.9 constant_dynamic-slice_fusion.x_ref
  135.4 0.0 collective-permute-done.first_ref
  135.4 7.1 %collective-permute-done.1.second_ref = bf16[80,1152]{1,0:T(8,128)(2,1)S(1)} collective-permute-done((bf16[80,1152]{1,0:T(8,128)(2,1)S(1)}, bf16[80,1152]{1,0:T(8,128)(2,1)S(1)}, u32[]{:S(2)}, u32[]{:S(2)}) %collective-permute-start.1) | collective-permute-done | bytes 184352 | tf_op jit(solution)/shard_map/ppermute | solution.py:347
  142.5 4.6 %collective-permute-done.2.third_ref = bf16[80,1152]{1,0:T(8,128)(2,1)S(1)} collective-permute-done((bf16[80,1152]{1,0:T(8,128)(2,1)S(1)}, bf16[80,1152]{1,0:T(8,128)(2,1)S(1)}, u32[]{:S(2)}, u32[]{:S(2)}) %collective-permute-start.2) | collective-permute-done | bytes 184352 | tf_op jit(solution)/shard_map/ppermute | solution.py:347
  147.1 0.0 copy-done.9
  147.1 1.2 shard_map.145
  148.4 0.0 all-to-all-done.2.parts_ref
  148.4 0.0 copy-done.12
  148.4 0.8 shard_map.146
  (8 shorter events, 0.1 us)
Async XLA Ops:
  0.6 52.1 %copy-start = (bf16[1152,1076]{0,1:T(8,128)(2,1)S(1)}, bf16[1152,1076]{0,1:T(8,128)(2,1)}, u32[]{:S(2)}) copy-start(bf16[1152,1076]{0,1:T(8,128)(2,1)} %param.15) | copy-start | bytes 7437316
  0.6 1.3 copy-start.2
  1.9 0.7 copy-start.11
  2.6 0.7 copy-start.17
  3.3 49.4 %copy-start.10 = (f32[1152]{0:T(1024)S(1)}, f32[1152]{0:T(1024)}, u32[]{:S(2)}) copy-start(f32[1152]{0:T(1024)} %gain_ref.5) | copy-start | bytes 13828
  3.3 49.4 %copy-start.14 = (f32[1152]{0:T(1024)S(1)}, f32[1152]{0:T(1024)}, u32[]{:S(2)}) copy-start(f32[1152]{0:T(1024)} %bias_ref.3) | copy-start | bytes 13828
  3.3 49.4 %copy-start.15 = (f32[1076]{0:T(1024)S(1)}, f32[1076]{0:T(1024)}, u32[]{:S(2)}) copy-start(f32[1076]{0:T(1024)} %b1_ref.3) | copy-start | bytes 12916
  3.3 49.5 %copy-start.19 = (s32[1,8]{1,0:T(1,128)S(1)}, s32[1,8]{1,0:T(1,128)}, u32[]{:S(2)}) copy-start(s32[1,8]{1,0:T(1,128)} %counts_ref.5) | copy-start | bytes 100
  4.7 0.9 copy-start.6
  5.6 0.7 copy-start.7
  6.3 42.3 %all-to-all-start = ((bf16[16,24,1152]{2,1,0:T(8,128)(2,1)}), bf16[16,24,1152]{2,1,0:T(8,128)(2,1)S(1)}, u32[]{:S(2)}, u32[]{:S(2)}) async-start(bf16[16,24,1152]{2,1,0:T(8,128)(2,1)} %bitcast.20), calls=%async_computation | async-start | bytes 1769472 | tf_op jit(solution)/shard_map/all_to_all | solution.py:266
  48.6 55.9 %all-to-all-start.1 = ((bf16[16,8,1152]{2,1,0:T(8,128)(2,1)}), bf16[16,8,1152]{2,1,0:T(8,128)(2,1)}, u32[]{:S(2)}, u32[]{:S(2)}) async-start(bf16[16,8,1152]{2,1,0:T(8,128)(2,1)} %bitcast.21), calls=%async_computation.1 | async-start | bytes 589824 | tf_op jit(solution)/shard_map/all_to_all | solution.py:266
  52.8 1.7 %copy-start.1 = (bf16[1076,1152]{1,0:T(8,128)(2,1)S(1)}, bf16[1076,1152]{1,0:T(8,128)(2,1)}, u32[]{:S(2)}) copy-start(bf16[1076,1152]{1,0:T(8,128)(2,1)} %w2_ref.3) | copy-start | bytes 7437316
  54.5 1.1 copy-start.3
  79.5 0.7 copy-start.16
  80.2 0.7 copy-start.18
  80.9 0.7 copy-start.20
  84.6 1.1 copy-start.4
  85.7 0.9 copy-start.13
  104.4 0.7 copy-start.21
  105.1 0.7 copy-start.22
  108.1 13.6 %copy-start.8 = (f32[8,1152]{1,0:T(8,128)}, f32[8,1152]{1,0:T(8,128)S(1)}, u32[]{:S(2)}) copy-start(f32[8,1152]{1,0:T(8,128)S(1)} %get-tuple-element.24.upstream_ref) | copy-start | bytes 110596
  108.1 40.3 %all-to-all-start.2 = ((bf16[16,8,1280]{2,1,0:T(8,128)(2,1)}), bf16[16,8,1280]{2,1,0:T(8,128)(2,1)S(1)}, u32[]{:S(2)}, u32[]{:S(2)}) async-start(bf16[16,8,1280]{2,1,0:T(8,128)(2,1)} %bitcast.11), calls=%async_computation.2 | async-start | bytes 655360 | tf_op jit(solution)/shard_map/all_to_all | solution.py:266
  116.1 1.4 copy-start.5
  121.7 25.4 %copy-start.9 = (f32[8,1152]{1,0:T(8,128)S(1)}, f32[8,1152]{1,0:T(8,128)}, u32[]{:S(2)}) copy-start(f32[8,1152]{1,0:T(8,128)} %copy-done.8) | copy-start | bytes 110596
  121.7 13.7 %collective-permute-start = (bf16[80,1152]{1,0:T(8,128)(2,1)S(1)}, bf16[80,1152]{1,0:T(8,128)(2,1)S(1)}, u32[]{:S(2)}, u32[]{:S(2)}) collective-permute-start(bf16[80,1152]{1,0:T(8,128)(2,1)S(1)} %get-tuple-element.28), channel_id=1, source_target_pairs={{0,2},{1,3},{2,0},{3,1},{4,6},{5,7},{6,4},{7,5},{8,10},{9,11},{10,... | collective-permute-start | bytes 552968 | tf_op jit(solution)/shard_map/ppermute | solution.py:347
  125.7 16.8 %collective-permute-start.1 = (bf16[80,1152]{1,0:T(8,128)(2,1)S(1)}, bf16[80,1152]{1,0:T(8,128)(2,1)S(1)}, u32[]{:S(2)}, u32[]{:S(2)}) collective-permute-start(bf16[80,1152]{1,0:T(8,128)(2,1)S(1)} %get-tuple-element.29), channel_id=1, source_target_pairs={{0,1},{1,2},{2,3},{3,0},{4,5},{5,6},{6,7},{7,4},{8,9},{9,10},{10,1... | collective-permute-start | bytes 552968 | tf_op jit(solution)/shard_map/ppermute | solution.py:347
  131.5 15.6 %collective-permute-start.2 = (bf16[80,1152]{1,0:T(8,128)(2,1)S(1)}, bf16[80,1152]{1,0:T(8,128)(2,1)S(1)}, u32[]{:S(2)}, u32[]{:S(2)}) collective-permute-start(bf16[80,1152]{1,0:T(8,128)(2,1)S(1)} %get-tuple-element.30), channel_id=1, source_target_pairs={{0,3},{1,0},{2,1},{3,2},{4,7},{5,4},{6,5},{7,6},{8,11},{9,8},{10,9... | collective-permute-start | bytes 552968 | tf_op jit(solution)/shard_map/ppermute | solution.py:347
  133.7 14.7 %copy-start.12 = (bf16[8,1152]{1,0:T(8,128)(2,1)S(1)}, bf16[8,1152]{1,0:T(8,128)(2,1)}, u32[]{:S(2)}) copy-start(bf16[8,1152]{1,0:T(8,128)(2,1)} %text_ref.3) | copy-start | bytes 55300

commit v3 on v2

--- a/solution.py
+++ b/solution.py
@@ -12,9 +12,10 @@
 gelu_coef = 0.7978845608028654
 f32 = jnp.float32
 bf16 = jnp.bfloat16
-VMEM_LIMIT = 48 * 1024 * 1024
+VMEM_LIMIT = 28 * 1024 * 1024
 whole = pl.BlockSpec(memory_space=pltpu.VMEM)
 scalars = pl.BlockSpec(memory_space=pltpu.SMEM)
+stored = pl.BlockSpec(memory_space=pltpu.HBM)
 NT = (((1,), (1,)), ((), ()))
 TN = (((0,), (0,)), ((), ()))
 LANES = 128
@@ -37,6 +38,16 @@
     return high, (values - high.astype(f32)).astype(bf16)
 
 
+def fetch(sources, targets, semaphores):
+    copies = [
+        pltpu.make_async_copy(source, target, semaphores.at[k])
+        for k, (source, target) in enumerate(zip(sources, targets))
+    ]
+    for copy in copies:
+        copy.start()
+    return copies
+
+
 def split_three(values):
     high, rest = split_bf16(values)
     return high, rest, (values - high.astype(f32) - rest.astype(f32)).astype(bf16)
@@ -54,20 +65,21 @@
     return jnp.where(condition, 1.0, 0.0).astype(bf16)
 
 
-def pack_kernel(dp_ref, owners_ref, x_ref, text_ref, out_ref, copies_ref, *, padded):
+def pack_kernel(dp_ref, owners_hbm, x_hbm, out_ref, owners_ref, x_ref, semaphores, *, padded):
+    copies = fetch((owners_hbm.at[0], x_hbm), (owners_ref, x_ref), semaphores)
     rows = x_ref.shape[0]
     slots = owners_ref.shape[0]
     block_rows = rows // slots
     block = quotient(iota((1, rows), 1), block_rows)
     within = iota((1, rows), 1) - block * block_rows
     owner = jnp.zeros((1, rows), jnp.int32)
+    copies[0].wait()
     for b in range(slots):
         owner = jnp.where(block == b, owners_ref[dp_ref[0], b], owner)
     target = owner * padded + within
     pick = one_hot(iota((slots * padded, rows), 0) == target)
+    copies[1].wait()
     out_ref[...] = jnp.dot(pick, x_ref[...], preferred_element_type=f32).astype(bf16)
-    text = text_ref[...].astype(f32)
-    copies_ref[...] = jnp.concatenate([text] * (copies_ref.shape[0] // text.shape[0]), axis=0).astype(bf16)
 
 
 def image_bounds(counts_ref, dims, axis):
@@ -83,7 +95,34 @@
     return starts, ends
 
 
-def pool_kernel(dp_ref, counts_ref, x_ref, gain_ref, bias_ref, w1t_ref, b1_ref, w2_ref, out_ref, *, share):
+def pool_kernel(
+    dp_ref,
+    counts_hbm,
+    x_hbm,
+    gain_hbm,
+    bias_hbm,
+    b1_hbm,
+    w1t_hbm,
+    w2_hbm,
+    out_ref,
+    counts_ref,
+    x_ref,
+    gain_ref,
+    bias_ref,
+    b1_ref,
+    w1t_ref,
+    w2_ref,
+    semaphores,
+    *,
+    share,
+):
+    copies = fetch(
+        (counts_hbm, x_hbm, gain_hbm, bias_hbm, b1_hbm, w1t_hbm, w2_hbm),
+        (counts_ref, x_ref, gain_ref, bias_ref, b1_ref, w1t_ref, w2_ref),
+        semaphores,
+    )
+    for copy in copies[:5]:
+        copy.wait()
     rows = x_ref.shape[0]
     images = counts_ref.shape[1]
     position = dp_ref[0] * rows + iota((images, rows), 1)
@@ -94,6 +133,8 @@
     normed = (xhat * gain_ref[...][None, :] + bias_ref[...][None, :]).astype(bf16)
     offset = b1_ref[...][None, :]
     total = share * jnp.dot(member, x, preferred_element_type=f32)
+    for copy in copies[5:]:
+        copy.wait()
     for first, many in column_chunks(w1t_ref.shape[0], 256):
         cols = slice(first, first + many)
         pre = lax.dot_general(normed, w1t_ref[cols, :], NT, preferred_element_type=f32) + offset[:, cols]
@@ -107,8 +148,33 @@
 
 
 def slope_kernel(
-    dp_ref, counts_ref, owners_ref, in_ref, gain_ref, bias_ref, w1t_ref, b1_ref, slope_ref, rows_ref, member_ref
+    dp_ref,
+    in_ref,
+    counts_hbm,
+    owners_hbm,
+    gain_hbm,
+    bias_hbm,
+    b1_hbm,
+    text_hbm,
+    w1t_hbm,
+    slope_ref,
+    rows_ref,
+    member_ref,
+    texts_ref,
+    counts_ref,
+    owners_ref,
+    gain_ref,
+    bias_ref,
+    b1_ref,
+    text_ref,
+    w1t_ref,
+    semaphores,
 ):
+    copies = fetch(
+        (counts_hbm, owners_hbm.at[0], gain_hbm, bias_hbm, b1_hbm, text_hbm, w1t_hbm),
+        (counts_ref, owners_ref, gain_ref, bias_ref, b1_ref, text_ref, w1t_ref),
+        semaphores,
+    )
     rows = rows_ref.shape[0]
     slots = owners_ref.shape[0]
     block_rows = rows // slots
@@ -118,6 +184,10 @@
     pick = one_hot(iota((rows, in_ref.shape[0]), 1) == source * padded + within)
     x = jnp.dot(pick, in_ref[...], preferred_element_type=f32)
     rows_ref[...] = x.astype(bf16)
+    for copy in copies[:6]:
+        copy.wait()
+    text = text_ref[...].astype(f32)
+    texts_ref[...] = jnp.concatenate([text] * (texts_ref.shape[0] // text.shape[0]), axis=0).astype(bf16)
     block = jnp.where(owners_ref[...] == dp_ref[0], iota((slots, slots), 1), 0)
     block = jnp.sum(block.astype(f32), axis=1, keepdims=True)
     by_source = one_hot(iota((rows, slots), 1) == source)
@@ -128,6 +198,7 @@
     xhat, _ = layer_statistics(x)
     normed = (xhat * gain_ref[...][None, :] + bias_ref[...][None, :]).astype(bf16)
     offset = b1_ref[...][None, :]
+    copies[6].wait()
     for first, many in column_chunks(w1t_ref.shape[0], 256):
         cols = slice(first, first + many)
         pre = lax.dot_general(normed, w1t_ref[cols, :], NT, preferred_element_type=f32) + offset[:, cols]
@@ -142,13 +213,36 @@
     return jnp.minimum(values, 0.0) - jnp.log1p(jnp.exp(-jnp.abs(values)))
 
 
-def embed_kernel(
-    loss_ref, counts_ref, labels_ref, scale_ref, shift_ref, pieces_ref, texts_ref, upstream_ref, parts_ref
+def gradient_kernel(
+    loss_ref,
+    mp_ref,
+    scale_ref,
+    shift_ref,
+    pieces_ref,
+    texts_ref,
+    member_ref,
+    slope_ref,
+    counts_hbm,
+    labels_hbm,
+    w2_hbm,
+    w1t_hbm,
+    upstream_ref,
+    parts_ref,
+    d_act_ref,
+    *refs,
+    steps,
+    ring,
 ):
+    outs, (counts_ref, labels_ref, w2_ref, w1t_ref, semaphores) = refs[: len(steps)], refs[len(steps) :]
+    copies = fetch(
+        (counts_hbm, labels_hbm, w2_hbm, w1t_hbm), (counts_ref, labels_ref, w2_ref, w1t_ref), semaphores
+    )
     total = pieces_ref[0]
     for k in range(1, pieces_ref.shape[0]):
         total = total + pieces_ref[k]
     images, width = total.shape
+    copies[0].wait()
+    copies[1].wait()
     texts = texts_ref[...]
     all_images = texts.shape[0]
     image = iota((images, 1), 0)
@@ -192,21 +286,20 @@
     lane = iota((all_images, LANES), 1)
     loss_lanes = jnp.where(lane == 0, loss_high.astype(f32), jnp.where(lane == 1, loss_low.astype(f32), 0.0))
     parts_ref[:, width:] = loss_lanes.astype(bf16)
-
-
-def back_kernel(
-    mp_ref, upstream_ref, member_ref, slope_ref, w1t_ref, w2_ref, *refs, steps, ring
-):
-    outs, d_act_ref = refs[:-1], refs[-1]
-    share = outs[0].shape[0]
+    copies[2].wait()
     d_image = upstream_ref[...].astype(bf16)
     d_act = lax.dot_general(d_image, w2_ref[...], NT, preferred_element_type=f32)
     both = jnp.concatenate(split_bf16(d_act), axis=0)
     d_act_ref[...] = both
+    copies[3].wait()
+    share = outs[0].shape[0]
     for out_ref, step in zip(outs, steps):
-        first = pl.multiple_of(lax.rem(mp_ref[0] + step, ring) * share, share)
-        rows = pl.ds(first, share)
+        rows = own_range(mp_ref, step, ring, share)
         out_ref[...] = back_rows(member_ref[rows, :], both, slope_ref[rows, :], w1t_ref[...]).astype(bf16)
+
+
+def own_range(mp_ref, step, ring, share):
+    return pl.ds(pl.multiple_of(lax.rem(mp_ref[0] + step, ring) * share, share), share)
 
 
 def back_rows(member, both, slope, w1t):
@@ -216,21 +309,42 @@
     return jnp.dot(d_pre, w1t, preferred_element_type=f32)
 
 
-def own_kernel(d_act_ref, member_ref, slope_ref, w1t_ref, out_ref):
-    out_ref[...] = back_rows(member_ref[...], d_act_ref[...], slope_ref[...], w1t_ref[...])
-
-
-def row_kernel(own_ref, first_ref, second_ref, third_ref, x_ref, gain_ref, member_ref, upstream_ref, out_ref):
+def own_kernel(mp_ref, d_act_ref, member_ref, slope_ref, w1t_hbm, out_ref, w1t_ref, semaphores, *, ring):
+    copies = fetch((w1t_hbm,), (w1t_ref,), semaphores)
+    rows = own_range(mp_ref, 0, ring, out_ref.shape[0])
+    copies[0].wait()
+    out_ref[...] = back_rows(member_ref[rows, :], d_act_ref[...], slope_ref[rows, :], w1t_ref[...])
+
+
+def row_kernel(
+    mp_ref,
+    own_ref,
+    first_ref,
+    second_ref,
+    third_ref,
+    x_ref,
+    member_ref,
+    upstream_ref,
+    gain_hbm,
+    out_ref,
+    gain_ref,
+    semaphores,
+    *,
+    ring,
+):
+    copies = fetch((gain_hbm,), (gain_ref,), semaphores)
+    rows = own_range(mp_ref, 0, ring, out_ref.shape[0])
     back = own_ref[...] + first_ref[...].astype(f32)
     back = back + second_ref[...].astype(f32) + third_ref[...].astype(f32)
-    xhat, inverse_deviation = layer_statistics(x_ref[...].astype(f32))
+    xhat, inverse_deviation = layer_statistics(x_ref[rows, :].astype(f32))
+    copies[0].wait()
     dxhat = back * gain_ref[...][None, :]
     dx = inverse_deviation * (
         dxhat
         - jnp.mean(dxhat, axis=-1, keepdims=True)
         - xhat * jnp.mean(dxhat * xhat, axis=-1, keepdims=True)
     )
-    upstream = jnp.dot(member_ref[...], upstream_ref[...], precision=HIGHEST, preferred_element_type=f32)
+    upstream = jnp.dot(member_ref[rows, :], upstream_ref[...], precision=HIGHEST, preferred_element_type=f32)
     out_ref[...] = dx + upstream
 
 
@@ -247,15 +361,18 @@
     loss_ref[...] = jnp.sum(total[:1, width:], axis=1, keepdims=True)
 
 
-def call(kernel, outs, specs, operands, flops=0, read=0):
+def call(kernel, outs, operands, scratch=(), flops=0, read=0):
+    fetched = sum(space is stored for space, _ in operands)
+    extra = [pltpu.SemaphoreType.DMA((fetched,))] if fetched else []
     return pl.pallas_call(
         kernel,
         out_shape=outs,
-        in_specs=specs,
+        in_specs=[space for space, _ in operands],
         out_specs=jax.tree.map(lambda _: whole, outs),
+        scratch_shapes=list(scratch) + extra,
         compiler_params=pltpu.CompilerParams(vmem_limit_bytes=VMEM_LIMIT),
         cost_estimate=pl.CostEstimate(flops=flops, bytes_accessed=read, transcendentals=0),
-    )(*operands)
+    )(*[pltpu.with_memory_space_constraint(array, pltpu.HBM) if space is stored else array for space, array in operands])
 
 
 def shape(dims, kind):
@@ -293,82 +410,114 @@
     all_images = labels.shape[0]
     padded = -(-row_count // dp_size // 8) * 8
     fc1_t = fc1_weight.T
-    plan = owners[0]
     matmul = 2 * row_count * width * hidden
     weight_bytes = 2 * width * hidden
 
-    outgoing, text_copies = call(
+    gain, bias, offset = layer_norm_gain, layer_norm_bias, fc1_bias
+    gain_room, offset_room = pltpu.VMEM((width,), f32), pltpu.VMEM((hidden,), f32)
+    plan_dims, counts_dims = owners.shape[1:], counts.shape
+    first_room, second_room = pltpu.VMEM((hidden, width), bf16), pltpu.VMEM((hidden, width), bf16)
+
+    outgoing = call(
         functools.partial(pack_kernel, padded=padded),
-        (shape((dp_size * padded, width), bf16), shape((all_images, width), bf16)),
-        [scalars, scalars, whole, whole],
-        (dp_index, plan, patches, text_embed),
+        shape((dp_size * padded, width), bf16),
+        [(scalars, dp_index), (stored, owners), (stored, patches)],
+        [pltpu.SMEM(plan_dims, jnp.int32), pltpu.VMEM((row_count, width), bf16)],
     )
     incoming = exchange(outgoing, "dp")
-    texts = exchange(text_copies, "loss")
 
     patches, outgoing = lax.optimization_barrier((patches, outgoing))
     partial_sums = call(
         functools.partial(pool_kernel, share=1.0 / mp_size),
         shape((images, width), f32),
-        [scalars, scalars] + [whole] * 6,
-        (dp_index, counts, patches, layer_norm_gain, layer_norm_bias, fc1_t, fc1_bias, fc2_weight),
+        [(scalars, dp_index)]
+        + [(stored, array) for array in (counts, patches, gain, bias, offset, fc1_t, fc2_weight)],
+        [
+            pltpu.SMEM(counts_dims, jnp.int32),
+            pltpu.VMEM((row_count, width), bf16),
+            gain_room,
+            gain_room,
+            offset_room,
+            first_room,
+            second_room,
+        ],
         flops=matmul,
         read=2 * weight_bytes,
     )
     slab_sums = jnp.sum(lax.all_gather(partial_sums, "mp", axis=0), axis=0)
-    slope, rows, member = call(
+    incoming, slab_sums = lax.optimization_barrier((incoming, slab_sums))
+    slope, rows, member, text_copies = call(
         slope_kernel,
-        (shape((row_count, hidden), f32), shape((row_count, width), bf16), shape((row_count, images), f32)),
-        [scalars, scalars] + [whole] * 6,
-        (dp_index, counts, plan, incoming, layer_norm_gain, layer_norm_bias, fc1_t, fc1_bias),
+        (
+            shape((row_count, hidden), f32),
+            shape((row_count, width), bf16),
+            shape((row_count, images), f32),
+            shape((all_images, width), bf16),
+        ),
+        [(scalars, dp_index), (whole, incoming)]
+        + [(stored, array) for array in (counts, owners, gain, bias, offset, text_embed, fc1_t)],
+        [
+            pltpu.SMEM(counts_dims, jnp.int32),
+            pltpu.VMEM(plan_dims, jnp.int32),
+            gain_room,
+            gain_room,
+            offset_room,
+            pltpu.VMEM((images, width), bf16),
+            first_room,
+        ],
         flops=matmul,
         read=2 * weight_bytes,
     )
+    texts = exchange(text_copies, "loss")
     slab_sums, slope = lax.optimization_barrier((slab_sums, slope))
     pieces = lax.all_gather(slab_sums, "dp", axis=0)
-    upstream, parts = call(
-        embed_kernel,
-        (shape((images, width), f32), shape((all_images, width + LANES), bf16)),
-        [scalars] * 5 + [whole] * 2,
-        (loss_index, counts, labels, logit_scale, logit_bias, pieces, texts),
-    )
     steps = (2, 1, 3)
-    *remote, d_act = call(
-        functools.partial(back_kernel, steps=steps, ring=mp_size),
-        [shape((share_rows, width), bf16)] * len(steps) + [shape((2 * images, hidden), bf16)],
-        [scalars] + [whole] * 5,
-        (mp_index, upstream, member, slope, fc1_t, fc2_weight),
+    upstream, parts, d_act, *chunks = call(
+        functools.partial(gradient_kernel, steps=steps, ring=mp_size),
+        [
+            shape((images, width), f32),
+            shape((all_images, width + LANES), bf16),
+            shape((2 * images, hidden), bf16),
+        ]
+        + [shape((share_rows, width), bf16)] * len(steps),
+        [(scalars, array) for array in (loss_index, mp_index, logit_scale, logit_bias)]
+        + [(whole, array) for array in (pieces, texts, member, slope)]
+        + [(stored, array) for array in (counts, labels, fc2_weight, fc1_t)],
+        [
+            pltpu.SMEM(counts_dims, jnp.int32),
+            pltpu.SMEM((all_images,), jnp.int32),
+            second_room,
+            first_room,
+        ],
         flops=matmul,
         read=2 * weight_bytes,
     )
     received = []
-    for chunk, step in zip(remote, steps):
+    for chunk, step in zip(chunks, steps):
         pairs = [(i, (i + step) % mp_size) for i in range(mp_size)]
         received.append(lax.ppermute(chunk, "mp", pairs))
-    first_row = mp_index[0] * share_rows
-    own_rows = lax.dynamic_slice_in_dim(rows, first_row, share_rows, 0)
-    own_member = lax.dynamic_slice_in_dim(member, first_row, share_rows, 0)
-    own_slope = lax.dynamic_slice_in_dim(slope, first_row, share_rows, 0)
     own_back = call(
-        own_kernel,
+        functools.partial(own_kernel, ring=mp_size),
         shape((share_rows, width), f32),
-        [whole] * 4,
-        (d_act, own_member, own_slope, fc1_t),
+        [(scalars, mp_index), (whole, d_act), (whole, member), (whole, slope), (stored, fc1_t)],
+        [first_room],
         flops=matmul // mp_size,
         read=weight_bytes,
     )
+    parts, own_back = lax.optimization_barrier((parts, own_back))
     all_parts = exchange(parts, "loss").reshape(loss_size, images, width + LANES)
     grad_text, loss = call(
         text_kernel,
         (shape((images, width), f32), shape((1, 1), f32)),
-        [whole] * 2,
-        (all_parts, text_embed),
+        [(whole, all_parts), (whole, text_embed)],
     )
     grad_rows = call(
-        row_kernel,
+        functools.partial(row_kernel, ring=mp_size),
         shape((share_rows, width), f32),
-        [whole] * 8,
-        (own_back, *received, own_rows, layer_norm_gain, own_member, upstream),
+        [(scalars, mp_index), (whole, own_back)]
+        + [(whole, array) for array in received]
+        + [(whole, rows), (whole, member), (whole, upstream), (stored, gain)],
+        [gain_room],
     )
     return (grad_rows, grad_text, loss[0, 0])
 

time: 150 us -> 121 us (0.81)
  waiting for transfers between devices: 36.4 us -> 18.3 us
  local copies, waits for them, and re-layouts: 14.9 us -> 0.02 us
  Pallas kernels: 18.4 us -> 22.9 us
  blocking collectives: 35.7 us -> 34 us
    all_to_all x3, waiting for transfers between devices: 24.7 us -> 5.06 us  [exchange(): return lax.all_to_all(block, axis, split_axis=0, concat_axis=0, tiled=True)]
    unnamed x46 -> x6, local copies, waits for them, and re-layouts: 13.9 us -> 0.02 us
    all_gather x1, blocking collectives: 17.9 us -> 13 us  [shards(): slab_sums = jnp.sum(lax.all_gather(partial_sums, 'mp', axis=0), axis=0)]
    pallas_call x8 -> x7, Pallas kernels: 18.4 us -> 22.9 us  [call(): pl.pallas_call(kernel, out_shape=outs, in_specs=[space for space, _ in op...]
    all_gather x1, blocking collectives: 17.8 us -> 20.9 us  [shards(): pieces = lax.all_gather(slab_sums, 'dp', axis=0)]
    ppermute x3, waiting for transfers between devices: 11.7 us -> 13.3 us  [shards(): received.append(lax.ppermute(chunk, 'mp', pairs))]
  transfers between devices with their start and end apart: 6 -> 6, of which waited for: 3 -> 3; matrix products, arithmetic and copies ran while one was open for 1% -> 0% of each run, Pallas kernels for 9% -> 7%
where the time goes in v3:
time: 121 us; the launch traced here: 120 us
  starting transfers between devices  42.3 us (35%)
  blocking collectives  34 us (28%)
  Pallas kernels  22.9 us (19%)
  waiting for transfers between devices  18.3 us (15%)
  between operations  2.09 us (2%)
    all_to_all x3, starting transfers between devices, exchange(): return lax.all_to_all(block, axis, split_axis=0, concat_axis=0, tiled=True)  29.6 us
    pallas_call x7, Pallas kernels, call(): pl.pallas_call(kernel, out_shape=outs, in_specs=[space for space, _ in op...  22.9 us
    all_gather x1, blocking collectives, shards(): pieces = lax.all_gather(slab_sums, 'dp', axis=0)  20.9 us
    ppermute x3, waiting for transfers between devices, shards(): received.append(lax.ppermute(chunk, 'mp', pairs))  13.3 us
    all_gather x1, blocking collectives, shards(): slab_sums = jnp.sum(lax.all_gather(partial_sums, 'mp', axis=0), axis=0)  13 us
    ppermute x3, starting transfers between devices, shards(): received.append(lax.ppermute(chunk, 'mp', pairs))  12.6 us
    all_to_all x3, waiting for transfers between devices, exchange(): return lax.all_to_all(block, axis, split_axis=0, concat_axis=0, tiled=True)  5.06 us
  transfers between devices with their start and end apart: 6, of which 3 were waited for; matrix products, arithmetic and copies ran while one was open for 0% of the time, Pallas kernels for 7%

profile of v3, /device:TPU:1, one launch (start us, length us, event | category | flops | bytes accessed | tf_op | source)
XLA Modules:
  0.0 119.6 jit_solution(8911815466889510476)
XLA Ops:
  0.6 2.7 %shard_map.139 = bf16[384,1152]{1,0:T(8,128)(2,1)} custom-call(s32[1]{0:T(128)} %bitcast.2.dp_ref, s32[1,16,16]{2,1,0:T(8,128)} %owners_hbm.3, bf16[320,1152]{1,0:T(8,128)(2,1)} %x_hbm.2), custom_call_target="tpu_custom_call" | custom-call | tf_op jit(solution)/shard_map/pallas_call | solution.py:367
  3.3 17.6 %all-to-all-start = ((bf16[16,24,1152]{2,1,0:T(8,128)(2,1)}), bf16[16,24,1152]{2,1,0:T(8,128)(2,1)S(1)}, u32[]{:S(2)}, u32[]{:S(2)}) async-start(bf16[16,24,1152]{2,1,0:T(8,128)(2,1)} %bitcast.3), calls=%async_computation | async-start | bytes 1769472 | tf_op jit(solution)/shard_map/all_to_all | solution.py:383
  20.9 6.6 %shard_map.140 = f32[8,1152]{1,0:T(8,128)S(1)} custom-call(s32[1]{0:T(128)} %bitcast.2.dp_ref, s32[1,8]{1,0:T(1,128)} %counts_hbm.5, bf16[320,1152]{1,0:T(8,128)(2,1)} %x_hbm.2, f32[1152]{0:T(1024)} %gain_hbm.5, f32[1152]{0:T(1024)} %bias_hbm.3, f32[1076]{0:T(1024)} %b1_hbm.3, bf16[1076,1152]{1,0:T(8,128)(2,1)} %bitcast.16, bf16[1076,1152]{1,0:T(8,128)(2,1)} %w2_hbm.3), custom_call_target="tpu_custom_call" | custom-call | flops 793313280 | bytes 4958208 | tf_op jit(solution)/shard_map/pallas_call | solution.py:367
  27.5 13.0 %all-gather = f32[32,1152]{1,0:T(8,128)S(1)} all-gather(f32[8,1152]{1,0:T(8,128)S(1)} %shard_map.140), channel_id=2, replica_groups=mesh['dp'=16,'loss'=16,'mp'=4] {'mp'}, dimensions={0}, use_global_device_ids=true | all-gather | bytes 184320 | tf_op jit(solution)/shard_map/all_gather | solution.py:447
  40.5 5.1 %all-to-all-done = bf16[16,24,1152]{2,1,0:T(8,128)(2,1)S(1)} async-done(((bf16[16,24,1152]{2,1,0:T(8,128)(2,1)}), bf16[16,24,1152]{2,1,0:T(8,128)(2,1)S(1)}, u32[]{:S(2)}, u32[]{:S(2)}) %all-to-all-start) | async-done | bytes 884768 | tf_op jit(solution)/shard_map/all_to_all | solution.py:383
  45.6 3.9 %shard_map.141 = (f32[320,1076]{1,0:T(8,128)S(1)}, bf16[320,1152]{1,0:T(8,128)(2,1)S(1)}, f32[320,8]{1,0:T(8,128)S(1)}, bf16[128,1152]{1,0:T(8,128)(2,1)}) custom-call(s32[1]{0:T(128)} %bitcast.2.dp_ref, bf16[384,1152]{1,0:T(8,128)(2,1)S(1)} %bitcast.13, s32[1,8]{1,0:T(1,128)} %counts_hbm.5, s32[1,16,16]{2,1,0:T(8,128)} %owners_hbm.3, f32[1152]{0:T(1024)} %gain_hbm.5, ...), custom_call_target="tpu_custom_call" | custom-call | flops 793313280 | bytes 4958208 | tf_op jit(solution)/shard_map/pallas_call | solution.py:367
  49.5 4.2 %all-to-all-start.1 = ((bf16[16,8,1152]{2,1,0:T(8,128)(2,1)}), bf16[16,8,1152]{2,1,0:T(8,128)(2,1)S(1)}, u32[]{:S(2)}, u32[]{:S(2)}) async-start(bf16[16,8,1152]{2,1,0:T(8,128)(2,1)} %bitcast.8), calls=%async_computation.1 | async-start | bytes 589824 | tf_op jit(solution)/shard_map/all_to_all | solution.py:383
  55.0 20.9 %all-gather.1 = f32[128,1152]{1,0:T(8,128)S(1)} all-gather(f32[8,1152]{1,0:T(8,128)S(1)} %bitcast_reduce_fusion), channel_id=3, replica_groups=mesh['dp'=16,'loss'=16,'mp'=4] {'dp'}, dimensions={0}, use_global_device_ids=true | all-gather | bytes 626688 | tf_op jit(solution)/shard_map/all_gather | solution.py:473
  75.9 0.0 all-to-all-done.1
  75.9 4.5 %shard_map.142 = (f32[8,1152]{1,0:T(8,128)S(1)}, bf16[128,1280]{1,0:T(8,128)(2,1)}, bf16[16,1076]{1,0:T(8,128)(2,1)S(1)}, bf16[80,1152]{1,0:T(8,128)(2,1)S(1)}, ...) custom-call(s32[1]{0:T(128)} %bitcast.1.loss_ref, s32[1]{0:T(128)} %bitcast.mp_ref, f32[1]{0:T(128)S(6)} %copy.15.scale_ref, ...), custom_call_target="tpu_custom_call" | custom-call | flops 793313280 | bytes 4958208 | tf_op jit(solution)/shard_map/pallas_call | solution.py:367
  80.4 0.0 copy-start.1
  80.4 0.0 copy-start.2
  80.4 2.6 %shard_map.143.own_ref = f32[80,1152]{1,0:T(8,128)S(1)} custom-call(s32[1]{0:T(128)} %bitcast.mp_ref, bf16[16,1076]{1,0:T(8,128)(2,1)S(1)} %get-tuple-element.31.d_act_ref, f32[320,8]{1,0:T(8,128)S(1)} %get-tuple-element.28.member_ref, f32[320,1076]{1,0:T(8,128)S(1)} %get-tuple-element.29.slope_ref, bf16[1076,1152]{1,0:T(8,128)(2,1)} %bitcast.19), custom_call_target="tpu_custom_call" | custom-call | flops 198328320 | bytes 2479104 | tf_op jit(solution)/shard_map/pallas_call | solution.py:367
  83.1 0.0 copy-done.1
  83.1 0.0 copy-start
  83.1 0.0 copy-done.2
  83.1 7.9 %all-to-all-start.2 = ((bf16[16,8,1280]{2,1,0:T(8,128)(2,1)}), bf16[16,8,1280]{2,1,0:T(8,128)(2,1)S(1)}, u32[]{:S(2)}, u32[]{:S(2)}) async-start(bf16[16,8,1280]{2,1,0:T(8,128)(2,1)} %bitcast.10), calls=%async_computation.2 | async-start | bytes 655360 | tf_op jit(solution)/shard_map/all_to_all | solution.py:383
  90.9 4.9 %collective-permute-start = (bf16[80,1152]{1,0:T(8,128)(2,1)}, bf16[80,1152]{1,0:T(8,128)(2,1)S(1)}, u32[]{:S(2)}, u32[]{:S(2)}) collective-permute-start(bf16[80,1152]{1,0:T(8,128)(2,1)} %copy-done.2), channel_id=1, source_target_pairs={{0,2},{1,3},{2,0},{3,1},{4,6},{5,7},{6,4},{7,5},{8,10},{9,11},{10,... | collective-permute-start | bytes 552968 | tf_op jit(solution)/shard_map/ppermute | solution.py:498
  95.9 5.8 %collective-permute-start.1 = (bf16[80,1152]{1,0:T(8,128)(2,1)}, bf16[80,1152]{1,0:T(8,128)(2,1)S(1)}, u32[]{:S(2)}, u32[]{:S(2)}) collective-permute-start(bf16[80,1152]{1,0:T(8,128)(2,1)} %copy-done.1), channel_id=1, source_target_pairs={{0,1},{1,2},{2,3},{3,0},{4,5},{5,6},{6,7},{7,4},{8,9},{9,10},{10,1... | collective-permute-start | bytes 552968 | tf_op jit(solution)/shard_map/ppermute | solution.py:498
  101.7 1.9 %collective-permute-start.2 = (bf16[80,1152]{1,0:T(8,128)(2,1)S(1)}, bf16[80,1152]{1,0:T(8,128)(2,1)S(1)}, u32[]{:S(2)}, u32[]{:S(2)}) collective-permute-start(bf16[80,1152]{1,0:T(8,128)(2,1)S(1)} %get-tuple-element.35), channel_id=1, source_target_pairs={{0,3},{1,0},{2,1},{3,2},{4,7},{5,4},{6,5},{7,6},{8,11},{9,8},{10,9... | collective-permute-start | bytes 552968 | tf_op jit(solution)/shard_map/ppermute | solution.py:498
  103.6 2.5 %collective-permute-done.first_ref = bf16[80,1152]{1,0:T(8,128)(2,1)S(1)} collective-permute-done((bf16[80,1152]{1,0:T(8,128)(2,1)}, bf16[80,1152]{1,0:T(8,128)(2,1)S(1)}, u32[]{:S(2)}, u32[]{:S(2)}) %collective-permute-start) | collective-permute-done | bytes 184352 | tf_op jit(solution)/shard_map/ppermute | solution.py:498
  106.1 10.8 %collective-permute-done.1.second_ref = bf16[80,1152]{1,0:T(8,128)(2,1)S(1)} collective-permute-done((bf16[80,1152]{1,0:T(8,128)(2,1)}, bf16[80,1152]{1,0:T(8,128)(2,1)S(1)}, u32[]{:S(2)}, u32[]{:S(2)}) %collective-permute-start.1) | collective-permute-done | bytes 184352 | tf_op jit(solution)/shard_map/ppermute | solution.py:498
  116.9 0.0 collective-permute-done.2.third_ref
  116.9 1.9 %shard_map.144 = f32[80,1152]{1,0:T(8,128)} custom-call(s32[1]{0:T(128)} %bitcast.mp_ref, f32[80,1152]{1,0:T(8,128)S(1)} %shard_map.143.own_ref, bf16[80,1152]{1,0:T(8,128)(2,1)S(1)} %collective-permute-done.first_ref, bf16[80,1152]{1,0:T(8,128)(2,1)S(1)} %collective-permute-done.1.second_ref, bf16[80,1152]{1,0:T(8,128)(2,1)S(1)} %collective-permute-done.2.third_ref, ...), custom_call_target="tpu_custom_call" | custom-call | tf_op jit(solution)/shard_map/pallas_call | solution.py:367
  118.8 0.0 all-to-all-done.2.parts_ref
  118.8 0.0 copy-done
  118.8 0.8 shard_map.145
  (1 shorter events, 0.0 us)
Async XLA Ops:
  3.3 42.3 %all-to-all-start = ((bf16[16,24,1152]{2,1,0:T(8,128)(2,1)}), bf16[16,24,1152]{2,1,0:T(8,128)(2,1)S(1)}, u32[]{:S(2)}, u32[]{:S(2)}) async-start(bf16[16,24,1152]{2,1,0:T(8,128)(2,1)} %bitcast.3), calls=%async_computation | async-start | bytes 1769472 | tf_op jit(solution)/shard_map/all_to_all | solution.py:383
  49.5 26.4 %all-to-all-start.1 = ((bf16[16,8,1152]{2,1,0:T(8,128)(2,1)}), bf16[16,8,1152]{2,1,0:T(8,128)(2,1)S(1)}, u32[]{:S(2)}, u32[]{:S(2)}) async-start(bf16[16,8,1152]{2,1,0:T(8,128)(2,1)} %bitcast.8), calls=%async_computation.1 | async-start | bytes 589824 | tf_op jit(solution)/shard_map/all_to_all | solution.py:383
  80.4 2.7 %copy-start.1 = (bf16[80,1152]{1,0:T(8,128)(2,1)}, bf16[80,1152]{1,0:T(8,128)(2,1)S(1)}, u32[]{:S(2)}) copy-start(bf16[80,1152]{1,0:T(8,128)(2,1)S(1)} %get-tuple-element.34) | copy-start | bytes 552964
  80.4 2.7 %copy-start.2 = (bf16[80,1152]{1,0:T(8,128)(2,1)}, bf16[80,1152]{1,0:T(8,128)(2,1)S(1)}, u32[]{:S(2)}) copy-start(bf16[80,1152]{1,0:T(8,128)(2,1)S(1)} %get-tuple-element.33) | copy-start | bytes 552964
  83.1 35.7 %copy-start = (bf16[8,1152]{1,0:T(8,128)(2,1)S(1)}, bf16[8,1152]{1,0:T(8,128)(2,1)}, u32[]{:S(2)}) copy-start(bf16[8,1152]{1,0:T(8,128)(2,1)} %text_ref.1) | copy-start | bytes 55300
  83.1 35.7 %all-to-all-start.2 = ((bf16[16,8,1280]{2,1,0:T(8,128)(2,1)}), bf16[16,8,1280]{2,1,0:T(8,128)(2,1)S(1)}, u32[]{:S(2)}, u32[]{:S(2)}) async-start(bf16[16,8,1280]{2,1,0:T(8,128)(2,1)} %bitcast.10), calls=%async_computation.2 | async-start | bytes 655360 | tf_op jit(solution)/shard_map/all_to_all | solution.py:383
  90.9 15.2 %collective-permute-start = (bf16[80,1152]{1,0:T(8,128)(2,1)}, bf16[80,1152]{1,0:T(8,128)(2,1)S(1)}, u32[]{:S(2)}, u32[]{:S(2)}) collective-permute-start(bf16[80,1152]{1,0:T(8,128)(2,1)} %copy-done.2), channel_id=1, source_target_pairs={{0,2},{1,3},{2,0},{3,1},{4,6},{5,7},{6,4},{7,5},{8,10},{9,11},{10,... | collective-permute-start | bytes 552968 | tf_op jit(solution)/shard_map/ppermute | solution.py:498
  95.9 21.0 %collective-permute-start.1 = (bf16[80,1152]{1,0:T(8,128)(2,1)}, bf16[80,1152]{1,0:T(8,128)(2,1)S(1)}, u32[]{:S(2)}, u32[]{:S(2)}) collective-permute-start(bf16[80,1152]{1,0:T(8,128)(2,1)} %copy-done.1), channel_id=1, source_target_pairs={{0,1},{1,2},{2,3},{3,0},{4,5},{5,6},{6,7},{7,4},{8,9},{9,10},{10,1... | collective-permute-start | bytes 552968 | tf_op jit(solution)/shard_map/ppermute | solution.py:498
  101.7 15.2 %collective-permute-start.2 = (bf16[80,1152]{1,0:T(8,128)(2,1)S(1)}, bf16[80,1152]{1,0:T(8,128)(2,1)S(1)}, u32[]{:S(2)}, u32[]{:S(2)}) collective-permute-start(bf16[80,1152]{1,0:T(8,128)(2,1)S(1)} %get-tuple-element.35), channel_id=1, source_target_pairs={{0,3},{1,0},{2,1},{3,2},{4,7},{5,4},{6,5},{7,6},{8,11},{9,8},{10,9... | collective-permute-start | bytes 552968 | tf_op jit(solution)/shard_map/ppermute | solution.py:498

commit v4 on v3

--- a/solution.py
+++ b/solution.py
@@ -19,6 +19,9 @@
 NT = (((1,), (1,)), ((), ()))
 TN = (((0,), (0,)), ((), ()))
 LANES = 128
+HIDDEN_STEP = 256
+COPY_STEP = 384
+MOST_COPIES = 24
 HIGHEST = lax.Precision.HIGHEST
 
 
@@ -33,14 +36,18 @@
     return center * inverse_deviation, inverse_deviation
 
 
-def split_bf16(values):
-    high = values.astype(bf16)
-    return high, (values - high.astype(f32)).astype(bf16)
-
-
-def fetch(sources, targets, semaphores):
+def stacked_parts(values, many):
+    parts = []
+    for _ in range(many):
+        part = values.astype(bf16).astype(f32)
+        parts.append(part)
+        values = values - part
+    return jnp.concatenate(parts, axis=0).astype(bf16)
+
+
+def fetch(sources, targets, semaphores, first=0):
     copies = [
-        pltpu.make_async_copy(source, target, semaphores.at[k])
+        pltpu.make_async_copy(source, target, semaphores.at[first + k])
         for k, (source, target) in enumerate(zip(sources, targets))
     ]
     for copy in copies:
@@ -48,9 +55,17 @@
     return copies
 
 
-def split_three(values):
-    high, rest = split_bf16(values)
-    return high, rest, (values - high.astype(f32) - rest.astype(f32)).astype(bf16)
+def row_pieces(array, step):
+    return [array.at[pl.ds(first, many), :] for first, many in column_chunks(array.shape[0], step)]
+
+
+def column_pieces(array, step):
+    return [array.at[:, pl.ds(first, many)] for first, many in column_chunks(array.shape[1], step)]
+
+
+def wait_all(copies):
+    for copy in copies:
+        copy.wait()
 
 
 def quotient(values, by):
@@ -66,7 +81,8 @@
 
 
 def pack_kernel(dp_ref, owners_hbm, x_hbm, out_ref, owners_ref, x_ref, semaphores, *, padded):
-    copies = fetch((owners_hbm.at[0], x_hbm), (owners_ref, x_ref), semaphores)
+    copies = fetch((owners_hbm.at[0],), (owners_ref,), semaphores)
+    copies += fetch(row_pieces(x_hbm, 80), row_pieces(x_ref, 80), semaphores, 1)
     rows = x_ref.shape[0]
     slots = owners_ref.shape[0]
     block_rows = rows // slots
@@ -78,7 +94,7 @@
         owner = jnp.where(block == b, owners_ref[dp_ref[0], b], owner)
     target = owner * padded + within
     pick = one_hot(iota((slots * padded, rows), 0) == target)
-    copies[1].wait()
+    wait_all(copies[1:])
     out_ref[...] = jnp.dot(pick, x_ref[...], preferred_element_type=f32).astype(bf16)
 
 
@@ -117,12 +133,15 @@
     share,
 ):
     copies = fetch(
-        (counts_hbm, x_hbm, gain_hbm, bias_hbm, b1_hbm, w1t_hbm, w2_hbm),
-        (counts_ref, x_ref, gain_ref, bias_ref, b1_ref, w1t_ref, w2_ref),
+        (counts_hbm, gain_hbm, bias_hbm, b1_hbm, *row_pieces(x_hbm, 80)),
+        (counts_ref, gain_ref, bias_ref, b1_ref, *row_pieces(x_ref, 80)),
         semaphores,
     )
-    for copy in copies[:5]:
-        copy.wait()
+    begin = len(copies)
+    firsts = fetch(column_pieces(w1t_hbm, COPY_STEP), column_pieces(w1t_ref, COPY_STEP), semaphores, begin)
+    begin += len(firsts)
+    seconds = fetch(column_pieces(w2_hbm, COPY_STEP), column_pieces(w2_ref, COPY_STEP), semaphores, begin)
+    wait_all(copies)
     rows = x_ref.shape[0]
     images = counts_ref.shape[1]
     position = dp_ref[0] * rows + iota((images, rows), 1)
@@ -133,15 +152,16 @@
     normed = (xhat * gain_ref[...][None, :] + bias_ref[...][None, :]).astype(bf16)
     offset = b1_ref[...][None, :]
     total = share * jnp.dot(member, x, preferred_element_type=f32)
-    for copy in copies[5:]:
-        copy.wait()
-    for first, many in column_chunks(w1t_ref.shape[0], 256):
+    wait_all(firsts)
+    for first, many in column_chunks(w1t_ref.shape[0], HIDDEN_STEP):
         cols = slice(first, first + many)
         pre = lax.dot_general(normed, w1t_ref[cols, :], NT, preferred_element_type=f32) + offset[:, cols]
         inner = gelu_coef * (pre + 0.044715 * pre * pre * pre)
         act = (0.5 * pre * (1.0 + jnp.tanh(inner))).astype(bf16)
         pooled = jnp.dot(member, act, preferred_element_type=f32)
-        both = jnp.concatenate(split_bf16(pooled), axis=0)
+        if first == 0:
+            wait_all(seconds)
+        both = stacked_parts(pooled, 2)
         product = jnp.dot(both, w2_ref[cols, :], preferred_element_type=f32)
         total = total + product[:images] + product[images:]
     out_ref[...] = total
@@ -171,10 +191,11 @@
     semaphores,
 ):
     copies = fetch(
-        (counts_hbm, owners_hbm.at[0], gain_hbm, bias_hbm, b1_hbm, text_hbm, w1t_hbm),
-        (counts_ref, owners_ref, gain_ref, bias_ref, b1_ref, text_ref, w1t_ref),
+        (counts_hbm, owners_hbm.at[0], gain_hbm, bias_hbm, b1_hbm, text_hbm),
+        (counts_ref, owners_ref, gain_ref, bias_ref, b1_ref, text_ref),
         semaphores,
     )
+    firsts = fetch(column_pieces(w1t_hbm, COPY_STEP), column_pieces(w1t_ref, COPY_STEP), semaphores, len(copies))
     rows = rows_ref.shape[0]
     slots = owners_ref.shape[0]
     block_rows = rows // slots
@@ -184,8 +205,7 @@
     pick = one_hot(iota((rows, in_ref.shape[0]), 1) == source * padded + within)
     x = jnp.dot(pick, in_ref[...], preferred_element_type=f32)
     rows_ref[...] = x.astype(bf16)
-    for copy in copies[:6]:
-        copy.wait()
+    wait_all(copies)
     text = text_ref[...].astype(f32)
     texts_ref[...] = jnp.concatenate([text] * (texts_ref.shape[0] // text.shape[0]), axis=0).astype(bf16)
     block = jnp.where(owners_ref[...] == dp_ref[0], iota((slots, slots), 1), 0)
@@ -198,8 +218,8 @@
     xhat, _ = layer_statistics(x)
     normed = (xhat * gain_ref[...][None, :] + bias_ref[...][None, :]).astype(bf16)
     offset = b1_ref[...][None, :]
-    copies[6].wait()
-    for first, many in column_chunks(w1t_ref.shape[0], 256):
+    wait_all(firsts)
+    for first, many in column_chunks(w1t_ref.shape[0], HIDDEN_STEP):
         cols = slice(first, first + many)
         pre = lax.dot_general(normed, w1t_ref[cols, :], NT, preferred_element_type=f32) + offset[:, cols]
         square = pre * pre
@@ -229,20 +249,25 @@
     upstream_ref,
     parts_ref,
     d_act_ref,
-    *refs,
-    steps,
+    out_ref,
+    counts_ref,
+    labels_ref,
+    w2_ref,
+    w1t_ref,
+    semaphores,
+    *,
     ring,
 ):
-    outs, (counts_ref, labels_ref, w2_ref, w1t_ref, semaphores) = refs[: len(steps)], refs[len(steps) :]
-    copies = fetch(
-        (counts_hbm, labels_hbm, w2_hbm, w1t_hbm), (counts_ref, labels_ref, w2_ref, w1t_ref), semaphores
-    )
+    copies = fetch((counts_hbm, labels_hbm), (counts_ref, labels_ref), semaphores)
+    begin = len(copies)
+    seconds = fetch(column_pieces(w2_hbm, COPY_STEP), column_pieces(w2_ref, COPY_STEP), semaphores, begin)
+    begin += len(seconds)
+    firsts = fetch(column_pieces(w1t_hbm, COPY_STEP), column_pieces(w1t_ref, COPY_STEP), semaphores, begin)
     total = pieces_ref[0]
     for k in range(1, pieces_ref.shape[0]):
         total = total + pieces_ref[k]
     images, width = total.shape
-    copies[0].wait()
-    copies[1].wait()
+    wait_all(copies)
     texts = texts_ref[...]
     all_images = texts.shape[0]
     image = iota((images, 1), 0)
@@ -259,61 +284,66 @@
     norm_t = jnp.sqrt(jnp.sum(wide * wide, axis=-1, keepdims=True) + eps)
     inverse_t = (1.0 / norm_t).T
     scale = scale_ref[0]
-    unit_parts = split_three(unit_e)
-    raw = lax.dot_general(jnp.concatenate(unit_parts, axis=0), texts, NT, preferred_element_type=f32)
+    raw = lax.dot_general(stacked_parts(unit_e, 3), texts, NT, preferred_element_type=f32)
     raw = raw[:images] + raw[images : 2 * images] + raw[2 * images :]
     score = scale * (raw * inverse_t) + shift_ref[0]
     sign = jnp.where(iota((images, all_images), 1) == label, 1.0, -1.0)
     margin = sign * score
     dscore = -sign * jax.nn.sigmoid(-margin) / all_images
-    du = jnp.dot(
-        jnp.concatenate(split_three(dscore * inverse_t), axis=0), texts, preferred_element_type=f32
-    )
+    du = jnp.dot(stacked_parts(dscore * inverse_t, 3), texts, preferred_element_type=f32)
     du = scale * (du[:images] + du[images : 2 * images] + du[2 * images :])
     dembed = (du - unit_e * jnp.sum(unit_e * du, axis=-1, keepdims=True)) / norm_e
     upstream_ref[...] = grad_scale * (dembed / count)
-    high, low = split_bf16(scale * dscore)
-    unit_high, unit_low = unit_parts[:2]
+    scaled = stacked_parts(scale * dscore, 2).astype(f32)
+    unit = stacked_parts(unit_e, 2).astype(f32)
     parts = lax.dot_general(
-        jnp.concatenate([high, high, low], axis=0),
-        jnp.concatenate([unit_high, unit_low, unit_high], axis=0),
+        jnp.concatenate([scaled[:images], scaled], axis=0).astype(bf16),
+        jnp.concatenate([unit, unit[:images]], axis=0).astype(bf16),
         TN,
         preferred_element_type=f32,
     )
     parts_ref[:, :width] = parts.astype(bf16)
     loss = jnp.sum(jnp.sum(log_sigmoid(margin), axis=1, keepdims=True), axis=0, keepdims=True) / -all_images
-    loss_high, loss_low = split_bf16(loss)
+    loss_high = loss.astype(bf16).astype(f32)
     lane = iota((all_images, LANES), 1)
-    loss_lanes = jnp.where(lane == 0, loss_high.astype(f32), jnp.where(lane == 1, loss_low.astype(f32), 0.0))
+    loss_lanes = jnp.where(lane == 0, loss_high, jnp.where(lane == 1, loss - loss_high, 0.0))
     parts_ref[:, width:] = loss_lanes.astype(bf16)
-    copies[2].wait()
+    wait_all(seconds)
     d_image = upstream_ref[...].astype(bf16)
     d_act = lax.dot_general(d_image, w2_ref[...], NT, preferred_element_type=f32)
-    both = jnp.concatenate(split_bf16(d_act), axis=0)
+    both = stacked_parts(d_act, 2)
     d_act_ref[...] = both
-    copies[3].wait()
-    share = outs[0].shape[0]
-    for out_ref, step in zip(outs, steps):
-        rows = own_range(mp_ref, step, ring, share)
-        out_ref[...] = back_rows(member_ref[rows, :], both, slope_ref[rows, :], w1t_ref[...]).astype(bf16)
-
-
-def own_range(mp_ref, step, ring, share):
+    wait_all(firsts)
+    share = out_ref.shape[0] // 2
+    back = back_of_shares(mp_ref, (mp_ref[1], 2), ring, share, member_ref, both, slope_ref, w1t_ref)
+    out_ref[...] = back.astype(bf16)
+
+
+def share_range(mp_ref, step, ring, share):
     return pl.ds(pl.multiple_of(lax.rem(mp_ref[0] + step, ring) * share, share), share)
 
 
+def back_of_shares(mp_ref, steps, ring, share, member_ref, d_act, slope_ref, w1t_ref):
+    ranges = [share_range(mp_ref, step, ring, share) for step in steps]
+    member = jnp.concatenate([member_ref[rows, :] for rows in ranges], axis=0)
+    slope = jnp.concatenate([slope_ref[rows, :] for rows in ranges], axis=0)
+    return back_rows(member, d_act, slope, w1t_ref[...])
+
+
 def back_rows(member, both, slope, w1t):
-    member = member.astype(bf16)
-    d_rows = jnp.dot(jnp.concatenate([member, member], axis=1), both, preferred_element_type=f32)
+    d_rows = jnp.dot(jnp.concatenate([member, member], axis=1).astype(bf16), both, preferred_element_type=f32)
     d_pre = (d_rows * slope).astype(bf16)
     return jnp.dot(d_pre, w1t, preferred_element_type=f32)
 
 
-def own_kernel(mp_ref, d_act_ref, member_ref, slope_ref, w1t_hbm, out_ref, w1t_ref, semaphores, *, ring):
-    copies = fetch((w1t_hbm,), (w1t_ref,), semaphores)
-    rows = own_range(mp_ref, 0, ring, out_ref.shape[0])
-    copies[0].wait()
-    out_ref[...] = back_rows(member_ref[rows, :], d_act_ref[...], slope_ref[rows, :], w1t_ref[...])
+def rest_kernel(mp_ref, d_act_ref, member_ref, slope_ref, w1t_hbm, second_ref, own_ref, w1t_ref, semaphores, *, ring):
+    firsts = fetch(column_pieces(w1t_hbm, COPY_STEP), column_pieces(w1t_ref, COPY_STEP), semaphores)
+    wait_all(firsts)
+    share = own_ref.shape[0]
+    steps = (ring - mp_ref[1], 0)
+    back = back_of_shares(mp_ref, steps, ring, share, member_ref, d_act_ref[...], slope_ref, w1t_ref)
+    second_ref[...] = back[:share]
+    own_ref[...] = back[share:]
 
 
 def row_kernel(
@@ -321,7 +351,6 @@
     own_ref,
     first_ref,
     second_ref,
-    third_ref,
     x_ref,
     member_ref,
     upstream_ref,
@@ -333,9 +362,8 @@
     ring,
 ):
     copies = fetch((gain_hbm,), (gain_ref,), semaphores)
-    rows = own_range(mp_ref, 0, ring, out_ref.shape[0])
-    back = own_ref[...] + first_ref[...].astype(f32)
-    back = back + second_ref[...].astype(f32) + third_ref[...].astype(f32)
+    rows = share_range(mp_ref, 0, ring, out_ref.shape[0])
+    back = own_ref[...] + first_ref[: out_ref.shape[0], :].astype(f32) + second_ref[...].astype(f32)
     xhat, inverse_deviation = layer_statistics(x_ref[rows, :].astype(f32))
     copies[0].wait()
     dxhat = back * gain_ref[...][None, :]
@@ -350,10 +378,11 @@
 
 def text_kernel(parts_ref, text_ref, grad_ref, loss_ref):
     text = text_ref[...].astype(f32)
-    width = text.shape[1]
-    total = parts_ref[0].astype(f32)
-    for k in range(1, parts_ref.shape[0]):
-        total = total + parts_ref[k].astype(f32)
+    texts, width = text.shape
+    parts = parts_ref[...].astype(f32)
+    total = parts[:texts]
+    for first in range(texts, parts.shape[0], texts):
+        total = total + parts[first : first + texts]
     norm = jnp.sqrt(jnp.sum(text * text, axis=-1, keepdims=True) + eps)
     unit = text / norm
     dv = total[:, :width]
@@ -362,8 +391,8 @@
 
 
 def call(kernel, outs, operands, scratch=(), flops=0, read=0):
-    fetched = sum(space is stored for space, _ in operands)
-    extra = [pltpu.SemaphoreType.DMA((fetched,))] if fetched else []
+    fetched = any(space is stored for space, _ in operands)
+    extra = [pltpu.SemaphoreType.DMA((MOST_COPIES,))] if fetched else []
     return pl.pallas_call(
         kernel,
         out_shape=outs,
@@ -399,10 +428,17 @@
 ):
     dp_size = lax.axis_size("dp")
     mp_size = lax.axis_size("mp")
-    loss_size = lax.axis_size("loss")
     dp_index = lax.axis_index("dp").astype(jnp.int32)[None]
     mp_index = lax.axis_index("mp").astype(jnp.int32)[None]
     loss_index = lax.axis_index("loss").astype(jnp.int32)[None]
+    turn = jnp.where((mp_index + dp_index) % 2 == 0, 1, mp_size - 1)
+    ring_place = jnp.concatenate([mp_index, turn])
+    first_pairs, second_pairs = [], []
+    for d in range(dp_size):
+        for m in range(mp_size):
+            step = 1 if (d + m) % 2 == 0 else mp_size - 1
+            first_pairs.append((d * mp_size + m, d * mp_size + (m + step) % mp_size))
+            second_pairs.append((d * mp_size + m, d * mp_size + (m - step) % mp_size))
     row_count, width = patches.shape
     hidden = fc1_weight.shape[1]
     share_rows = row_count // mp_size
@@ -471,16 +507,15 @@
     texts = exchange(text_copies, "loss")
     slab_sums, slope = lax.optimization_barrier((slab_sums, slope))
     pieces = lax.all_gather(slab_sums, "dp", axis=0)
-    steps = (2, 1, 3)
-    upstream, parts, d_act, *chunks = call(
-        functools.partial(gradient_kernel, steps=steps, ring=mp_size),
+    upstream, parts, d_act, first_chunks = call(
+        functools.partial(gradient_kernel, ring=mp_size),
         [
             shape((images, width), f32),
             shape((all_images, width + LANES), bf16),
             shape((2 * images, hidden), bf16),
-        ]
-        + [shape((share_rows, width), bf16)] * len(steps),
-        [(scalars, array) for array in (loss_index, mp_index, logit_scale, logit_bias)]
+            shape((2 * share_rows, width), bf16),
+        ],
+        [(scalars, array) for array in (loss_index, ring_place, logit_scale, logit_bias)]
         + [(whole, array) for array in (pieces, texts, member, slope)]
         + [(stored, array) for array in (counts, labels, fc2_weight, fc1_t)],
         [
@@ -492,20 +527,18 @@
         flops=matmul,
         read=2 * weight_bytes,
     )
-    received = []
-    for chunk, step in zip(chunks, steps):
-        pairs = [(i, (i + step) % mp_size) for i in range(mp_size)]
-        received.append(lax.ppermute(chunk, "mp", pairs))
-    own_back = call(
-        functools.partial(own_kernel, ring=mp_size),
-        shape((share_rows, width), f32),
-        [(scalars, mp_index), (whole, d_act), (whole, member), (whole, slope), (stored, fc1_t)],
+    first_received = lax.ppermute(first_chunks, ("dp", "mp"), first_pairs)
+    second_chunk, own_back = call(
+        functools.partial(rest_kernel, ring=mp_size),
+        [shape((share_rows, width), f32)] * 2,
+        [(scalars, ring_place), (whole, d_act), (whole, member), (whole, slope), (stored, fc1_t)],
         [first_room],
-        flops=matmul // mp_size,
+        flops=matmul // 2,
         read=weight_bytes,
     )
-    parts, own_back = lax.optimization_barrier((parts, own_back))
-    all_parts = exchange(parts, "loss").reshape(loss_size, images, width + LANES)
+    second_sum = (second_chunk + first_received[share_rows:].astype(f32)).astype(bf16)
+    second_received = lax.ppermute(second_sum, ("dp", "mp"), second_pairs)
+    all_parts = exchange(parts, "loss")
     grad_text, loss = call(
         text_kernel,
         (shape((images, width), f32), shape((1, 1), f32)),
@@ -514,9 +547,9 @@
     grad_rows = call(
         functools.partial(row_kernel, ring=mp_size),
         shape((share_rows, width), f32),
-        [(scalars, mp_index), (whole, own_back)]
-        + [(whole, array) for array in received]
-        + [(whole, rows), (whole, member), (whole, upstream), (stored, gain)],
+        [(scalars, ring_place)]
+        + [(whole, array) for array in (own_back, first_received, second_received, rows, member, upstream)]
+        + [(stored, gain)],
         [gain_room],
     )
     return (grad_rows, grad_text, loss[0, 0])

time: 121 us -> 113 us (0.934)
  waiting for transfers between devices: 18.3 us -> 11.4 us
  starting transfers between devices: 42.3 us -> 38.2 us
  Pallas kernels: 22.9 us -> 24.6 us
    ppermute x3 -> x2, waiting for transfers between devices: 13.3 us -> 5.79 us  [the longest x1 5.79 us: shards(): second_received = lax.ppermute(second_sum, ('dp', 'mp'), second_pairs)]
    ppermute x3 -> x2, starting transfers between devices: 12.6 us -> 9.37 us  [the longest x1 7.45 us: shards(): first_received = lax.ppermute(first_chunks, ('dp', 'mp'), first_pairs)]
    pallas_call x7, Pallas kernels: 22.9 us -> 24.6 us  [call(): pl.pallas_call(kernel, out_shape=outs, in_specs=[space for space, _ in op...]
  transfers between devices with their start and end apart: 6 -> 5, of which waited for: 3 -> 2; matrix products, arithmetic and copies ran while one was open for 0% -> 0% of each run, Pallas kernels for 7% -> 11%
where the time goes in v4:
time: 113 us; the launch traced here: 111 us
  starting transfers between devices  38.2 us (34%)
  blocking collectives  34 us (30%)
  Pallas kernels  24.6 us (22%)
  waiting for transfers between devices  11.4 us (10%)
  between operations  2.08 us (2%)
    all_to_all x3, starting transfers between devices, exchange(): return lax.all_to_all(block, axis, split_axis=0, concat_axis=0, tiled=True)  28.9 us
    pallas_call x7, Pallas kernels, call(): pl.pallas_call(kernel, out_shape=outs, in_specs=[space for space, _ in op...  24.6 us
    all_gather x1, blocking collectives, shards(): pieces = lax.all_gather(slab_sums, 'dp', axis=0)  20.9 us
    all_gather x1, blocking collectives, shards(): slab_sums = jnp.sum(lax.all_gather(partial_sums, 'mp', axis=0), axis=0)  13 us
    ppermute x1, starting transfers between devices, shards(): first_received = lax.ppermute(first_chunks, ('dp', 'mp'), first_pairs)  7.45 us
    ppermute x1, waiting for transfers between devices, shards(): second_received = lax.ppermute(second_sum, ('dp', 'mp'), second_pairs)  5.79 us
    all_to_all x3, waiting for transfers between devices, exchange(): return lax.all_to_all(block, axis, split_axis=0, concat_axis=0, tiled=True)  5.57 us
  transfers between devices with their start and end apart: 5, of which 2 were waited for; matrix products, arithmetic and copies ran while one was open for 0% of the time, Pallas kernels for 11%

profile of v4, /device:TPU:1, one launch (start us, length us, event | category | flops | bytes accessed | tf_op | source)
XLA Modules:
  0.0 111.1 jit_solution(11544484395389999339)
XLA Ops:
  0.6 3.0 %shard_map.139 = bf16[384,1152]{1,0:T(8,128)(2,1)} custom-call(s32[1]{0:T(128)} %bitcast.1.dp_ref, s32[1,16,16]{2,1,0:T(8,128)} %owners_hbm.3, bf16[320,1152]{1,0:T(8,128)(2,1)} %x_hbm.2), custom_call_target="tpu_custom_call" | custom-call | tf_op jit(solution)/shard_map/pallas_call | solution.py:396
  3.6 17.6 %all-to-all-start = ((bf16[16,24,1152]{2,1,0:T(8,128)(2,1)}), bf16[16,24,1152]{2,1,0:T(8,128)(2,1)S(1)}, u32[]{:S(2)}, u32[]{:S(2)}) async-start(bf16[16,24,1152]{2,1,0:T(8,128)(2,1)} %bitcast.3), calls=%async_computation | async-start | bytes 1769472 | tf_op jit(solution)/shard_map/all_to_all | solution.py:412
  21.2 6.0 %shard_map.140 = f32[8,1152]{1,0:T(8,128)S(1)} custom-call(s32[1]{0:T(128)} %bitcast.1.dp_ref, s32[1,8]{1,0:T(1,128)} %counts_hbm.5, bf16[320,1152]{1,0:T(8,128)(2,1)} %x_hbm.2, f32[1152]{0:T(1024)} %gain_hbm.5, f32[1152]{0:T(1024)} %bias_hbm.3, f32[1076]{0:T(1024)} %b1_hbm.3, bf16[1076,1152]{1,0:T(8,128)(2,1)} %bitcast.19, bf16[1076,1152]{1,0:T(8,128)(2,1)} %w2_hbm.3), custom_call_target="tpu_custom_call" | custom-call | flops 793313280 | bytes 4958208 | tf_op jit(solution)/shard_map/pallas_call | solution.py:396
  27.2 13.0 %all-gather = f32[32,1152]{1,0:T(8,128)S(1)} all-gather(f32[8,1152]{1,0:T(8,128)S(1)} %shard_map.140), channel_id=2, replica_groups=mesh['dp'=16,'loss'=16,'mp'=4] {'mp'}, dimensions={0}, use_global_device_ids=true | all-gather | bytes 184320 | tf_op jit(solution)/shard_map/all_gather | solution.py:483
  40.3 5.6 %all-to-all-done = bf16[16,24,1152]{2,1,0:T(8,128)(2,1)S(1)} async-done(((bf16[16,24,1152]{2,1,0:T(8,128)(2,1)}), bf16[16,24,1152]{2,1,0:T(8,128)(2,1)S(1)}, u32[]{:S(2)}, u32[]{:S(2)}) %all-to-all-start) | async-done | bytes 884768 | tf_op jit(solution)/shard_map/all_to_all | solution.py:412
  45.9 4.0 %shard_map.141 = (f32[320,1076]{1,0:T(8,128)S(1)}, bf16[320,1152]{1,0:T(8,128)(2,1)S(1)}, f32[320,8]{1,0:T(8,128)S(1)}, bf16[128,1152]{1,0:T(8,128)(2,1)}) custom-call(s32[1]{0:T(128)} %bitcast.1.dp_ref, bf16[384,1152]{1,0:T(8,128)(2,1)S(1)} %bitcast.14, s32[1,8]{1,0:T(1,128)} %counts_hbm.5, s32[1,16,16]{2,1,0:T(8,128)} %owners_hbm.3, f32[1152]{0:T(1024)} %gain_hbm.5, ...), custom_call_target="tpu_custom_call" | custom-call | flops 793313280 | bytes 4958208 | tf_op jit(solution)/shard_map/pallas_call | solution.py:396
  49.9 3.7 %all-to-all-start.1 = ((bf16[16,8,1152]{2,1,0:T(8,128)(2,1)}), bf16[16,8,1152]{2,1,0:T(8,128)(2,1)S(1)}, u32[]{:S(2)}, u32[]{:S(2)}) async-start(bf16[16,8,1152]{2,1,0:T(8,128)(2,1)} %bitcast.8), calls=%async_computation.1 | async-start | bytes 589824 | tf_op jit(solution)/shard_map/all_to_all | solution.py:412
  54.9 0.1 pad_add_fusion.mp_ref
  54.9 20.9 %all-gather.1 = f32[128,1152]{1,0:T(8,128)S(1)} all-gather(f32[8,1152]{1,0:T(8,128)S(1)} %bitcast_reduce_fusion), channel_id=3, replica_groups=mesh['dp'=16,'loss'=16,'mp'=4] {'dp'}, dimensions={0}, use_global_device_ids=true | all-gather | bytes 626688 | tf_op jit(solution)/shard_map/all_gather | solution.py:509
  75.9 0.0 all-to-all-done.1
  75.9 4.8 %shard_map.142 = (f32[8,1152]{1,0:T(8,128)S(1)}, bf16[128,1280]{1,0:T(8,128)(2,1)S(1)}, bf16[16,1076]{1,0:T(8,128)(2,1)S(1)}, bf16[160,1152]{1,0:T(8,128)(2,1)}) custom-call(s32[1]{0:T(128)} %bitcast.2.loss_ref, s32[2]{0:T(128)S(1)} %pad_add_fusion.mp_ref, f32[1]{0:T(128)S(6)} %copy.15.scale_ref, f32[1]{0:T(128)S(6)} %copy.16.shift_ref, ...), custom_call_target="tpu_custom_call" | custom-call | flops 793313280 | bytes 4958208 | tf_op jit(solution)/shard_map/pallas_call | solution.py:396
  80.7 0.0 copy-start
  80.7 0.7 copy-done
  81.4 7.5 %collective-permute-start = (bf16[160,1152]{1,0:T(8,128)(2,1)}, bf16[160,1152]{1,0:T(8,128)(2,1)S(1)}, u32[]{:S(2)}, u32[]{:S(2)}) collective-permute-start(bf16[160,1152]{1,0:T(8,128)(2,1)} %get-tuple-element.30), channel_id=1, source_target_pairs={{0,1},{1,0},{2,3},{3,2},{64,67},{65,66},{66,65},{67,64},{128,129},... | collective-permute-start | bytes 1105928 | tf_op jit(solution)/shard_map/ppermute | solution.py:530
  88.9 7.6 %all-to-all-start.2 = ((bf16[16,8,1280]{2,1,0:T(8,128)(2,1)}), bf16[16,8,1280]{2,1,0:T(8,128)(2,1)S(1)}, u32[]{:S(2)}, u32[]{:S(2)}) async-start(bf16[16,8,1280]{2,1,0:T(8,128)(2,1)} %bitcast.18), calls=%async_computation.2 | async-start | bytes 655360 | tf_op jit(solution)/shard_map/all_to_all | solution.py:412
  96.5 3.3 %shard_map.143 = (f32[80,1152]{1,0:T(8,128)S(1)}, f32[80,1152]{1,0:T(8,128)S(1)}) custom-call(s32[2]{0:T(128)S(1)} %pad_add_fusion.mp_ref, bf16[16,1076]{1,0:T(8,128)(2,1)S(1)} %get-tuple-element.28.d_act_ref, f32[320,8]{1,0:T(8,128)S(1)} %get-tuple-element.26.member_ref, f32[320,1076]{1,0:T(8,128)S(1)} %get-tuple-element.27.slope_ref, ...), custom_call_target="tpu_custom_call" | custom-call | flops 396656640 | bytes 2479104 | tf_op jit(solution)/shard_map/pallas_call | solution.py:396
  99.8 0.0 copy-start.1
  99.9 0.0 collective-permute-done.first_ref
  99.9 1.9 %collective-permute-start.1 = (bf16[80,1152]{1,0:T(8,128)(2,1)S(1)}, bf16[80,1152]{1,0:T(8,128)(2,1)S(1)}, u32[]{:S(2)}, u32[]{:S(2)}) collective-permute-start(bf16[80,1152]{1,0:T(8,128)(2,1)S(1)} %add_convert_fusion), channel_id=1, source_target_pairs={{0,3},{1,2},{2,1},{3,0},{64,65},{65,64},{66,67},{67,66},{128,131},... | collective-permute-start | bytes 552968 | tf_op jit(solution)/shard_map/ppermute | solution.py:540
  101.8 5.8 %collective-permute-done.1.second_ref = bf16[80,1152]{1,0:T(8,128)(2,1)S(1)} collective-permute-done((bf16[80,1152]{1,0:T(8,128)(2,1)S(1)}, bf16[80,1152]{1,0:T(8,128)(2,1)S(1)}, u32[]{:S(2)}, u32[]{:S(2)}) %collective-permute-start.1) | collective-permute-done | bytes 184352 | tf_op jit(solution)/shard_map/ppermute | solution.py:540
  107.6 2.6 %shard_map.144 = f32[80,1152]{1,0:T(8,128)} custom-call(s32[2]{0:T(128)S(1)} %pad_add_fusion.mp_ref, f32[80,1152]{1,0:T(8,128)S(1)} %get-tuple-element.29.own_ref, bf16[160,1152]{1,0:T(8,128)(2,1)S(1)} %collective-permute-done.first_ref, bf16[80,1152]{1,0:T(8,128)(2,1)S(1)} %collective-permute-done.1.second_ref, ...), custom_call_target="tpu_custom_call" | custom-call | tf_op jit(solution)/shard_map/pallas_call | solution.py:396
  110.3 0.0 all-to-all-done.2
  110.3 0.0 copy-done.1
  110.3 0.8 shard_map.145
  (2 shorter events, 0.1 us)
Async XLA Ops:
  3.6 42.3 %all-to-all-start = ((bf16[16,24,1152]{2,1,0:T(8,128)(2,1)}), bf16[16,24,1152]{2,1,0:T(8,128)(2,1)S(1)}, u32[]{:S(2)}, u32[]{:S(2)}) async-start(bf16[16,24,1152]{2,1,0:T(8,128)(2,1)} %bitcast.3), calls=%async_computation | async-start | bytes 1769472 | tf_op jit(solution)/shard_map/all_to_all | solution.py:412
  49.9 26.0 %all-to-all-start.1 = ((bf16[16,8,1152]{2,1,0:T(8,128)(2,1)}), bf16[16,8,1152]{2,1,0:T(8,128)(2,1)S(1)}, u32[]{:S(2)}, u32[]{:S(2)}) async-start(bf16[16,8,1152]{2,1,0:T(8,128)(2,1)} %bitcast.8), calls=%async_computation.1 | async-start | bytes 589824 | tf_op jit(solution)/shard_map/all_to_all | solution.py:412
  80.7 0.7 copy-start
  81.4 18.4 %collective-permute-start = (bf16[160,1152]{1,0:T(8,128)(2,1)}, bf16[160,1152]{1,0:T(8,128)(2,1)S(1)}, u32[]{:S(2)}, u32[]{:S(2)}) collective-permute-start(bf16[160,1152]{1,0:T(8,128)(2,1)} %get-tuple-element.30), channel_id=1, source_target_pairs={{0,1},{1,0},{2,3},{3,2},{64,67},{65,66},{66,65},{67,64},{128,129},... | collective-permute-start | bytes 1105928 | tf_op jit(solution)/shard_map/ppermute | solution.py:530
  88.9 21.4 %all-to-all-start.2 = ((bf16[16,8,1280]{2,1,0:T(8,128)(2,1)}), bf16[16,8,1280]{2,1,0:T(8,128)(2,1)S(1)}, u32[]{:S(2)}, u32[]{:S(2)}) async-start(bf16[16,8,1280]{2,1,0:T(8,128)(2,1)} %bitcast.18), calls=%async_computation.2 | async-start | bytes 655360 | tf_op jit(solution)/shard_map/all_to_all | solution.py:412
  99.8 10.4 %copy-start.1 = (bf16[8,1152]{1,0:T(8,128)(2,1)S(1)}, bf16[8,1152]{1,0:T(8,128)(2,1)}, u32[]{:S(2)}) copy-start(bf16[8,1152]{1,0:T(8,128)(2,1)} %text_ref.1) | copy-start | bytes 55300
  99.9 7.7 %collective-permute-start.1 = (bf16[80,1152]{1,0:T(8,128)(2,1)S(1)}, bf16[80,1152]{1,0:T(8,128)(2,1)S(1)}, u32[]{:S(2)}, u32[]{:S(2)}) collective-permute-start(bf16[80,1152]{1,0:T(8,128)(2,1)S(1)} %add_convert_fusion), channel_id=1, source_target_pairs={{0,3},{1,2},{2,1},{3,0},{64,65},{65,64},{66,67},{67,66},{128,131},... | collective-permute-start | bytes 552968 | tf_op jit(solution)/shard_map/ppermute | solution.py:540

commit v5 on v4

--- a/solution.py
+++ b/solution.py
@@ -21,6 +21,8 @@
 LANES = 128
 HIDDEN_STEP = 256
 COPY_STEP = 384
+PATCH_STEP = 80
+PACK_STEP = 96
 MOST_COPIES = 24
 HIGHEST = lax.Precision.HIGHEST
 
@@ -80,9 +82,9 @@
     return jnp.where(condition, 1.0, 0.0).astype(bf16)
 
 
-def pack_kernel(dp_ref, owners_hbm, x_hbm, out_ref, owners_ref, x_ref, semaphores, *, padded):
+def pack_kernel(dp_ref, owners_hbm, x_hbm, out_hbm, owners_ref, x_ref, out_ref, semaphores, *, padded):
     copies = fetch((owners_hbm.at[0],), (owners_ref,), semaphores)
-    copies += fetch(row_pieces(x_hbm, 80), row_pieces(x_ref, 80), semaphores, 1)
+    copies += fetch(row_pieces(x_hbm, PATCH_STEP), row_pieces(x_ref, PATCH_STEP), semaphores, 1)
     rows = x_ref.shape[0]
     slots = owners_ref.shape[0]
     block_rows = rows // slots
@@ -93,9 +95,15 @@
     for b in range(slots):
         owner = jnp.where(block == b, owners_ref[dp_ref[0], b], owner)
     target = owner * padded + within
-    pick = one_hot(iota((slots * padded, rows), 0) == target)
     wait_all(copies[1:])
-    out_ref[...] = jnp.dot(pick, x_ref[...], preferred_element_type=f32).astype(bf16)
+    x = x_ref[...]
+    written = []
+    for first, many in column_chunks(out_ref.shape[0], PACK_STEP):
+        pick = one_hot(first + iota((many, rows), 0) == target)
+        out_ref[first : first + many, :] = jnp.dot(pick, x, preferred_element_type=f32).astype(bf16)
+        piece = pl.ds(first, many)
+        written += fetch((out_ref.at[piece, :],), (out_hbm.at[piece, :],), semaphores, len(copies) + len(written))
+    wait_all(written)
 
 
 def image_bounds(counts_ref, dims, axis):
@@ -133,8 +141,8 @@
     share,
 ):
     copies = fetch(
-        (counts_hbm, gain_hbm, bias_hbm, b1_hbm, *row_pieces(x_hbm, 80)),
-        (counts_ref, gain_ref, bias_ref, b1_ref, *row_pieces(x_ref, 80)),
+        (counts_hbm, gain_hbm, bias_hbm, b1_hbm, *row_pieces(x_hbm, PATCH_STEP)),
+        (counts_ref, gain_ref, bias_ref, b1_ref, *row_pieces(x_ref, PATCH_STEP)),
         semaphores,
     )
     begin = len(copies)
@@ -170,29 +178,29 @@
 def slope_kernel(
     dp_ref,
     in_ref,
+    slabs_ref,
+    text_ref,
     counts_hbm,
     owners_hbm,
     gain_hbm,
     bias_hbm,
     b1_hbm,
-    text_hbm,
     w1t_hbm,
     slope_ref,
     rows_ref,
     member_ref,
-    texts_ref,
+    packed_ref,
     counts_ref,
     owners_ref,
     gain_ref,
     bias_ref,
     b1_ref,
-    text_ref,
     w1t_ref,
     semaphores,
 ):
     copies = fetch(
-        (counts_hbm, owners_hbm.at[0], gain_hbm, bias_hbm, b1_hbm, text_hbm),
-        (counts_ref, owners_ref, gain_ref, bias_ref, b1_ref, text_ref),
+        (counts_hbm, owners_hbm.at[0], gain_hbm, bias_hbm, b1_hbm),
+        (counts_ref, owners_ref, gain_ref, bias_ref, b1_ref),
         semaphores,
     )
     firsts = fetch(column_pieces(w1t_hbm, COPY_STEP), column_pieces(w1t_ref, COPY_STEP), semaphores, len(copies))
@@ -206,14 +214,18 @@
     x = jnp.dot(pick, in_ref[...], preferred_element_type=f32)
     rows_ref[...] = x.astype(bf16)
     wait_all(copies)
-    text = text_ref[...].astype(f32)
-    texts_ref[...] = jnp.concatenate([text] * (texts_ref.shape[0] // text.shape[0]), axis=0).astype(bf16)
+    images = member_ref.shape[1]
+    total = slabs_ref[:images, :]
+    for first in range(images, slabs_ref.shape[0], images):
+        total = total + slabs_ref[first : first + images, :]
+    packed = [stacked_parts(total, 2).astype(f32), text_ref[...].astype(f32)]
+    packed_ref[...] = jnp.concatenate(packed, axis=0).astype(bf16)
     block = jnp.where(owners_ref[...] == dp_ref[0], iota((slots, slots), 1), 0)
     block = jnp.sum(block.astype(f32), axis=1, keepdims=True)
     by_source = one_hot(iota((rows, slots), 1) == source)
     block = jnp.dot(by_source, jnp.broadcast_to(block, (slots, LANES)).astype(bf16), preferred_element_type=f32)
     position = source * rows + block[:, :1].astype(jnp.int32) * block_rows + within
-    starts, ends = image_bounds(counts_ref, (1, member_ref.shape[1]), 1)
+    starts, ends = image_bounds(counts_ref, (1, images), 1)
     member_ref[...] = jnp.where((position >= starts) & (position < ends), 1.0, 0.0)
     xhat, _ = layer_statistics(x)
     normed = (xhat * gain_ref[...][None, :] + bias_ref[...][None, :]).astype(bf16)
@@ -238,8 +250,7 @@
     mp_ref,
     scale_ref,
     shift_ref,
-    pieces_ref,
-    texts_ref,
+    packed_ref,
     member_ref,
     slope_ref,
     counts_hbm,
@@ -247,13 +258,14 @@
     w2_hbm,
     w1t_hbm,
     upstream_ref,
-    parts_ref,
+    parts_hbm,
     d_act_ref,
     out_ref,
+    w1t_ref,
     counts_ref,
     labels_ref,
     w2_ref,
-    w1t_ref,
+    parts_ref,
     semaphores,
     *,
     ring,
@@ -263,12 +275,16 @@
     seconds = fetch(column_pieces(w2_hbm, COPY_STEP), column_pieces(w2_ref, COPY_STEP), semaphores, begin)
     begin += len(seconds)
     firsts = fetch(column_pieces(w1t_hbm, COPY_STEP), column_pieces(w1t_ref, COPY_STEP), semaphores, begin)
-    total = pieces_ref[0]
-    for k in range(1, pieces_ref.shape[0]):
-        total = total + pieces_ref[k]
-    images, width = total.shape
+    packed = packed_ref[...].astype(f32)
+    images, width = upstream_ref.shape
+    total = jnp.zeros((images, width), f32)
+    blocks = []
+    for first in range(0, packed.shape[0], 3 * images):
+        total = total + (packed[first : first + images] + packed[first + images : first + 2 * images])
+        blocks.append(packed[first + 2 * images : first + 3 * images])
+    wide = jnp.concatenate(blocks, axis=0)
+    texts = wide.astype(bf16)
     wait_all(copies)
-    texts = texts_ref[...]
     all_images = texts.shape[0]
     image = iota((images, 1), 0)
     count = jnp.zeros((images, 1), jnp.int32)
@@ -280,7 +296,6 @@
     embed = total / count
     norm_e = jnp.sqrt(jnp.sum(embed * embed, axis=-1, keepdims=True) + eps)
     unit_e = embed / norm_e
-    wide = texts.astype(f32)
     norm_t = jnp.sqrt(jnp.sum(wide * wide, axis=-1, keepdims=True) + eps)
     inverse_t = (1.0 / norm_t).T
     scale = scale_ref[0]
@@ -308,6 +323,7 @@
     lane = iota((all_images, LANES), 1)
     loss_lanes = jnp.where(lane == 0, loss_high, jnp.where(lane == 1, loss - loss_high, 0.0))
     parts_ref[:, width:] = loss_lanes.astype(bf16)
+    written = fetch((parts_ref,), (parts_hbm,), semaphores, begin + len(firsts))
     wait_all(seconds)
     d_image = upstream_ref[...].astype(bf16)
     d_act = lax.dot_general(d_image, w2_ref[...], NT, preferred_element_type=f32)
@@ -317,6 +333,7 @@
     share = out_ref.shape[0] // 2
     back = back_of_shares(mp_ref, (mp_ref[1], 2), ring, share, member_ref, both, slope_ref, w1t_ref)
     out_ref[...] = back.astype(bf16)
+    wait_all(written)
 
 
 def share_range(mp_ref, step, ring, share):
@@ -336,44 +353,54 @@
     return jnp.dot(d_pre, w1t, preferred_element_type=f32)
 
 
-def rest_kernel(mp_ref, d_act_ref, member_ref, slope_ref, w1t_hbm, second_ref, own_ref, w1t_ref, semaphores, *, ring):
-    firsts = fetch(column_pieces(w1t_hbm, COPY_STEP), column_pieces(w1t_ref, COPY_STEP), semaphores)
-    wait_all(firsts)
-    share = own_ref.shape[0]
-    steps = (ring - mp_ref[1], 0)
-    back = back_of_shares(mp_ref, steps, ring, share, member_ref, d_act_ref[...], slope_ref, w1t_ref)
-    second_ref[...] = back[:share]
-    own_ref[...] = back[share:]
-
-
-def row_kernel(
+def second_kernel(mp_ref, d_act_ref, member_ref, slope_ref, w1t_ref, out_ref, *, ring):
+    steps = (ring - mp_ref[1],)
+    share = out_ref.shape[0]
+    out_ref[...] = back_of_shares(mp_ref, steps, ring, share, member_ref, d_act_ref[...], slope_ref, w1t_ref)
+
+
+def own_kernel(
     mp_ref,
-    own_ref,
+    d_act_ref,
+    member_ref,
+    slope_ref,
+    w1t_ref,
     first_ref,
-    second_ref,
     x_ref,
-    member_ref,
     upstream_ref,
     gain_hbm,
-    out_ref,
+    back_ref,
+    xhat_ref,
+    deviation_ref,
+    added_ref,
+    gain_row_ref,
     gain_ref,
     semaphores,
     *,
     ring,
 ):
     copies = fetch((gain_hbm,), (gain_ref,), semaphores)
-    rows = share_range(mp_ref, 0, ring, out_ref.shape[0])
-    back = own_ref[...] + first_ref[: out_ref.shape[0], :].astype(f32) + second_ref[...].astype(f32)
+    share = back_ref.shape[0]
+    rows = share_range(mp_ref, 0, ring, share)
+    own = back_of_shares(mp_ref, (0,), ring, share, member_ref, d_act_ref[...], slope_ref, w1t_ref)
+    back_ref[...] = own + first_ref[:share, :].astype(f32)
     xhat, inverse_deviation = layer_statistics(x_ref[rows, :].astype(f32))
-    copies[0].wait()
-    dxhat = back * gain_ref[...][None, :]
-    dx = inverse_deviation * (
+    xhat_ref[...] = xhat
+    deviation_ref[...] = inverse_deviation
+    added_ref[...] = jnp.dot(member_ref[rows, :], upstream_ref[...], precision=HIGHEST, preferred_element_type=f32)
+    wait_all(copies)
+    gain_row_ref[...] = gain_ref[...][None, :]
+
+
+def row_kernel(back_ref, second_ref, xhat_ref, deviation_ref, added_ref, gain_ref, out_ref):
+    dxhat = (back_ref[...] + second_ref[...].astype(f32)) * gain_ref[...]
+    xhat = xhat_ref[...]
+    dx = deviation_ref[...] * (
         dxhat
         - jnp.mean(dxhat, axis=-1, keepdims=True)
         - xhat * jnp.mean(dxhat * xhat, axis=-1, keepdims=True)
     )
-    upstream = jnp.dot(member_ref[rows, :], upstream_ref[...], precision=HIGHEST, preferred_element_type=f32)
-    out_ref[...] = dx + upstream
+    out_ref[...] = dx + added_ref[...]
 
 
 def text_kernel(parts_ref, text_ref, grad_ref, loss_ref):
@@ -391,13 +418,13 @@
 
 
 def call(kernel, outs, operands, scratch=(), flops=0, read=0):
-    fetched = any(space is stored for space, _ in operands)
-    extra = [pltpu.SemaphoreType.DMA((MOST_COPIES,))] if fetched else []
+    copied = any(space is stored for space, _ in [*operands, *outs])
+    extra = [pltpu.SemaphoreType.DMA((MOST_COPIES,))] if copied else []
     return pl.pallas_call(
         kernel,
-        out_shape=outs,
+        out_shape=[array for _, array in outs],
         in_specs=[space for space, _ in operands],
-        out_specs=jax.tree.map(lambda _: whole, outs),
+        out_specs=[space for space, _ in outs],
         scratch_shapes=list(scratch) + extra,
         compiler_params=pltpu.CompilerParams(vmem_limit_bytes=VMEM_LIMIT),
         cost_estimate=pl.CostEstimate(flops=flops, bytes_accessed=read, transcendentals=0),
@@ -454,18 +481,25 @@
     plan_dims, counts_dims = owners.shape[1:], counts.shape
     first_room, second_room = pltpu.VMEM((hidden, width), bf16), pltpu.VMEM((hidden, width), bf16)
 
-    outgoing = call(
+    swap = [(a * dp_size + b, b * dp_size + a) for a in range(dp_size) for b in range(dp_size)]
+    text_block = lax.ppermute(text_embed, ("dp", "loss"), swap)
+
+    (outgoing,) = call(
         functools.partial(pack_kernel, padded=padded),
-        shape((dp_size * padded, width), bf16),
+        [(stored, shape((dp_size * padded, width), bf16))],
         [(scalars, dp_index), (stored, owners), (stored, patches)],
-        [pltpu.SMEM(plan_dims, jnp.int32), pltpu.VMEM((row_count, width), bf16)],
+        [
+            pltpu.SMEM(plan_dims, jnp.int32),
+            pltpu.VMEM((row_count, width), bf16),
+            pltpu.VMEM((dp_size * padded, width), bf16),
+        ],
     )
     incoming = exchange(outgoing, "dp")
 
     patches, outgoing = lax.optimization_barrier((patches, outgoing))
-    partial_sums = call(
+    (partial_sums,) = call(
         functools.partial(pool_kernel, share=1.0 / mp_size),
-        shape((images, width), f32),
+        [(whole, shape((images, width), f32))],
         [(scalars, dp_index)]
         + [(stored, array) for array in (counts, patches, gain, bias, offset, fc1_t, fc2_weight)],
         [
@@ -480,77 +514,83 @@
         flops=matmul,
         read=2 * weight_bytes,
     )
-    slab_sums = jnp.sum(lax.all_gather(partial_sums, "mp", axis=0), axis=0)
-    incoming, slab_sums = lax.optimization_barrier((incoming, slab_sums))
-    slope, rows, member, text_copies = call(
+    slab_pieces = lax.all_gather(partial_sums, "mp", axis=0, tiled=True)
+    incoming, slab_pieces = lax.optimization_barrier((incoming, slab_pieces))
+    slope, rows, member, packed = call(
         slope_kernel,
-        (
-            shape((row_count, hidden), f32),
-            shape((row_count, width), bf16),
-            shape((row_count, images), f32),
-            shape((all_images, width), bf16),
-        ),
-        [(scalars, dp_index), (whole, incoming)]
-        + [(stored, array) for array in (counts, owners, gain, bias, offset, text_embed, fc1_t)],
+        [
+            (whole, shape((row_count, hidden), f32)),
+            (whole, shape((row_count, width), bf16)),
+            (whole, shape((row_count, images), f32)),
+            (whole, shape((3 * images, width), bf16)),
+        ],
+        [(scalars, dp_index), (whole, incoming), (whole, slab_pieces), (whole, text_block)]
+        + [(stored, array) for array in (counts, owners, gain, bias, offset, fc1_t)],
         [
             pltpu.SMEM(counts_dims, jnp.int32),
             pltpu.VMEM(plan_dims, jnp.int32),
             gain_room,
             gain_room,
             offset_room,
-            pltpu.VMEM((images, width), bf16),
             first_room,
         ],
         flops=matmul,
         read=2 * weight_bytes,
     )
-    texts = exchange(text_copies, "loss")
-    slab_sums, slope = lax.optimization_barrier((slab_sums, slope))
-    pieces = lax.all_gather(slab_sums, "dp", axis=0)
-    upstream, parts, d_act, first_chunks = call(
+    all_packed = lax.all_gather(packed, "dp", axis=0, tiled=True)
+    upstream, parts, d_act, first_chunks, fc1_near = call(
         functools.partial(gradient_kernel, ring=mp_size),
         [
-            shape((images, width), f32),
-            shape((all_images, width + LANES), bf16),
-            shape((2 * images, hidden), bf16),
-            shape((2 * share_rows, width), bf16),
+            (whole, shape((images, width), f32)),
+            (stored, shape((all_images, width + LANES), bf16)),
+            (whole, shape((2 * images, hidden), bf16)),
+            (whole, shape((2 * share_rows, width), bf16)),
+            (whole, shape((hidden, width), bf16)),
         ],
         [(scalars, array) for array in (loss_index, ring_place, logit_scale, logit_bias)]
-        + [(whole, array) for array in (pieces, texts, member, slope)]
+        + [(whole, array) for array in (all_packed, member, slope)]
         + [(stored, array) for array in (counts, labels, fc2_weight, fc1_t)],
         [
             pltpu.SMEM(counts_dims, jnp.int32),
             pltpu.SMEM((all_images,), jnp.int32),
             second_room,
-            first_room,
+            pltpu.VMEM((all_images, width + LANES), bf16),
         ],
         flops=matmul,
         read=2 * weight_bytes,
     )
     first_received = lax.ppermute(first_chunks, ("dp", "mp"), first_pairs)
-    second_chunk, own_back = call(
-        functools.partial(rest_kernel, ring=mp_size),
-        [shape((share_rows, width), f32)] * 2,
-        [(scalars, ring_place), (whole, d_act), (whole, member), (whole, slope), (stored, fc1_t)],
-        [first_room],
-        flops=matmul // 2,
+    factors = [(scalars, ring_place)] + [(whole, array) for array in (d_act, member, slope, fc1_near)]
+    (second_chunk,) = call(
+        functools.partial(second_kernel, ring=mp_size),
+        [(whole, shape((share_rows, width), f32))],
+        factors,
+        flops=matmul // mp_size,
         read=weight_bytes,
     )
     second_sum = (second_chunk + first_received[share_rows:].astype(f32)).astype(bf16)
     second_received = lax.ppermute(second_sum, ("dp", "mp"), second_pairs)
+    prepared = call(
+        functools.partial(own_kernel, ring=mp_size),
+        [(whole, shape((share_rows, width), f32))] * 2
+        + [(whole, shape((share_rows, 1), f32)), (whole, shape((share_rows, width), f32)), (whole, shape((1, width), f32))],
+        factors + [(whole, array) for array in (first_received, rows, upstream)] + [(stored, gain)],
+        [gain_room],
+        flops=matmul // mp_size,
+        read=weight_bytes,
+    )
     all_parts = exchange(parts, "loss")
     grad_text, loss = call(
         text_kernel,
-        (shape((images, width), f32), shape((1, 1), f32)),
+        [(whole, shape((images, width), f32)), (whole, shape((1, 1), f32))],
         [(whole, all_parts), (whole, text_embed)],
     )
-    grad_rows = call(
-        functools.partial(row_kernel, ring=mp_size),
-        shape((share_rows, width), f32),
-        [(scalars, ring_place)]
-        + [(whole, array) for array in (own_back, first_received, second_received, rows, member, upstream)]
-        + [(stored, gain)],
-        [gain_room],
+    own_back, *others = prepared
+    own_back, grad_text, loss = lax.optimization_barrier((own_back, grad_text, loss))
+    (grad_rows,) = call(
+        row_kernel,
+        [(whole, shape((share_rows, width), f32))],
+        [(whole, array) for array in (own_back, second_received, *others)],
     )
     return (grad_rows, grad_text, loss[0, 0])
 

time: 113 us -> 117 us (1.035)
  the two profiles are of different devices: /device:TPU:1 before, /device:TPU:32 now
where the time goes in v5:
time: 117 us; the launch traced here: 116 us
  blocking collectives  40.3 us (34%)
  starting transfers between devices  39.5 us (34%)
  Pallas kernels  22.6 us (19%)
  local copies, waits for them, and re-layouts  9.69 us (8%)
  between operations  2.11 us (2%)
  waiting for transfers between devices  1.27 us (1%)
    all_gather x1, blocking collectives, shards(): all_packed = lax.all_gather(packed, 'dp', axis=0, tiled=True)  25.3 us
    pallas_call x8, Pallas kernels, call(): pl.pallas_call(kernel, out_shape=[array for _, array in outs], in_specs=[...  22.6 us
    all_gather x1, blocking collectives, shards(): slab_pieces = lax.all_gather(partial_sums, 'mp', axis=0, tiled=True)  15 us
    ppermute x1, starting transfers between devices, shards(): text_block = lax.ppermute(text_embed, ('dp', 'loss'), swap)  12.7 us
    all_to_all x2, starting transfers between devices, exchange(): return lax.all_to_all(block, axis, split_axis=0, concat_axis=0, tiled=True)  12.3 us
    ppermute x1, starting transfers between devices, shards(): second_received = lax.ppermute(second_sum, ('dp', 'mp'), second_pairs)  9.69 us
    unnamed x26, local copies, waits for them, and re-layouts  9.69 us
    ppermute x1, starting transfers between devices, shards(): first_received = lax.ppermute(first_chunks, ('dp', 'mp'), first_pairs)  4.83 us
  transfers between devices with their start and end apart: 5, of which 2 were waited for; matrix products, arithmetic and copies ran while one was open for 1% of the time, Pallas kernels for 9%

profile of v5, /device:TPU:32, one launch (start us, length us, event | category | flops | bytes accessed | tf_op | source)
XLA Modules:
  0.0 116.2 jit_solution(731278933056213364)
XLA Ops:
  0.6 0.0 copy-start.12
  0.6 2.9 %shard_map.139 = bf16[384,1152]{1,0:T(8,128)(2,1)} custom-call(s32[1]{0:T(128)} %bitcast.1.dp_ref, s32[1,16,16]{2,1,0:T(8,128)} %owners_hbm.3, bf16[320,1152]{1,0:T(8,128)(2,1)} %x_hbm.2), custom_call_target="tpu_custom_call" | custom-call | tf_op jit(solution)/shard_map/pallas_call | solution.py:423
  3.5 6.9 %all-to-all-start = ((bf16[16,24,1152]{2,1,0:T(8,128)(2,1)}), bf16[16,24,1152]{2,1,0:T(8,128)(2,1)S(1)}, u32[]{:S(2)}, u32[]{:S(2)}) async-start(bf16[16,24,1152]{2,1,0:T(8,128)(2,1)} %bitcast.3), calls=%async_computation | async-start | bytes 1769472 | tf_op jit(solution)/shard_map/all_to_all | solution.py:439
  10.4 0.0 copy-done.12
  10.4 12.7 %collective-permute-start = (bf16[8,1152]{1,0:T(8,128)(2,1)S(1)}, bf16[8,1152]{1,0:T(8,128)(2,1)S(1)}, u32[]{:S(2)}, u32[]{:S(2)}) collective-permute-start(bf16[8,1152]{1,0:T(8,128)(2,1)S(1)} %copy-done.12), channel_id=1, source_target_pairs={{0,0},{4,64},{8,128},{12,192},{16,256},{20,320},{24,384},{28,448},... | collective-permute-start | bytes 55304 | tf_op jit(solution)/shard_map/ppermute | solution.py:485
  23.1 6.1 %shard_map.140 = f32[8,1152]{1,0:T(8,128)S(1)} custom-call(s32[1]{0:T(128)} %bitcast.1.dp_ref, s32[1,8]{1,0:T(1,128)} %counts_hbm.5, bf16[320,1152]{1,0:T(8,128)(2,1)} %x_hbm.2, f32[1152]{0:T(1024)} %gain_hbm.5, f32[1152]{0:T(1024)} %bias_hbm.3, f32[1076]{0:T(1024)} %b1_hbm.3, bf16[1076,1152]{1,0:T(8,128)(2,1)} %bitcast.12, bf16[1076,1152]{1,0:T(8,128)(2,1)} %w2_hbm.3), custom_call_target="tpu_custom_call" | custom-call | flops 793313280 | bytes 4958208 | tf_op jit(solution)/shard_map/pallas_call | solution.py:423
  29.2 0.1 pad_add_fusion.mp_ref
  29.3 15.0 %all_gather.6.slabs_ref = f32[32,1152]{1,0:T(8,128)S(1)} all-gather(f32[8,1152]{1,0:T(8,128)S(1)} %shard_map.140), channel_id=1, replica_groups=mesh['dp'=16,'loss'=16,'mp'=4] {'mp'}, dimensions={0}, use_global_device_ids=true | all-gather | bytes 184320 | tf_op jit(solution)/shard_map/all_gather | solution.py:517
  45.5 0.0 all-to-all-done
  45.5 0.0 collective-permute-done.text_ref
  45.6 3.9 %shard_map.141 = (f32[320,1076]{1,0:T(8,128)S(1)}, bf16[320,1152]{1,0:T(8,128)(2,1)S(1)}, f32[320,8]{1,0:T(8,128)S(1)}, bf16[24,1152]{1,0:T(8,128)(2,1)S(1)}) custom-call(s32[1]{0:T(128)} %bitcast.1.dp_ref, bf16[384,1152]{1,0:T(8,128)(2,1)S(1)} %bitcast.9, f32[32,1152]{1,0:T(8,128)S(1)} %all_gather.6.slabs_ref, ...), custom_call_target="tpu_custom_call" | custom-call | flops 793313280 | bytes 4958208 | tf_op jit(solution)/shard_map/pallas_call | solution.py:423
  49.5 25.3 %all_gather.7.packed_ref = bf16[384,1152]{1,0:T(8,128)(2,1)S(1)} all-gather(bf16[24,1152]{1,0:T(8,128)(2,1)S(1)} %get-tuple-element.28), channel_id=1, replica_groups=mesh['dp'=16,'loss'=16,'mp'=4] {'dp'}, dimensions={0}, use_global_device_ids=true | all-gather | bytes 940032 | tf_op jit(solution)/shard_map/all_gather | solution.py:540
  74.8 4.8 %shard_map.142 = (f32[8,1152]{1,0:T(8,128)S(1)}, bf16[128,1280]{1,0:T(8,128)(2,1)S(1)}, bf16[16,1076]{1,0:T(8,128)(2,1)S(1)}, bf16[160,1152]{1,0:T(8,128)(2,1)}, bf16[1076,1152]{1,0:T(8,128)(2,1)S(1)}) custom-call(s32[1]{0:T(128)} %bitcast.2.loss_ref, s32[2]{0:T(128)S(1)} %pad_add_fusion.mp_ref, f32[1]{0:T(128)S(6)} %copy.15.scale_ref, ...), custom_call_target="tpu_custom_call" | custom-call | flops 793313280 | bytes 4958208 | tf_op jit(solution)/shard_map/pallas_call | solution.py:423
  79.6 0.0 copy-start
  79.6 1.4 %copy-done = bf16[1076,1152]{1,0:T(8,128)(2,1)} copy-done((bf16[1076,1152]{1,0:T(8,128)(2,1)}, bf16[1076,1152]{1,0:T(8,128)(2,1)S(1)}, u32[]{:S(2)}) %copy-start) | copy-done | bytes 2479128
  81.1 0.0 copy-start.9
  81.1 0.8 copy-done.9
  81.8 0.0 copy-start.10
  81.8 0.6 copy-done.10
  82.5 4.8 %collective-permute-start.1 = (bf16[160,1152]{1,0:T(8,128)(2,1)}, bf16[160,1152]{1,0:T(8,128)(2,1)S(1)}, u32[]{:S(2)}, u32[]{:S(2)}) collective-permute-start(bf16[160,1152]{1,0:T(8,128)(2,1)} %get-tuple-element.33), channel_id=1, source_target_pairs={{0,1},{1,0},{2,3},{3,2},{64,67},{65,66},{66,65},{67,64},{128,129},... | collective-permute-start | bytes 1105928 | tf_op jit(solution)/shard_map/ppermute | solution.py:562
  87.3 5.4 %all-to-all-start.1 = ((bf16[16,8,1280]{2,1,0:T(8,128)(2,1)}), bf16[16,8,1280]{2,1,0:T(8,128)(2,1)S(1)}, u32[]{:S(2)}, u32[]{:S(2)}) async-start(bf16[16,8,1280]{2,1,0:T(8,128)(2,1)} %bitcast.11), calls=%async_computation.1 | async-start | bytes 655360 | tf_op jit(solution)/shard_map/all_to_all | solution.py:439
  92.7 0.0 copy-start.1
  92.7 1.7 %copy-done.1 = bf16[1076,1152]{1,0:T(8,128)(2,1)S(1)} copy-done((bf16[1076,1152]{1,0:T(8,128)(2,1)S(1)}, bf16[1076,1152]{1,0:T(8,128)(2,1)}, u32[]{:S(2)}) %copy-start.1) | copy-done | bytes 2479128
  94.4 0.0 copy-start.2
  94.4 0.0 copy-start.11
  94.4 1.3 %shard_map.145 = f32[80,1152]{1,0:T(8,128)S(1)} custom-call(s32[2]{0:T(128)S(1)} %pad_add_fusion.mp_ref, bf16[16,1076]{1,0:T(8,128)(2,1)S(1)} %get-tuple-element.31.d_act_ref, f32[320,8]{1,0:T(8,128)S(1)} %get-tuple-element.29.member_ref, f32[320,1076]{1,0:T(8,128)S(1)} %get-tuple-element.30.slope_ref, bf16[1076,1152]{1,0:T(8,128)(2,1)S(1)} %copy-done.1), custom_call_target="tpu_custom_call" | custom-call | flops 198328320 | bytes 2479104 | tf_op jit(solution)/shard_map/pallas_call | solution.py:423
  95.7 0.5 collective-permute-done.1.first_ref
  96.2 0.7 add_convert_fusion
  96.9 9.7 %collective-permute-start.2 = (bf16[80,1152]{1,0:T(8,128)(2,1)}, bf16[80,1152]{1,0:T(8,128)(2,1)S(1)}, u32[]{:S(2)}, u32[]{:S(2)}) collective-permute-start(bf16[80,1152]{1,0:T(8,128)(2,1)} %add_convert_fusion), channel_id=1, source_target_pairs={{0,3},{1,2},{2,1},{3,0},{64,65},{65,64},{66,67},{67,66},{128,131},... | collective-permute-start | bytes 552968 | tf_op jit(solution)/shard_map/ppermute | solution.py:572
  106.6 0.0 copy-done.2
  106.6 0.0 copy-done.11
  106.7 1.8 %shard_map.143 = (f32[80,1152]{1,0:T(8,128)S(1)}, f32[80,1152]{1,0:T(8,128)S(1)}, f32[80,1]{1,0:T(8,128)S(1)}, f32[80,1152]{1,0:T(8,128)S(1)}, f32[1,1152]{1,0:T(1,128)S(1)}) custom-call(s32[2]{0:T(128)S(1)} %pad_add_fusion.mp_ref, bf16[16,1076]{1,0:T(8,128)(2,1)S(1)} %get-tuple-element.31.d_act_ref, f32[320,8]{1,0:T(8,128)S(1)} %get-tuple-element.29.member_ref, ...), custom_call_target="tpu_custom_call" | custom-call | flops 198328320 | bytes 2479104 | tf_op jit(solution)/shard_map/pallas_call | solution.py:423
  108.5 0.0 copy-start.3
  108.5 0.7 copy-done.3
  109.2 0.0 copy-start.5
  109.2 0.7 copy-done.5
  109.9 0.0 copy-start.7
  109.9 0.7 copy-done.7
  110.7 0.0 all-to-all-done.1
  110.7 0.8 shard_map.144
  111.5 0.8 collective-permute-done.2.second_ref
  112.3 0.0 copy-start.4
  112.3 1.0 copy-done.4
  113.2 0.0 copy-start.6
  113.2 1.0 copy-done.6
  114.2 0.0 copy-start.8
  114.2 1.0 copy-done.8
  115.2 1.0 shard_map.146
Async XLA Ops:
  0.6 9.8 %copy-start.12 = (bf16[8,1152]{1,0:T(8,128)(2,1)S(1)}, bf16[8,1152]{1,0:T(8,128)(2,1)}, u32[]{:S(2)}) copy-start(bf16[8,1152]{1,0:T(8,128)(2,1)} %text_ref.1) | copy-start | bytes 55300
  3.5 42.0 %all-to-all-start = ((bf16[16,24,1152]{2,1,0:T(8,128)(2,1)}), bf16[16,24,1152]{2,1,0:T(8,128)(2,1)S(1)}, u32[]{:S(2)}, u32[]{:S(2)}) async-start(bf16[16,24,1152]{2,1,0:T(8,128)(2,1)} %bitcast.3), calls=%async_computation | async-start | bytes 1769472 | tf_op jit(solution)/shard_map/all_to_all | solution.py:439
  10.4 35.1 %collective-permute-start = (bf16[8,1152]{1,0:T(8,128)(2,1)S(1)}, bf16[8,1152]{1,0:T(8,128)(2,1)S(1)}, u32[]{:S(2)}, u32[]{:S(2)}) collective-permute-start(bf16[8,1152]{1,0:T(8,128)(2,1)S(1)} %copy-done.12), channel_id=1, source_target_pairs={{0,0},{4,64},{8,128},{12,192},{16,256},{20,320},{24,384},{28,448},... | collective-permute-start | bytes 55304 | tf_op jit(solution)/shard_map/ppermute | solution.py:485
  79.6 1.5 %copy-start = (bf16[1076,1152]{1,0:T(8,128)(2,1)}, bf16[1076,1152]{1,0:T(8,128)(2,1)S(1)}, u32[]{:S(2)}) copy-start(bf16[1076,1152]{1,0:T(8,128)(2,1)S(1)} %get-tuple-element.32.w1t_ref) | copy-start | bytes 7437316
  81.1 0.8 copy-start.9
  81.8 0.6 copy-start.10
  82.5 13.8 %collective-permute-start.1 = (bf16[160,1152]{1,0:T(8,128)(2,1)}, bf16[160,1152]{1,0:T(8,128)(2,1)S(1)}, u32[]{:S(2)}, u32[]{:S(2)}) collective-permute-start(bf16[160,1152]{1,0:T(8,128)(2,1)} %get-tuple-element.33), channel_id=1, source_target_pairs={{0,1},{1,0},{2,3},{3,2},{64,67},{65,66},{66,65},{67,64},{128,129},... | collective-permute-start | bytes 1105928 | tf_op jit(solution)/shard_map/ppermute | solution.py:562
  87.3 23.4 %all-to-all-start.1 = ((bf16[16,8,1280]{2,1,0:T(8,128)(2,1)}), bf16[16,8,1280]{2,1,0:T(8,128)(2,1)S(1)}, u32[]{:S(2)}, u32[]{:S(2)}) async-start(bf16[16,8,1280]{2,1,0:T(8,128)(2,1)} %bitcast.11), calls=%async_computation.1 | async-start | bytes 655360 | tf_op jit(solution)/shard_map/all_to_all | solution.py:439
  92.7 1.7 %copy-start.1 = (bf16[1076,1152]{1,0:T(8,128)(2,1)S(1)}, bf16[1076,1152]{1,0:T(8,128)(2,1)}, u32[]{:S(2)}) copy-start(bf16[1076,1152]{1,0:T(8,128)(2,1)} %copy-done) | copy-start | bytes 7437316
  94.4 12.2 %copy-start.2 = (bf16[1076,1152]{1,0:T(8,128)(2,1)S(1)}, bf16[1076,1152]{1,0:T(8,128)(2,1)}, u32[]{:S(2)}) copy-start(bf16[1076,1152]{1,0:T(8,128)(2,1)} %copy-done) | copy-start | bytes 7437316
  94.4 12.2 %copy-start.11 = (f32[8,1152]{1,0:T(8,128)S(1)}, f32[8,1152]{1,0:T(8,128)}, u32[]{:S(2)}) copy-start(f32[8,1152]{1,0:T(8,128)} %copy-done.10) | copy-start | bytes 110596
  96.9 15.3 %collective-permute-start.2 = (bf16[80,1152]{1,0:T(8,128)(2,1)}, bf16[80,1152]{1,0:T(8,128)(2,1)S(1)}, u32[]{:S(2)}, u32[]{:S(2)}) collective-permute-start(bf16[80,1152]{1,0:T(8,128)(2,1)} %add_convert_fusion), channel_id=1, source_target_pairs={{0,3},{1,2},{2,1},{3,0},{64,65},{65,64},{66,67},{67,66},{128,131},... | collective-permute-start | bytes 552968 | tf_op jit(solution)/shard_map/ppermute | solution.py:572
  108.5 0.7 copy-start.3
  109.2 0.7 copy-start.5
  109.9 0.7 copy-start.7
  112.3 1.0 copy-start.4
  113.2 1.0 copy-start.6
  114.2 1.0 copy-start.8

commit v6 on v5

--- a/solution.py
+++ b/solution.py
@@ -177,6 +177,7 @@
 
 def slope_kernel(
     dp_ref,
+    mp_ref,
     in_ref,
     slabs_ref,
     text_ref,
@@ -187,7 +188,7 @@
     b1_hbm,
     w1t_hbm,
     slope_ref,
-    rows_ref,
+    own_ref,
     member_ref,
     packed_ref,
     counts_ref,
@@ -196,7 +197,10 @@
     bias_ref,
     b1_ref,
     w1t_ref,
+    rows_ref,
     semaphores,
+    *,
+    ring,
 ):
     copies = fetch(
         (counts_hbm, owners_hbm.at[0], gain_hbm, bias_hbm, b1_hbm),
@@ -212,7 +216,8 @@
     within = iota((rows, 1), 0) - source * block_rows
     pick = one_hot(iota((rows, in_ref.shape[0]), 1) == source * padded + within)
     x = jnp.dot(pick, in_ref[...], preferred_element_type=f32)
-    rows_ref[...] = x.astype(bf16)
+    rows_ref[...] = x
+    own_ref[...] = rows_ref[share_range(mp_ref, 0, ring, own_ref.shape[0]), :].astype(bf16)
     wait_all(copies)
     images = member_ref.shape[1]
     total = slabs_ref[:images, :]
@@ -261,10 +266,10 @@
     parts_hbm,
     d_act_ref,
     out_ref,
-    w1t_ref,
     counts_ref,
     labels_ref,
     w2_ref,
+    w1t_ref,
     parts_ref,
     semaphores,
     *,
@@ -353,7 +358,8 @@
     return jnp.dot(d_pre, w1t, preferred_element_type=f32)
 
 
-def second_kernel(mp_ref, d_act_ref, member_ref, slope_ref, w1t_ref, out_ref, *, ring):
+def second_kernel(mp_ref, d_act_ref, member_ref, slope_ref, w1t_hbm, out_ref, w1t_ref, semaphores, *, ring):
+    wait_all(fetch(column_pieces(w1t_hbm, COPY_STEP), column_pieces(w1t_ref, COPY_STEP), semaphores))
     steps = (ring - mp_ref[1],)
     share = out_ref.shape[0]
     out_ref[...] = back_of_shares(mp_ref, steps, ring, share, member_ref, d_act_ref[...], slope_ref, w1t_ref)
@@ -364,46 +370,26 @@
     d_act_ref,
     member_ref,
     slope_ref,
+    first_ref,
+    parts_ref,
+    w1t_hbm,
+    gain_hbm,
+    text_hbm,
+    back_ref,
+    gain_row_ref,
+    grad_ref,
+    loss_ref,
     w1t_ref,
-    first_ref,
-    x_ref,
-    upstream_ref,
-    gain_hbm,
-    back_ref,
-    xhat_ref,
-    deviation_ref,
-    added_ref,
-    gain_row_ref,
     gain_ref,
+    text_ref,
     semaphores,
     *,
     ring,
 ):
-    copies = fetch((gain_hbm,), (gain_ref,), semaphores)
-    share = back_ref.shape[0]
-    rows = share_range(mp_ref, 0, ring, share)
-    own = back_of_shares(mp_ref, (0,), ring, share, member_ref, d_act_ref[...], slope_ref, w1t_ref)
-    back_ref[...] = own + first_ref[:share, :].astype(f32)
-    xhat, inverse_deviation = layer_statistics(x_ref[rows, :].astype(f32))
-    xhat_ref[...] = xhat
-    deviation_ref[...] = inverse_deviation
-    added_ref[...] = jnp.dot(member_ref[rows, :], upstream_ref[...], precision=HIGHEST, preferred_element_type=f32)
+    copies = fetch((gain_hbm, text_hbm), (gain_ref, text_ref), semaphores)
+    firsts = fetch(column_pieces(w1t_hbm, COPY_STEP), column_pieces(w1t_ref, COPY_STEP), semaphores, len(copies))
     wait_all(copies)
     gain_row_ref[...] = gain_ref[...][None, :]
-
-
-def row_kernel(back_ref, second_ref, xhat_ref, deviation_ref, added_ref, gain_ref, out_ref):
-    dxhat = (back_ref[...] + second_ref[...].astype(f32)) * gain_ref[...]
-    xhat = xhat_ref[...]
-    dx = deviation_ref[...] * (
-        dxhat
-        - jnp.mean(dxhat, axis=-1, keepdims=True)
-        - xhat * jnp.mean(dxhat * xhat, axis=-1, keepdims=True)
-    )
-    out_ref[...] = dx + added_ref[...]
-
-
-def text_kernel(parts_ref, text_ref, grad_ref, loss_ref):
     text = text_ref[...].astype(f32)
     texts, width = text.shape
     parts = parts_ref[...].astype(f32)
@@ -415,6 +401,23 @@
     dv = total[:, :width]
     grad_ref[...] = (dv - unit * jnp.sum(unit * dv, axis=-1, keepdims=True)) / norm
     loss_ref[...] = jnp.sum(total[:1, width:], axis=1, keepdims=True)
+    wait_all(firsts)
+    share = back_ref.shape[0]
+    own = back_of_shares(mp_ref, (0,), ring, share, member_ref, d_act_ref[...], slope_ref, w1t_ref)
+    back_ref[...] = own + first_ref[:share, :].astype(f32)
+
+
+def row_kernel(mp_ref, back_ref, second_ref, x_ref, member_ref, upstream_ref, gain_ref, out_ref, *, ring):
+    rows = share_range(mp_ref, 0, ring, out_ref.shape[0])
+    xhat, inverse_deviation = layer_statistics(x_ref[...].astype(f32))
+    added = jnp.dot(member_ref[rows, :], upstream_ref[...], precision=HIGHEST, preferred_element_type=f32)
+    dxhat = (back_ref[...] + second_ref[...].astype(f32)) * gain_ref[...]
+    dx = inverse_deviation * (
+        dxhat
+        - jnp.mean(dxhat, axis=-1, keepdims=True)
+        - xhat * jnp.mean(dxhat * xhat, axis=-1, keepdims=True)
+    )
+    out_ref[...] = dx + added
 
 
 def call(kernel, outs, operands, scratch=(), flops=0, read=0):
@@ -496,7 +499,7 @@
     )
     incoming = exchange(outgoing, "dp")
 
-    patches, outgoing = lax.optimization_barrier((patches, outgoing))
+    patches, outgoing, text_block = lax.optimization_barrier((patches, outgoing, text_block))
     (partial_sums,) = call(
         functools.partial(pool_kernel, share=1.0 / mp_size),
         [(whole, shape((images, width), f32))],
@@ -516,15 +519,15 @@
     )
     slab_pieces = lax.all_gather(partial_sums, "mp", axis=0, tiled=True)
     incoming, slab_pieces = lax.optimization_barrier((incoming, slab_pieces))
-    slope, rows, member, packed = call(
-        slope_kernel,
+    slope, own_rows, member, packed = call(
+        functools.partial(slope_kernel, ring=mp_size),
         [
             (whole, shape((row_count, hidden), f32)),
-            (whole, shape((row_count, width), bf16)),
+            (whole, shape((share_rows, width), bf16)),
             (whole, shape((row_count, images), f32)),
             (whole, shape((3 * images, width), bf16)),
         ],
-        [(scalars, dp_index), (whole, incoming), (whole, slab_pieces), (whole, text_block)]
+        [(scalars, dp_index), (scalars, ring_place), (whole, incoming), (whole, slab_pieces), (whole, text_block)]
         + [(stored, array) for array in (counts, owners, gain, bias, offset, fc1_t)],
         [
             pltpu.SMEM(counts_dims, jnp.int32),
@@ -533,19 +536,19 @@
             gain_room,
             offset_room,
             first_room,
+            pltpu.VMEM((row_count, width), f32),
         ],
         flops=matmul,
         read=2 * weight_bytes,
     )
     all_packed = lax.all_gather(packed, "dp", axis=0, tiled=True)
-    upstream, parts, d_act, first_chunks, fc1_near = call(
+    upstream, parts, d_act, first_chunks = call(
         functools.partial(gradient_kernel, ring=mp_size),
         [
             (whole, shape((images, width), f32)),
             (stored, shape((all_images, width + LANES), bf16)),
             (whole, shape((2 * images, hidden), bf16)),
             (whole, shape((2 * share_rows, width), bf16)),
-            (whole, shape((hidden, width), bf16)),
         ],
         [(scalars, array) for array in (loss_index, ring_place, logit_scale, logit_bias)]
         + [(whole, array) for array in (all_packed, member, slope)]
@@ -554,43 +557,38 @@
             pltpu.SMEM(counts_dims, jnp.int32),
             pltpu.SMEM((all_images,), jnp.int32),
             second_room,
+            first_room,
             pltpu.VMEM((all_images, width + LANES), bf16),
         ],
         flops=matmul,
         read=2 * weight_bytes,
     )
     first_received = lax.ppermute(first_chunks, ("dp", "mp"), first_pairs)
-    factors = [(scalars, ring_place)] + [(whole, array) for array in (d_act, member, slope, fc1_near)]
+    factors = [(scalars, ring_place)] + [(whole, array) for array in (d_act, member, slope)]
     (second_chunk,) = call(
         functools.partial(second_kernel, ring=mp_size),
         [(whole, shape((share_rows, width), f32))],
-        factors,
+        factors + [(stored, fc1_t)],
+        [first_room],
         flops=matmul // mp_size,
         read=weight_bytes,
     )
     second_sum = (second_chunk + first_received[share_rows:].astype(f32)).astype(bf16)
     second_received = lax.ppermute(second_sum, ("dp", "mp"), second_pairs)
-    prepared = call(
+    all_parts = exchange(parts, "loss")
+    own_back, gain_row, grad_text, loss = call(
         functools.partial(own_kernel, ring=mp_size),
-        [(whole, shape((share_rows, width), f32))] * 2
-        + [(whole, shape((share_rows, 1), f32)), (whole, shape((share_rows, width), f32)), (whole, shape((1, width), f32))],
-        factors + [(whole, array) for array in (first_received, rows, upstream)] + [(stored, gain)],
-        [gain_room],
+        [(whole, shape(dims, f32)) for dims in ((share_rows, width), (1, width), (images, width), (1, 1))],
+        factors + [(whole, first_received), (whole, all_parts)] + [(stored, array) for array in (fc1_t, gain, text_embed)],
+        [first_room, gain_room, pltpu.VMEM((images, width), bf16)],
         flops=matmul // mp_size,
         read=weight_bytes,
     )
-    all_parts = exchange(parts, "loss")
-    grad_text, loss = call(
-        text_kernel,
-        [(whole, shape((images, width), f32)), (whole, shape((1, 1), f32))],
-        [(whole, all_parts), (whole, text_embed)],
-    )
-    own_back, *others = prepared
-    own_back, grad_text, loss = lax.optimization_barrier((own_back, grad_text, loss))
     (grad_rows,) = call(
-        row_kernel,
+        functools.partial(row_kernel, ring=mp_size),
         [(whole, shape((share_rows, width), f32))],
-        [(whole, array) for array in (own_back, second_received, *others)],
+        [(scalars, ring_place)]
+        + [(whole, array) for array in (own_back, second_received, own_rows, member, upstream, gain_row)],
     )
     return (grad_rows, grad_text, loss[0, 0])
 

time: 117 us -> 127 us (1.085)
  the two profiles are of different devices: /device:TPU:32 before, /device:TPU:1 now
where the time goes in v6:
time: 127 us; the launch traced here: 126 us
  blocking collectives  56.2 us (44%)
  starting transfers between devices  32.7 us (26%)
  Pallas kernels  26.2 us (21%)
  waiting for transfers between devices  8.78 us (7%)
  between operations  2.07 us (2%)
    all_gather x1, blocking collectives, shards(): all_packed = lax.all_gather(packed, 'dp', axis=0, tiled=True)  43.4 us
    pallas_call x7, Pallas kernels, call(): pl.pallas_call(kernel, out_shape=[array for _, array in outs], in_specs=[...  26.2 us
    all_to_all x2, starting transfers between devices, exchange(): return lax.all_to_all(block, axis, split_axis=0, concat_axis=0, tiled=True)  22.8 us
    all_gather x1, blocking collectives, shards(): slab_pieces = lax.all_gather(partial_sums, 'mp', axis=0, tiled=True)  12.9 us
    all_to_all x2, waiting for transfers between devices, exchange(): return lax.all_to_all(block, axis, split_axis=0, concat_axis=0, tiled=True)  7.01 us
    ppermute x1, starting transfers between devices, shards(): first_received = lax.ppermute(first_chunks, ('dp', 'mp'), first_pairs)  6.02 us
  transfers between devices with their start and end apart: 5, of which 3 were waited for; matrix products, arithmetic and copies ran while one was open for 0% of the time, Pallas kernels for 10%

profile of v6, /device:TPU:1, one launch (start us, length us, event | category | flops | bytes accessed | tf_op | source)
XLA Modules:
  0.0 126.1 jit_solution(11105895605592083467)
XLA Ops:
  0.6 0.0 copy-start
  0.6 2.9 %shard_map.139 = bf16[384,1152]{1,0:T(8,128)(2,1)} custom-call(s32[1]{0:T(128)} %bitcast.1.dp_ref, s32[1,16,16]{2,1,0:T(8,128)} %owners_hbm.3, bf16[320,1152]{1,0:T(8,128)(2,1)} %x_hbm.2), custom_call_target="tpu_custom_call" | custom-call | tf_op jit(solution)/shard_map/pallas_call | solution.py:426
  3.5 17.6 %all-to-all-start = ((bf16[16,24,1152]{2,1,0:T(8,128)(2,1)}), bf16[16,24,1152]{2,1,0:T(8,128)(2,1)S(1)}, u32[]{:S(2)}, u32[]{:S(2)}) async-start(bf16[16,24,1152]{2,1,0:T(8,128)(2,1)} %bitcast.3), calls=%async_computation | async-start | bytes 1769472 | tf_op jit(solution)/shard_map/all_to_all | solution.py:442
  21.1 0.0 copy-done
  21.1 1.9 %collective-permute-start = (bf16[8,1152]{1,0:T(8,128)(2,1)S(1)}, bf16[8,1152]{1,0:T(8,128)(2,1)S(1)}, u32[]{:S(2)}, u32[]{:S(2)}) collective-permute-start(bf16[8,1152]{1,0:T(8,128)(2,1)S(1)} %copy-done), channel_id=1, source_target_pairs={{0,0},{4,64},{8,128},{12,192},{16,256},{20,320},{24,384},{28,448},... | collective-permute-start | bytes 55304 | tf_op jit(solution)/shard_map/ppermute | solution.py:488
  23.1 0.1 pad_add_fusion.mp_ref
  24.5 1.8 %collective-permute-done.text_ref = bf16[8,1152]{1,0:T(8,128)(2,1)S(1)} collective-permute-done((bf16[8,1152]{1,0:T(8,128)(2,1)S(1)}, bf16[8,1152]{1,0:T(8,128)(2,1)S(1)}, u32[]{:S(2)}, u32[]{:S(2)}) %collective-permute-start) | collective-permute-done | bytes 18464 | tf_op jit(solution)/shard_map/ppermute | solution.py:488
  26.2 6.0 %shard_map.140 = f32[8,1152]{1,0:T(8,128)S(1)} custom-call(s32[1]{0:T(128)} %bitcast.1.dp_ref, s32[1,8]{1,0:T(1,128)} %counts_hbm.5, bf16[320,1152]{1,0:T(8,128)(2,1)} %x_hbm.2, f32[1152]{0:T(1024)} %gain_hbm.5, f32[1152]{0:T(1024)} %bias_hbm.3, f32[1076]{0:T(1024)} %b1_hbm.3, bf16[1076,1152]{1,0:T(8,128)(2,1)} %bitcast.11, bf16[1076,1152]{1,0:T(8,128)(2,1)} %w2_hbm.3), custom_call_target="tpu_custom_call" | custom-call | flops 793313280 | bytes 4958208 | tf_op jit(solution)/shard_map/pallas_call | solution.py:426
  32.3 12.9 %all_gather.6.slabs_ref = f32[32,1152]{1,0:T(8,128)S(1)} all-gather(f32[8,1152]{1,0:T(8,128)S(1)} %shard_map.140), channel_id=1, replica_groups=mesh['dp'=16,'loss'=16,'mp'=4] {'mp'}, dimensions={0}, use_global_device_ids=true | all-gather | bytes 184320 | tf_op jit(solution)/shard_map/all_gather | solution.py:520
  45.1 0.7 all-to-all-done
  45.8 4.9 %shard_map.141 = (f32[320,1076]{1,0:T(8,128)S(1)}, bf16[80,1152]{1,0:T(8,128)(2,1)S(1)}, f32[320,8]{1,0:T(8,128)S(1)}, bf16[24,1152]{1,0:T(8,128)(2,1)S(1)}) custom-call(s32[1]{0:T(128)} %bitcast.1.dp_ref, s32[2]{0:T(128)S(1)} %pad_add_fusion.mp_ref, bf16[384,1152]{1,0:T(8,128)(2,1)S(1)} %bitcast.9, f32[32,1152]{1,0:T(8,128)S(1)} %all_gather.6.slabs_ref, ...), custom_call_target="tpu_custom_call" | custom-call | flops 793313280 | bytes 4958208 | tf_op jit(solution)/shard_map/pallas_call | solution.py:426
  50.7 43.4 %all_gather.7.packed_ref = bf16[384,1152]{1,0:T(8,128)(2,1)S(1)} all-gather(bf16[24,1152]{1,0:T(8,128)(2,1)S(1)} %get-tuple-element.23), channel_id=1, replica_groups=mesh['dp'=16,'loss'=16,'mp'=4] {'dp'}, dimensions={0}, use_global_device_ids=true | all-gather | bytes 940032 | tf_op jit(solution)/shard_map/all_gather | solution.py:544
  94.1 4.2 %shard_map.142 = (f32[8,1152]{1,0:T(8,128)S(1)}, bf16[128,1280]{1,0:T(8,128)(2,1)}, bf16[16,1076]{1,0:T(8,128)(2,1)S(1)}, bf16[160,1152]{1,0:T(8,128)(2,1)S(1)}) custom-call(s32[1]{0:T(128)} %bitcast.2.loss_ref, s32[2]{0:T(128)S(1)} %pad_add_fusion.mp_ref, f32[1]{0:T(128)S(6)} %copy.15.scale_ref, f32[1]{0:T(128)S(6)} %copy.16.shift_ref, ...), custom_call_target="tpu_custom_call" | custom-call | flops 793313280 | bytes 4958208 | tf_op jit(solution)/shard_map/pallas_call | solution.py:426
  98.3 6.0 %collective-permute-start.1 = (bf16[160,1152]{1,0:T(8,128)(2,1)S(1)}, bf16[160,1152]{1,0:T(8,128)(2,1)S(1)}, u32[]{:S(2)}, u32[]{:S(2)}) collective-permute-start(bf16[160,1152]{1,0:T(8,128)(2,1)S(1)} %get-tuple-element.27), channel_id=1, source_target_pairs={{0,1},{1,0},{2,3},{3,2},{64,67},{65,66},{66,65},{67,64},{128,129},... | collective-permute-start | bytes 1105928 | tf_op jit(solution)/shard_map/ppermute | solution.py:566
  104.3 5.2 %all-to-all-start.1 = ((bf16[16,8,1280]{2,1,0:T(8,128)(2,1)}), bf16[16,8,1280]{2,1,0:T(8,128)(2,1)S(1)}, u32[]{:S(2)}, u32[]{:S(2)}) async-start(bf16[16,8,1280]{2,1,0:T(8,128)(2,1)} %bitcast.6), calls=%async_computation.1 | async-start | bytes 655360 | tf_op jit(solution)/shard_map/all_to_all | solution.py:442
  109.5 3.2 %shard_map.144 = f32[80,1152]{1,0:T(8,128)S(1)} custom-call(s32[2]{0:T(128)S(1)} %pad_add_fusion.mp_ref, bf16[16,1076]{1,0:T(8,128)(2,1)S(1)} %get-tuple-element.26.d_act_ref, f32[320,8]{1,0:T(8,128)S(1)} %get-tuple-element.24.member_ref, f32[320,1076]{1,0:T(8,128)S(1)} %get-tuple-element.25.slope_ref, bf16[1076,1152]{1,0:T(8,128)(2,1)} %bitcast.14), custom_call_target="tpu_custom_call" | custom-call | flops 198328320 | bytes 2479104 | tf_op jit(solution)/shard_map/pallas_call | solution.py:426
  112.7 0.0 collective-permute-done.1.first_ref
  112.8 1.9 %collective-permute-start.2 = (bf16[80,1152]{1,0:T(8,128)(2,1)S(1)}, bf16[80,1152]{1,0:T(8,128)(2,1)S(1)}, u32[]{:S(2)}, u32[]{:S(2)}) collective-permute-start(bf16[80,1152]{1,0:T(8,128)(2,1)S(1)} %add_convert_fusion), channel_id=1, source_target_pairs={{0,3},{1,2},{2,1},{3,0},{64,65},{65,64},{66,67},{67,66},{128,131},... | collective-permute-start | bytes 552968 | tf_op jit(solution)/shard_map/ppermute | solution.py:577
  114.7 6.3 %all-to-all-done.1 = bf16[16,8,1280]{2,1,0:T(8,128)(2,1)S(1)} async-done(((bf16[16,8,1280]{2,1,0:T(8,128)(2,1)}), bf16[16,8,1280]{2,1,0:T(8,128)(2,1)S(1)}, u32[]{:S(2)}, u32[]{:S(2)}) %all-to-all-start.1) | async-done | bytes 327712 | tf_op jit(solution)/shard_map/all_to_all | solution.py:442
  121.0 3.2 %shard_map.143 = (f32[80,1152]{1,0:T(8,128)S(1)}, f32[1,1152]{1,0:T(1,128)S(1)}, f32[8,1152]{1,0:T(8,128)}, f32[1,1]{1,0:T(1,128)}) custom-call(s32[2]{0:T(128)S(1)} %pad_add_fusion.mp_ref, bf16[16,1076]{1,0:T(8,128)(2,1)S(1)} %get-tuple-element.26.d_act_ref, f32[320,8]{1,0:T(8,128)S(1)} %get-tuple-element.24.member_ref, ...), custom_call_target="tpu_custom_call" | custom-call | flops 198328320 | bytes 2479104 | tf_op jit(solution)/shard_map/pallas_call | solution.py:426
  124.3 0.0 collective-permute-done.2.second_ref
  124.3 1.8 %shard_map.145 = f32[80,1152]{1,0:T(8,128)} custom-call(s32[2]{0:T(128)S(1)} %pad_add_fusion.mp_ref, f32[80,1152]{1,0:T(8,128)S(1)} %get-tuple-element.29.back_ref, bf16[80,1152]{1,0:T(8,128)(2,1)S(1)} %collective-permute-done.2.second_ref, bf16[80,1152]{1,0:T(8,128)(2,1)S(1)} %get-tuple-element.30.x_ref, f32[320,8]{1,0:T(8,128)S(1)} %get-tuple-element.24.member_ref, ...), custom_call_target="tpu_custom_call" | custom-call | tf_op jit(solution)/shard_map/pallas_call | solution.py:426
  (1 shorter events, 0.0 us)
Async XLA Ops:
  0.6 20.5 %copy-start = (bf16[8,1152]{1,0:T(8,128)(2,1)S(1)}, bf16[8,1152]{1,0:T(8,128)(2,1)}, u32[]{:S(2)}) copy-start(bf16[8,1152]{1,0:T(8,128)(2,1)} %text_hbm.1) | copy-start | bytes 55300
  3.5 42.3 %all-to-all-start = ((bf16[16,24,1152]{2,1,0:T(8,128)(2,1)}), bf16[16,24,1152]{2,1,0:T(8,128)(2,1)S(1)}, u32[]{:S(2)}, u32[]{:S(2)}) async-start(bf16[16,24,1152]{2,1,0:T(8,128)(2,1)} %bitcast.3), calls=%async_computation | async-start | bytes 1769472 | tf_op jit(solution)/shard_map/all_to_all | solution.py:442
  21.1 5.1 %collective-permute-start = (bf16[8,1152]{1,0:T(8,128)(2,1)S(1)}, bf16[8,1152]{1,0:T(8,128)(2,1)S(1)}, u32[]{:S(2)}, u32[]{:S(2)}) collective-permute-start(bf16[8,1152]{1,0:T(8,128)(2,1)S(1)} %copy-done), channel_id=1, source_target_pairs={{0,0},{4,64},{8,128},{12,192},{16,256},{20,320},{24,384},{28,448},... | collective-permute-start | bytes 55304 | tf_op jit(solution)/shard_map/ppermute | solution.py:488
  98.3 14.5 %collective-permute-start.1 = (bf16[160,1152]{1,0:T(8,128)(2,1)S(1)}, bf16[160,1152]{1,0:T(8,128)(2,1)S(1)}, u32[]{:S(2)}, u32[]{:S(2)}) collective-permute-start(bf16[160,1152]{1,0:T(8,128)(2,1)S(1)} %get-tuple-element.27), channel_id=1, source_target_pairs={{0,1},{1,0},{2,3},{3,2},{64,67},{65,66},{66,65},{67,64},{128,129},... | collective-permute-start | bytes 1105928 | tf_op jit(solution)/shard_map/ppermute | solution.py:566
  104.3 16.8 %all-to-all-start.1 = ((bf16[16,8,1280]{2,1,0:T(8,128)(2,1)}), bf16[16,8,1280]{2,1,0:T(8,128)(2,1)S(1)}, u32[]{:S(2)}, u32[]{:S(2)}) async-start(bf16[16,8,1280]{2,1,0:T(8,128)(2,1)} %bitcast.6), calls=%async_computation.1 | async-start | bytes 655360 | tf_op jit(solution)/shard_map/all_to_all | solution.py:442
  112.8 11.5 %collective-permute-start.2 = (bf16[80,1152]{1,0:T(8,128)(2,1)S(1)}, bf16[80,1152]{1,0:T(8,128)(2,1)S(1)}, u32[]{:S(2)}, u32[]{:S(2)}) collective-permute-start(bf16[80,1152]{1,0:T(8,128)(2,1)S(1)} %add_convert_fusion), channel_id=1, source_target_pairs={{0,3},{1,2},{2,1},{3,0},{64,65},{65,64},{66,67},{67,66},{128,131},... | collective-permute-start | bytes 552968 | tf_op jit(solution)/shard_map/ppermute | solution.py:577

commit v7 on v6

--- a/solution.py
+++ b/solution.py
@@ -179,23 +179,23 @@
     dp_ref,
     mp_ref,
     in_ref,
-    slabs_ref,
-    text_ref,
     counts_hbm,
     owners_hbm,
     gain_hbm,
     bias_hbm,
     b1_hbm,
+    text_hbm,
     w1t_hbm,
     slope_ref,
     own_ref,
     member_ref,
-    packed_ref,
+    texts_ref,
     counts_ref,
     owners_ref,
     gain_ref,
     bias_ref,
     b1_ref,
+    text_ref,
     w1t_ref,
     rows_ref,
     semaphores,
@@ -203,8 +203,8 @@
     ring,
 ):
     copies = fetch(
-        (counts_hbm, owners_hbm.at[0], gain_hbm, bias_hbm, b1_hbm),
-        (counts_ref, owners_ref, gain_ref, bias_ref, b1_ref),
+        (counts_hbm, owners_hbm.at[0], gain_hbm, bias_hbm, b1_hbm, text_hbm),
+        (counts_ref, owners_ref, gain_ref, bias_ref, b1_ref, text_ref),
         semaphores,
     )
     firsts = fetch(column_pieces(w1t_hbm, COPY_STEP), column_pieces(w1t_ref, COPY_STEP), semaphores, len(copies))
@@ -220,11 +220,8 @@
     own_ref[...] = rows_ref[share_range(mp_ref, 0, ring, own_ref.shape[0]), :].astype(bf16)
     wait_all(copies)
     images = member_ref.shape[1]
-    total = slabs_ref[:images, :]
-    for first in range(images, slabs_ref.shape[0], images):
-        total = total + slabs_ref[first : first + images, :]
-    packed = [stacked_parts(total, 2).astype(f32), text_ref[...].astype(f32)]
-    packed_ref[...] = jnp.concatenate(packed, axis=0).astype(bf16)
+    text = text_ref[...].astype(f32)
+    texts_ref[...] = jnp.concatenate([text] * (texts_ref.shape[0] // text.shape[0]), axis=0).astype(bf16)
     block = jnp.where(owners_ref[...] == dp_ref[0], iota((slots, slots), 1), 0)
     block = jnp.sum(block.astype(f32), axis=1, keepdims=True)
     by_source = one_hot(iota((rows, slots), 1) == source)
@@ -255,7 +252,8 @@
     mp_ref,
     scale_ref,
     shift_ref,
-    packed_ref,
+    pieces_ref,
+    texts_ref,
     member_ref,
     slope_ref,
     counts_hbm,
@@ -280,15 +278,12 @@
     seconds = fetch(column_pieces(w2_hbm, COPY_STEP), column_pieces(w2_ref, COPY_STEP), semaphores, begin)
     begin += len(seconds)
     firsts = fetch(column_pieces(w1t_hbm, COPY_STEP), column_pieces(w1t_ref, COPY_STEP), semaphores, begin)
-    packed = packed_ref[...].astype(f32)
     images, width = upstream_ref.shape
-    total = jnp.zeros((images, width), f32)
-    blocks = []
-    for first in range(0, packed.shape[0], 3 * images):
-        total = total + (packed[first : first + images] + packed[first + images : first + 2 * images])
-        blocks.append(packed[first + 2 * images : first + 3 * images])
-    wide = jnp.concatenate(blocks, axis=0)
-    texts = wide.astype(bf16)
+    total = pieces_ref[:images, :]
+    for first in range(images, pieces_ref.shape[0], images):
+        total = total + pieces_ref[first : first + images, :]
+    texts = texts_ref[...]
+    wide = texts.astype(f32)
     wait_all(copies)
     all_images = texts.shape[0]
     image = iota((images, 1), 0)
@@ -484,9 +479,6 @@
     plan_dims, counts_dims = owners.shape[1:], counts.shape
     first_room, second_room = pltpu.VMEM((hidden, width), bf16), pltpu.VMEM((hidden, width), bf16)
 
-    swap = [(a * dp_size + b, b * dp_size + a) for a in range(dp_size) for b in range(dp_size)]
-    text_block = lax.ppermute(text_embed, ("dp", "loss"), swap)
-
     (outgoing,) = call(
         functools.partial(pack_kernel, padded=padded),
         [(stored, shape((dp_size * padded, width), bf16))],
@@ -499,7 +491,7 @@
     )
     incoming = exchange(outgoing, "dp")
 
-    patches, outgoing, text_block = lax.optimization_barrier((patches, outgoing, text_block))
+    patches, outgoing = lax.optimization_barrier((patches, outgoing))
     (partial_sums,) = call(
         functools.partial(pool_kernel, share=1.0 / mp_size),
         [(whole, shape((images, width), f32))],
@@ -517,31 +509,34 @@
         flops=matmul,
         read=2 * weight_bytes,
     )
-    slab_pieces = lax.all_gather(partial_sums, "mp", axis=0, tiled=True)
-    incoming, slab_pieces = lax.optimization_barrier((incoming, slab_pieces))
-    slope, own_rows, member, packed = call(
+    slab_sums = jnp.sum(lax.all_gather(partial_sums, "mp", axis=0), axis=0)
+    incoming, slab_sums = lax.optimization_barrier((incoming, slab_sums))
+    slope, own_rows, member, text_copies = call(
         functools.partial(slope_kernel, ring=mp_size),
         [
             (whole, shape((row_count, hidden), f32)),
             (whole, shape((share_rows, width), bf16)),
             (whole, shape((row_count, images), f32)),
-            (whole, shape((3 * images, width), bf16)),
+            (whole, shape((all_images, width), bf16)),
         ],
-        [(scalars, dp_index), (scalars, ring_place), (whole, incoming), (whole, slab_pieces), (whole, text_block)]
-        + [(stored, array) for array in (counts, owners, gain, bias, offset, fc1_t)],
+        [(scalars, dp_index), (scalars, ring_place), (whole, incoming)]
+        + [(stored, array) for array in (counts, owners, gain, bias, offset, text_embed, fc1_t)],
         [
             pltpu.SMEM(counts_dims, jnp.int32),
             pltpu.VMEM(plan_dims, jnp.int32),
             gain_room,
             gain_room,
             offset_room,
+            pltpu.VMEM((images, width), bf16),
             first_room,
             pltpu.VMEM((row_count, width), f32),
         ],
         flops=matmul,
         read=2 * weight_bytes,
     )
-    all_packed = lax.all_gather(packed, "dp", axis=0, tiled=True)
+    texts = exchange(text_copies, "loss")
+    slab_sums, slope = lax.optimization_barrier((slab_sums, slope))
+    pieces = lax.all_gather(slab_sums, "dp", axis=0, tiled=True)
     upstream, parts, d_act, first_chunks = call(
         functools.partial(gradient_kernel, ring=mp_size),
         [
@@ -551,7 +546,7 @@
             (whole, shape((2 * share_rows, width), bf16)),
         ],
         [(scalars, array) for array in (loss_index, ring_place, logit_scale, logit_bias)]
-        + [(whole, array) for array in (all_packed, member, slope)]
+        + [(whole, array) for array in (pieces, texts, member, slope)]
         + [(stored, array) for array in (counts, labels, fc2_weight, fc1_t)],
         [
             pltpu.SMEM(counts_dims, jnp.int32),

time: 127 us -> 112 us (0.88)
  blocking collectives: 56.2 us -> 34 us
  starting transfers between devices: 32.7 us -> 38.3 us
  waiting for transfers between devices: 8.78 us -> 11 us
    all_gather x2, blocking collectives: 56.2 us -> 34 us  [the longest x1 20.9 us: shards(): pieces = lax.all_gather(slab_sums, 'dp', axis=0, tiled=True)]
    all_to_all x2 -> x3, starting transfers between devices: 22.8 us -> 29 us  [exchange(): return lax.all_to_all(block, axis, split_axis=0, concat_axis=0, tiled=True)]
    all_to_all x2 -> x3, waiting for transfers between devices: 7.01 us -> 11 us  [exchange(): return lax.all_to_all(block, axis, split_axis=0, concat_axis=0, tiled=True)]
    ppermute x1 -> x0, starting transfers between devices: 1.92 us -> none  [shards(): text_block = lax.ppermute(text_embed, ('dp', 'loss'), swap)]
    ppermute x1 -> x0, waiting for transfers between devices: 1.76 us -> none  [shards(): text_block = lax.ppermute(text_embed, ('dp', 'loss'), swap)]
    ppermute x1, starting transfers between devices: 6.02 us -> 7.39 us  [shards(): first_received = lax.ppermute(first_chunks, ('dp', 'mp'), first_pairs)]
  transfers between devices with their start and end apart: 5 -> 5, of which waited for: 3 -> 2; matrix products, arithmetic and copies ran while one was open for 0% -> 0% of each run, Pallas kernels for 10% -> 11%
where the time goes in v7:
time: 112 us
  starting transfers between devices  38.3 us (34%)
  blocking collectives  34 us (30%)
  Pallas kernels  26.3 us (23%)
  waiting for transfers between devices  11 us (10%)
  between operations  2.05 us (2%)
    all_to_all x3, starting transfers between devices, exchange(): return lax.all_to_all(block, axis, split_axis=0, concat_axis=0, tiled=True)  29 us
    pallas_call x7, Pallas kernels, call(): pl.pallas_call(kernel, out_shape=[array for _, array in outs], in_specs=[...  26.3 us
    all_gather x1, blocking collectives, shards(): pieces = lax.all_gather(slab_sums, 'dp', axis=0, tiled=True)  20.9 us
    all_gather x1, blocking collectives, shards(): slab_sums = jnp.sum(lax.all_gather(partial_sums, 'mp', axis=0), axis=0)  13.1 us
    all_to_all x3, waiting for transfers between devices, exchange(): return lax.all_to_all(block, axis, split_axis=0, concat_axis=0, tiled=True)  11 us
    ppermute x1, starting transfers between devices, shards(): first_received = lax.ppermute(first_chunks, ('dp', 'mp'), first_pairs)  7.39 us
  transfers between devices with their start and end apart: 5, of which 2 were waited for; matrix products, arithmetic and copies ran while one was open for 0% of the time, Pallas kernels for 11%

profile of v7, /device:TPU:1, one launch (start us, length us, event | category | flops | bytes accessed | tf_op | source)
XLA Modules:
  0.0 111.7 jit_solution(7087909110364437887)
XLA Ops:
  0.6 2.9 %shard_map.139 = bf16[384,1152]{1,0:T(8,128)(2,1)} custom-call(s32[1]{0:T(128)} %bitcast.1.dp_ref, s32[1,16,16]{2,1,0:T(8,128)} %owners_hbm.3, bf16[320,1152]{1,0:T(8,128)(2,1)} %x_hbm.2), custom_call_target="tpu_custom_call" | custom-call | tf_op jit(solution)/shard_map/pallas_call | solution.py:421
  3.5 17.6 %all-to-all-start = ((bf16[16,24,1152]{2,1,0:T(8,128)(2,1)}), bf16[16,24,1152]{2,1,0:T(8,128)(2,1)S(1)}, u32[]{:S(2)}, u32[]{:S(2)}) async-start(bf16[16,24,1152]{2,1,0:T(8,128)(2,1)} %bitcast.3), calls=%async_computation | async-start | bytes 1769472 | tf_op jit(solution)/shard_map/all_to_all | solution.py:437
  21.1 6.0 %shard_map.140 = f32[8,1152]{1,0:T(8,128)S(1)} custom-call(s32[1]{0:T(128)} %bitcast.1.dp_ref, s32[1,8]{1,0:T(1,128)} %counts_hbm.5, bf16[320,1152]{1,0:T(8,128)(2,1)} %x_hbm.2, f32[1152]{0:T(1024)} %gain_hbm.5, f32[1152]{0:T(1024)} %bias_hbm.3, f32[1076]{0:T(1024)} %b1_hbm.3, bf16[1076,1152]{1,0:T(8,128)(2,1)} %bitcast.16, bf16[1076,1152]{1,0:T(8,128)(2,1)} %w2_hbm.3), custom_call_target="tpu_custom_call" | custom-call | flops 793313280 | bytes 4958208 | tf_op jit(solution)/shard_map/pallas_call | solution.py:421
  27.2 13.1 %all-gather = f32[32,1152]{1,0:T(8,128)S(1)} all-gather(f32[8,1152]{1,0:T(8,128)S(1)} %shard_map.140), channel_id=2, replica_groups=mesh['dp'=16,'loss'=16,'mp'=4] {'mp'}, dimensions={0}, use_global_device_ids=true | all-gather | bytes 184320 | tf_op jit(solution)/shard_map/all_gather | solution.py:512
  40.3 0.1 pad_add_fusion.mp_ref
  40.4 5.4 %all-to-all-done = bf16[16,24,1152]{2,1,0:T(8,128)(2,1)S(1)} async-done(((bf16[16,24,1152]{2,1,0:T(8,128)(2,1)}), bf16[16,24,1152]{2,1,0:T(8,128)(2,1)S(1)}, u32[]{:S(2)}, u32[]{:S(2)}) %all-to-all-start) | async-done | bytes 884768 | tf_op jit(solution)/shard_map/all_to_all | solution.py:437
  45.8 4.9 %shard_map.141 = (f32[320,1076]{1,0:T(8,128)S(1)}, bf16[80,1152]{1,0:T(8,128)(2,1)S(1)}, f32[320,8]{1,0:T(8,128)S(1)}, bf16[128,1152]{1,0:T(8,128)(2,1)}) custom-call(s32[1]{0:T(128)} %bitcast.1.dp_ref, s32[2]{0:T(128)S(1)} %pad_add_fusion.mp_ref, bf16[384,1152]{1,0:T(8,128)(2,1)S(1)} %bitcast.13, s32[1,8]{1,0:T(1,128)} %counts_hbm.5, ...), custom_call_target="tpu_custom_call" | custom-call | flops 793313280 | bytes 4958208 | tf_op jit(solution)/shard_map/pallas_call | solution.py:421
  50.7 3.8 %all-to-all-start.1 = ((bf16[16,8,1152]{2,1,0:T(8,128)(2,1)}), bf16[16,8,1152]{2,1,0:T(8,128)(2,1)S(1)}, u32[]{:S(2)}, u32[]{:S(2)}) async-start(bf16[16,8,1152]{2,1,0:T(8,128)(2,1)} %bitcast.7), calls=%async_computation.1 | async-start | bytes 589824 | tf_op jit(solution)/shard_map/all_to_all | solution.py:437
  55.8 20.9 %all_gather.11.pieces_ref = f32[128,1152]{1,0:T(8,128)S(1)} all-gather(f32[8,1152]{1,0:T(8,128)S(1)} %bitcast_reduce_fusion), channel_id=1, replica_groups=mesh['dp'=16,'loss'=16,'mp'=4] {'dp'}, dimensions={0}, use_global_device_ids=true | all-gather | bytes 626688 | tf_op jit(solution)/shard_map/all_gather | solution.py:539
  76.7 0.0 all-to-all-done.1
  76.7 4.2 %shard_map.142 = (f32[8,1152]{1,0:T(8,128)S(1)}, bf16[128,1280]{1,0:T(8,128)(2,1)}, bf16[16,1076]{1,0:T(8,128)(2,1)S(1)}, bf16[160,1152]{1,0:T(8,128)(2,1)S(1)}) custom-call(s32[1]{0:T(128)} %bitcast.2.loss_ref, s32[2]{0:T(128)S(1)} %pad_add_fusion.mp_ref, f32[1]{0:T(128)S(6)} %copy.15.scale_ref, f32[1]{0:T(128)S(6)} %copy.16.shift_ref, ...), custom_call_target="tpu_custom_call" | custom-call | flops 793313280 | bytes 4958208 | tf_op jit(solution)/shard_map/pallas_call | solution.py:421
  80.9 7.4 %collective-permute-start = (bf16[160,1152]{1,0:T(8,128)(2,1)S(1)}, bf16[160,1152]{1,0:T(8,128)(2,1)S(1)}, u32[]{:S(2)}, u32[]{:S(2)}) collective-permute-start(bf16[160,1152]{1,0:T(8,128)(2,1)S(1)} %get-tuple-element.29), channel_id=1, source_target_pairs={{0,1},{1,0},{2,3},{3,2},{64,67},{65,66},{66,65},{67,64},{128,129},... | collective-permute-start | bytes 1105928 | tf_op jit(solution)/shard_map/ppermute | solution.py:561
  88.3 7.6 %all-to-all-start.2 = ((bf16[16,8,1280]{2,1,0:T(8,128)(2,1)}), bf16[16,8,1280]{2,1,0:T(8,128)(2,1)S(1)}, u32[]{:S(2)}, u32[]{:S(2)}) async-start(bf16[16,8,1280]{2,1,0:T(8,128)(2,1)} %bitcast.9), calls=%async_computation.2 | async-start | bytes 655360 | tf_op jit(solution)/shard_map/all_to_all | solution.py:437
  96.0 3.2 %shard_map.144 = f32[80,1152]{1,0:T(8,128)S(1)} custom-call(s32[2]{0:T(128)S(1)} %pad_add_fusion.mp_ref, bf16[16,1076]{1,0:T(8,128)(2,1)S(1)} %get-tuple-element.28.d_act_ref, f32[320,8]{1,0:T(8,128)S(1)} %get-tuple-element.26.member_ref, f32[320,1076]{1,0:T(8,128)S(1)} %get-tuple-element.27.slope_ref, bf16[1076,1152]{1,0:T(8,128)(2,1)} %bitcast.19), custom_call_target="tpu_custom_call" | custom-call | flops 198328320 | bytes 2479104 | tf_op jit(solution)/shard_map/pallas_call | solution.py:421
  99.2 0.0 collective-permute-done.first_ref
  99.2 1.9 %collective-permute-start.1 = (bf16[80,1152]{1,0:T(8,128)(2,1)S(1)}, bf16[80,1152]{1,0:T(8,128)(2,1)S(1)}, u32[]{:S(2)}, u32[]{:S(2)}) collective-permute-start(bf16[80,1152]{1,0:T(8,128)(2,1)S(1)} %add_convert_fusion), channel_id=1, source_target_pairs={{0,3},{1,2},{2,1},{3,0},{64,65},{65,64},{66,67},{67,66},{128,131},... | collective-permute-start | bytes 552968 | tf_op jit(solution)/shard_map/ppermute | solution.py:572
  101.2 5.6 %all-to-all-done.2 = bf16[16,8,1280]{2,1,0:T(8,128)(2,1)S(1)} async-done(((bf16[16,8,1280]{2,1,0:T(8,128)(2,1)}), bf16[16,8,1280]{2,1,0:T(8,128)(2,1)S(1)}, u32[]{:S(2)}, u32[]{:S(2)}) %all-to-all-start.2) | async-done | bytes 327712 | tf_op jit(solution)/shard_map/all_to_all | solution.py:437
  106.7 3.2 %shard_map.143 = (f32[80,1152]{1,0:T(8,128)S(1)}, f32[1,1152]{1,0:T(1,128)S(1)}, f32[8,1152]{1,0:T(8,128)}, f32[1,1]{1,0:T(1,128)}) custom-call(s32[2]{0:T(128)S(1)} %pad_add_fusion.mp_ref, bf16[16,1076]{1,0:T(8,128)(2,1)S(1)} %get-tuple-element.28.d_act_ref, f32[320,8]{1,0:T(8,128)S(1)} %get-tuple-element.26.member_ref, ...), custom_call_target="tpu_custom_call" | custom-call | flops 198328320 | bytes 2479104 | tf_op jit(solution)/shard_map/pallas_call | solution.py:421
  110.0 0.0 collective-permute-done.1.second_ref
  110.0 1.8 %shard_map.145 = f32[80,1152]{1,0:T(8,128)} custom-call(s32[2]{0:T(128)S(1)} %pad_add_fusion.mp_ref, f32[80,1152]{1,0:T(8,128)S(1)} %get-tuple-element.31.back_ref, bf16[80,1152]{1,0:T(8,128)(2,1)S(1)} %collective-permute-done.1.second_ref, bf16[80,1152]{1,0:T(8,128)(2,1)S(1)} %get-tuple-element.32.x_ref, f32[320,8]{1,0:T(8,128)S(1)} %get-tuple-element.26.member_ref, ...), custom_call_target="tpu_custom_call" | custom-call | tf_op jit(solution)/shard_map/pallas_call | solution.py:421
  (2 shorter events, 0.0 us)
Async XLA Ops:
  3.5 42.3 %all-to-all-start = ((bf16[16,24,1152]{2,1,0:T(8,128)(2,1)}), bf16[16,24,1152]{2,1,0:T(8,128)(2,1)S(1)}, u32[]{:S(2)}, u32[]{:S(2)}) async-start(bf16[16,24,1152]{2,1,0:T(8,128)(2,1)} %bitcast.3), calls=%async_computation | async-start | bytes 1769472 | tf_op jit(solution)/shard_map/all_to_all | solution.py:437
  50.7 26.0 %all-to-all-start.1 = ((bf16[16,8,1152]{2,1,0:T(8,128)(2,1)}), bf16[16,8,1152]{2,1,0:T(8,128)(2,1)S(1)}, u32[]{:S(2)}, u32[]{:S(2)}) async-start(bf16[16,8,1152]{2,1,0:T(8,128)(2,1)} %bitcast.7), calls=%async_computation.1 | async-start | bytes 589824 | tf_op jit(solution)/shard_map/all_to_all | solution.py:437
  80.9 18.2 %collective-permute-start = (bf16[160,1152]{1,0:T(8,128)(2,1)S(1)}, bf16[160,1152]{1,0:T(8,128)(2,1)S(1)}, u32[]{:S(2)}, u32[]{:S(2)}) collective-permute-start(bf16[160,1152]{1,0:T(8,128)(2,1)S(1)} %get-tuple-element.29), channel_id=1, source_target_pairs={{0,1},{1,0},{2,3},{3,2},{64,67},{65,66},{66,65},{67,64},{128,129},... | collective-permute-start | bytes 1105928 | tf_op jit(solution)/shard_map/ppermute | solution.py:561
  88.3 18.4 %all-to-all-start.2 = ((bf16[16,8,1280]{2,1,0:T(8,128)(2,1)}), bf16[16,8,1280]{2,1,0:T(8,128)(2,1)S(1)}, u32[]{:S(2)}, u32[]{:S(2)}) async-start(bf16[16,8,1280]{2,1,0:T(8,128)(2,1)} %bitcast.9), calls=%async_computation.2 | async-start | bytes 655360 | tf_op jit(solution)/shard_map/all_to_all | solution.py:437
  99.2 10.7 %collective-permute-start.1 = (bf16[80,1152]{1,0:T(8,128)(2,1)S(1)}, bf16[80,1152]{1,0:T(8,128)(2,1)S(1)}, u32[]{:S(2)}, u32[]{:S(2)}) collective-permute-start(bf16[80,1152]{1,0:T(8,128)(2,1)S(1)} %add_convert_fusion), channel_id=1, source_target_pairs={{0,3},{1,2},{2,1},{3,0},{64,65},{65,64},{66,67},{67,66},{128,131},... | collective-permute-start | bytes 552968 | tf_op jit(solution)/shard_map/ppermute | solution.py:572

commit v8 on v7

--- a/solution.py
+++ b/solution.py
@@ -197,10 +197,7 @@
     b1_ref,
     text_ref,
     w1t_ref,
-    rows_ref,
     semaphores,
-    *,
-    ring,
 ):
     copies = fetch(
         (counts_hbm, owners_hbm.at[0], gain_hbm, bias_hbm, b1_hbm, text_hbm),
@@ -208,7 +205,7 @@
         semaphores,
     )
     firsts = fetch(column_pieces(w1t_hbm, COPY_STEP), column_pieces(w1t_ref, COPY_STEP), semaphores, len(copies))
-    rows = rows_ref.shape[0]
+    rows = slope_ref.shape[0]
     slots = owners_ref.shape[0]
     block_rows = rows // slots
     padded = in_ref.shape[0] // slots
@@ -216,8 +213,11 @@
     within = iota((rows, 1), 0) - source * block_rows
     pick = one_hot(iota((rows, in_ref.shape[0]), 1) == source * padded + within)
     x = jnp.dot(pick, in_ref[...], preferred_element_type=f32)
-    rows_ref[...] = x
-    own_ref[...] = rows_ref[share_range(mp_ref, 0, ring, own_ref.shape[0]), :].astype(bf16)
+    share = own_ref.shape[0]
+    own = mp_ref[0] * share + iota((share, 1), 0)
+    own_source = quotient(own, block_rows)
+    own_pick = one_hot(iota((share, in_ref.shape[0]), 1) == own_source * padded + own - own_source * block_rows)
+    own_ref[...] = jnp.dot(own_pick, in_ref[...], preferred_element_type=f32).astype(bf16)
     wait_all(copies)
     images = member_ref.shape[1]
     text = text_ref[...].astype(f32)
@@ -353,38 +353,16 @@
     return jnp.dot(d_pre, w1t, preferred_element_type=f32)
 
 
-def second_kernel(mp_ref, d_act_ref, member_ref, slope_ref, w1t_hbm, out_ref, w1t_ref, semaphores, *, ring):
+def rest_kernel(mp_ref, d_act_ref, member_ref, slope_ref, w1t_hbm, second_ref, own_ref, w1t_ref, semaphores, *, ring):
     wait_all(fetch(column_pieces(w1t_hbm, COPY_STEP), column_pieces(w1t_ref, COPY_STEP), semaphores))
-    steps = (ring - mp_ref[1],)
-    share = out_ref.shape[0]
-    out_ref[...] = back_of_shares(mp_ref, steps, ring, share, member_ref, d_act_ref[...], slope_ref, w1t_ref)
-
-
-def own_kernel(
-    mp_ref,
-    d_act_ref,
-    member_ref,
-    slope_ref,
-    first_ref,
-    parts_ref,
-    w1t_hbm,
-    gain_hbm,
-    text_hbm,
-    back_ref,
-    gain_row_ref,
-    grad_ref,
-    loss_ref,
-    w1t_ref,
-    gain_ref,
-    text_ref,
-    semaphores,
-    *,
-    ring,
-):
-    copies = fetch((gain_hbm, text_hbm), (gain_ref, text_ref), semaphores)
-    firsts = fetch(column_pieces(w1t_hbm, COPY_STEP), column_pieces(w1t_ref, COPY_STEP), semaphores, len(copies))
-    wait_all(copies)
-    gain_row_ref[...] = gain_ref[...][None, :]
+    steps = (ring - mp_ref[1], 0)
+    share = own_ref.shape[0]
+    back = back_of_shares(mp_ref, steps, ring, share, member_ref, d_act_ref[...], slope_ref, w1t_ref)
+    second_ref[...] = back[:share]
+    own_ref[...] = back[share:]
+
+
+def text_kernel(parts_ref, text_ref, grad_ref, loss_ref):
     text = text_ref[...].astype(f32)
     texts, width = text.shape
     parts = parts_ref[...].astype(f32)
@@ -396,17 +374,31 @@
     dv = total[:, :width]
     grad_ref[...] = (dv - unit * jnp.sum(unit * dv, axis=-1, keepdims=True)) / norm
     loss_ref[...] = jnp.sum(total[:1, width:], axis=1, keepdims=True)
-    wait_all(firsts)
-    share = back_ref.shape[0]
-    own = back_of_shares(mp_ref, (0,), ring, share, member_ref, d_act_ref[...], slope_ref, w1t_ref)
-    back_ref[...] = own + first_ref[:share, :].astype(f32)
-
-
-def row_kernel(mp_ref, back_ref, second_ref, x_ref, member_ref, upstream_ref, gain_ref, out_ref, *, ring):
-    rows = share_range(mp_ref, 0, ring, out_ref.shape[0])
+
+
+def row_kernel(
+    mp_ref,
+    own_ref,
+    first_ref,
+    second_ref,
+    x_ref,
+    member_ref,
+    upstream_ref,
+    gain_hbm,
+    out_ref,
+    gain_ref,
+    semaphores,
+    *,
+    ring,
+):
+    copies = fetch((gain_hbm,), (gain_ref,), semaphores)
+    share = out_ref.shape[0]
+    rows = share_range(mp_ref, 0, ring, share)
     xhat, inverse_deviation = layer_statistics(x_ref[...].astype(f32))
     added = jnp.dot(member_ref[rows, :], upstream_ref[...], precision=HIGHEST, preferred_element_type=f32)
-    dxhat = (back_ref[...] + second_ref[...].astype(f32)) * gain_ref[...]
+    back = own_ref[...] + first_ref[:share, :].astype(f32) + second_ref[...].astype(f32)
+    wait_all(copies)
+    dxhat = back * gain_ref[...][None, :]
     dx = inverse_deviation * (
         dxhat
         - jnp.mean(dxhat, axis=-1, keepdims=True)
@@ -512,7 +504,7 @@
     slab_sums = jnp.sum(lax.all_gather(partial_sums, "mp", axis=0), axis=0)
     incoming, slab_sums = lax.optimization_barrier((incoming, slab_sums))
     slope, own_rows, member, text_copies = call(
-        functools.partial(slope_kernel, ring=mp_size),
+        slope_kernel,
         [
             (whole, shape((row_count, hidden), f32)),
             (whole, shape((share_rows, width), bf16)),
@@ -529,7 +521,6 @@
             offset_room,
             pltpu.VMEM((images, width), bf16),
             first_room,
-            pltpu.VMEM((row_count, width), f32),
         ],
         flops=matmul,
         read=2 * weight_bytes,
@@ -560,30 +551,29 @@
     )
     first_received = lax.ppermute(first_chunks, ("dp", "mp"), first_pairs)
     factors = [(scalars, ring_place)] + [(whole, array) for array in (d_act, member, slope)]
-    (second_chunk,) = call(
-        functools.partial(second_kernel, ring=mp_size),
-        [(whole, shape((share_rows, width), f32))],
+    second_chunk, own_back = call(
+        functools.partial(rest_kernel, ring=mp_size),
+        [(whole, shape((share_rows, width), f32))] * 2,
         factors + [(stored, fc1_t)],
         [first_room],
-        flops=matmul // mp_size,
+        flops=matmul // 2,
         read=weight_bytes,
     )
     second_sum = (second_chunk + first_received[share_rows:].astype(f32)).astype(bf16)
     second_received = lax.ppermute(second_sum, ("dp", "mp"), second_pairs)
     all_parts = exchange(parts, "loss")
-    own_back, gain_row, grad_text, loss = call(
-        functools.partial(own_kernel, ring=mp_size),
-        [(whole, shape(dims, f32)) for dims in ((share_rows, width), (1, width), (images, width), (1, 1))],
-        factors + [(whole, first_received), (whole, all_parts)] + [(stored, array) for array in (fc1_t, gain, text_embed)],
-        [first_room, gain_room, pltpu.VMEM((images, width), bf16)],
-        flops=matmul // mp_size,
-        read=weight_bytes,
+    grad_text, loss = call(
+        text_kernel,
+        [(whole, shape((images, width), f32)), (whole, shape((1, 1), f32))],
+        [(whole, all_parts), (whole, text_embed)],
     )
     (grad_rows,) = call(
         functools.partial(row_kernel, ring=mp_size),
         [(whole, shape((share_rows, width), f32))],
         [(scalars, ring_place)]
-        + [(whole, array) for array in (own_back, second_received, own_rows, member, upstream, gain_row)],
+        + [(whole, array) for array in (own_back, first_received, second_received, own_rows, member, upstream)]
+        + [(stored, gain)],
+        [gain_room],
     )
     return (grad_rows, grad_text, loss[0, 0])
 

time: 112 us -> 113 us (level); the launches traced: 112 us -> 111 us
  Pallas kernels: 26.3 us -> 24.9 us
    ppermute x1, waiting for transfers between devices: 0.01 us -> 5.79 us  [shards(): second_received = lax.ppermute(second_sum, ('dp', 'mp'), second_pairs)]
    all_to_all x3, waiting for transfers between devices: 11 us -> 5.41 us  [exchange(): return lax.all_to_all(block, axis, split_axis=0, concat_axis=0, tiled=True)]
    pallas_call x7, Pallas kernels: 26.3 us -> 24.9 us  [call(): pl.pallas_call(kernel, out_shape=[array for _, array in outs], in_specs=[...]
where the time goes in v8:
time: 113 us; the launch traced here: 111 us
  starting transfers between devices  38.3 us (34%)
  blocking collectives  34 us (30%)
  Pallas kernels  24.9 us (22%)
  waiting for transfers between devices  11.2 us (10%)
  between operations  2.06 us (2%)
    all_to_all x3, starting transfers between devices, exchange(): return lax.all_to_all(block, axis, split_axis=0, concat_axis=0, tiled=True)  29 us
    pallas_call x7, Pallas kernels, call(): pl.pallas_call(kernel, out_shape=[array for _, array in outs], in_specs=[...  24.9 us
    all_gather x1, blocking collectives, shards(): pieces = lax.all_gather(slab_sums, 'dp', axis=0, tiled=True)  20.9 us
    all_gather x1, blocking collectives, shards(): slab_sums = jnp.sum(lax.all_gather(partial_sums, 'mp', axis=0), axis=0)  13.1 us
    ppermute x1, starting transfers between devices, shards(): first_received = lax.ppermute(first_chunks, ('dp', 'mp'), first_pairs)  7.38 us
    ppermute x1, waiting for transfers between devices, shards(): second_received = lax.ppermute(second_sum, ('dp', 'mp'), second_pairs)  5.79 us
    all_to_all x3, waiting for transfers between devices, exchange(): return lax.all_to_all(block, axis, split_axis=0, concat_axis=0, tiled=True)  5.41 us
  transfers between devices with their start and end apart: 5, of which 2 were waited for; matrix products, arithmetic and copies ran while one was open for 0% of the time, Pallas kernels for 11%

profile of v8, /device:TPU:1, one launch (start us, length us, event | category | flops | bytes accessed | tf_op | source)
XLA Modules:
  0.0 110.6 jit_solution(6439070199271544046)
XLA Ops:
  0.6 2.9 %shard_map.139 = bf16[384,1152]{1,0:T(8,128)(2,1)} custom-call(s32[1]{0:T(128)} %bitcast.1.dp_ref, s32[1,16,16]{2,1,0:T(8,128)} %owners_hbm.3, bf16[320,1152]{1,0:T(8,128)(2,1)} %x_hbm.2), custom_call_target="tpu_custom_call" | custom-call | tf_op jit(solution)/shard_map/pallas_call | solution.py:413
  3.5 17.6 %all-to-all-start = ((bf16[16,24,1152]{2,1,0:T(8,128)(2,1)}), bf16[16,24,1152]{2,1,0:T(8,128)(2,1)S(1)}, u32[]{:S(2)}, u32[]{:S(2)}) async-start(bf16[16,24,1152]{2,1,0:T(8,128)(2,1)} %bitcast.3), calls=%async_computation | async-start | bytes 1769472 | tf_op jit(solution)/shard_map/all_to_all | solution.py:429
  21.1 6.0 %shard_map.140 = f32[8,1152]{1,0:T(8,128)S(1)} custom-call(s32[1]{0:T(128)} %bitcast.1.dp_ref, s32[1,8]{1,0:T(1,128)} %counts_hbm.5, bf16[320,1152]{1,0:T(8,128)(2,1)} %x_hbm.2, f32[1152]{0:T(1024)} %gain_hbm.5, f32[1152]{0:T(1024)} %bias_hbm.3, f32[1076]{0:T(1024)} %b1_hbm.3, bf16[1076,1152]{1,0:T(8,128)(2,1)} %bitcast.16, bf16[1076,1152]{1,0:T(8,128)(2,1)} %w2_hbm.3), custom_call_target="tpu_custom_call" | custom-call | flops 793313280 | bytes 4958208 | tf_op jit(solution)/shard_map/pallas_call | solution.py:413
  27.2 13.1 %all-gather = f32[32,1152]{1,0:T(8,128)S(1)} all-gather(f32[8,1152]{1,0:T(8,128)S(1)} %shard_map.140), channel_id=2, replica_groups=mesh['dp'=16,'loss'=16,'mp'=4] {'mp'}, dimensions={0}, use_global_device_ids=true | all-gather | bytes 184320 | tf_op jit(solution)/shard_map/all_gather | solution.py:504
  40.3 0.1 pad_add_fusion.mp_ref
  40.4 5.4 %all-to-all-done = bf16[16,24,1152]{2,1,0:T(8,128)(2,1)S(1)} async-done(((bf16[16,24,1152]{2,1,0:T(8,128)(2,1)}), bf16[16,24,1152]{2,1,0:T(8,128)(2,1)S(1)}, u32[]{:S(2)}, u32[]{:S(2)}) %all-to-all-start) | async-done | bytes 884768 | tf_op jit(solution)/shard_map/all_to_all | solution.py:429
  45.8 5.1 %shard_map.141 = (f32[320,1076]{1,0:T(8,128)S(1)}, bf16[80,1152]{1,0:T(8,128)(2,1)S(1)}, f32[320,8]{1,0:T(8,128)S(1)}, bf16[128,1152]{1,0:T(8,128)(2,1)}) custom-call(s32[1]{0:T(128)} %bitcast.1.dp_ref, s32[2]{0:T(128)S(1)} %pad_add_fusion.mp_ref, bf16[384,1152]{1,0:T(8,128)(2,1)S(1)} %bitcast.13, s32[1,8]{1,0:T(1,128)} %counts_hbm.5, ...), custom_call_target="tpu_custom_call" | custom-call | flops 793313280 | bytes 4958208 | tf_op jit(solution)/shard_map/pallas_call | solution.py:413
  50.9 3.8 %all-to-all-start.1 = ((bf16[16,8,1152]{2,1,0:T(8,128)(2,1)}), bf16[16,8,1152]{2,1,0:T(8,128)(2,1)S(1)}, u32[]{:S(2)}, u32[]{:S(2)}) async-start(bf16[16,8,1152]{2,1,0:T(8,128)(2,1)} %bitcast.7), calls=%async_computation.1 | async-start | bytes 589824 | tf_op jit(solution)/shard_map/all_to_all | solution.py:429
  56.0 20.9 %all_gather.11.pieces_ref = f32[128,1152]{1,0:T(8,128)S(1)} all-gather(f32[8,1152]{1,0:T(8,128)S(1)} %bitcast_reduce_fusion), channel_id=1, replica_groups=mesh['dp'=16,'loss'=16,'mp'=4] {'dp'}, dimensions={0}, use_global_device_ids=true | all-gather | bytes 626688 | tf_op jit(solution)/shard_map/all_gather | solution.py:530
  76.9 0.0 all-to-all-done.1
  76.9 4.2 %shard_map.142 = (f32[8,1152]{1,0:T(8,128)S(1)}, bf16[128,1280]{1,0:T(8,128)(2,1)}, bf16[16,1076]{1,0:T(8,128)(2,1)S(1)}, bf16[160,1152]{1,0:T(8,128)(2,1)S(1)}) custom-call(s32[1]{0:T(128)} %bitcast.2.loss_ref, s32[2]{0:T(128)S(1)} %pad_add_fusion.mp_ref, f32[1]{0:T(128)S(6)} %copy.15.scale_ref, f32[1]{0:T(128)S(6)} %copy.16.shift_ref, ...), custom_call_target="tpu_custom_call" | custom-call | flops 793313280 | bytes 4958208 | tf_op jit(solution)/shard_map/pallas_call | solution.py:413
  81.1 7.4 %collective-permute-start = (bf16[160,1152]{1,0:T(8,128)(2,1)S(1)}, bf16[160,1152]{1,0:T(8,128)(2,1)S(1)}, u32[]{:S(2)}, u32[]{:S(2)}) collective-permute-start(bf16[160,1152]{1,0:T(8,128)(2,1)S(1)} %get-tuple-element.30), channel_id=1, source_target_pairs={{0,1},{1,0},{2,3},{3,2},{64,67},{65,66},{66,65},{67,64},{128,129},... | collective-permute-start | bytes 1105928 | tf_op jit(solution)/shard_map/ppermute | solution.py:552
  88.5 7.7 %all-to-all-start.2 = ((bf16[16,8,1280]{2,1,0:T(8,128)(2,1)}), bf16[16,8,1280]{2,1,0:T(8,128)(2,1)S(1)}, u32[]{:S(2)}, u32[]{:S(2)}) async-start(bf16[16,8,1280]{2,1,0:T(8,128)(2,1)} %bitcast.9), calls=%async_computation.2 | async-start | bytes 655360 | tf_op jit(solution)/shard_map/all_to_all | solution.py:429
  96.1 0.0 copy-start
  96.1 3.3 %shard_map.143 = (f32[80,1152]{1,0:T(8,128)S(1)}, f32[80,1152]{1,0:T(8,128)S(1)}) custom-call(s32[2]{0:T(128)S(1)} %pad_add_fusion.mp_ref, bf16[16,1076]{1,0:T(8,128)(2,1)S(1)} %get-tuple-element.28.d_act_ref, f32[320,8]{1,0:T(8,128)S(1)} %get-tuple-element.26.member_ref, f32[320,1076]{1,0:T(8,128)S(1)} %get-tuple-element.27.slope_ref, ...), custom_call_target="tpu_custom_call" | custom-call | flops 396656640 | bytes 2479104 | tf_op jit(solution)/shard_map/pallas_call | solution.py:413
  99.5 0.0 collective-permute-done.first_ref
  99.5 1.9 %collective-permute-start.1 = (bf16[80,1152]{1,0:T(8,128)(2,1)S(1)}, bf16[80,1152]{1,0:T(8,128)(2,1)S(1)}, u32[]{:S(2)}, u32[]{:S(2)}) collective-permute-start(bf16[80,1152]{1,0:T(8,128)(2,1)S(1)} %add_convert_fusion), channel_id=1, source_target_pairs={{0,3},{1,2},{2,1},{3,0},{64,65},{65,64},{66,67},{67,66},{128,131},... | collective-permute-start | bytes 552968 | tf_op jit(solution)/shard_map/ppermute | solution.py:563
  101.4 5.8 %collective-permute-done.1.second_ref = bf16[80,1152]{1,0:T(8,128)(2,1)S(1)} collective-permute-done((bf16[80,1152]{1,0:T(8,128)(2,1)S(1)}, bf16[80,1152]{1,0:T(8,128)(2,1)S(1)}, u32[]{:S(2)}, u32[]{:S(2)}) %collective-permute-start.1) | collective-permute-done | bytes 184352 | tf_op jit(solution)/shard_map/ppermute | solution.py:563
  107.2 2.6 %shard_map.144 = f32[80,1152]{1,0:T(8,128)} custom-call(s32[2]{0:T(128)S(1)} %pad_add_fusion.mp_ref, f32[80,1152]{1,0:T(8,128)S(1)} %get-tuple-element.29.own_ref, bf16[160,1152]{1,0:T(8,128)(2,1)S(1)} %collective-permute-done.first_ref, bf16[80,1152]{1,0:T(8,128)(2,1)S(1)} %collective-permute-done.1.second_ref, ...), custom_call_target="tpu_custom_call" | custom-call | tf_op jit(solution)/shard_map/pallas_call | solution.py:413
  109.8 0.0 all-to-all-done.2
  109.8 0.0 copy-done
  109.8 0.8 shard_map.145
  (2 shorter events, 0.1 us)
Async XLA Ops:
  3.5 42.3 %all-to-all-start = ((bf16[16,24,1152]{2,1,0:T(8,128)(2,1)}), bf16[16,24,1152]{2,1,0:T(8,128)(2,1)S(1)}, u32[]{:S(2)}, u32[]{:S(2)}) async-start(bf16[16,24,1152]{2,1,0:T(8,128)(2,1)} %bitcast.3), calls=%async_computation | async-start | bytes 1769472 | tf_op jit(solution)/shard_map/all_to_all | solution.py:429
  50.9 26.0 %all-to-all-start.1 = ((bf16[16,8,1152]{2,1,0:T(8,128)(2,1)}), bf16[16,8,1152]{2,1,0:T(8,128)(2,1)S(1)}, u32[]{:S(2)}, u32[]{:S(2)}) async-start(bf16[16,8,1152]{2,1,0:T(8,128)(2,1)} %bitcast.7), calls=%async_computation.1 | async-start | bytes 589824 | tf_op jit(solution)/shard_map/all_to_all | solution.py:429
  81.1 18.4 %collective-permute-start = (bf16[160,1152]{1,0:T(8,128)(2,1)S(1)}, bf16[160,1152]{1,0:T(8,128)(2,1)S(1)}, u32[]{:S(2)}, u32[]{:S(2)}) collective-permute-start(bf16[160,1152]{1,0:T(8,128)(2,1)S(1)} %get-tuple-element.30), channel_id=1, source_target_pairs={{0,1},{1,0},{2,3},{3,2},{64,67},{65,66},{66,65},{67,64},{128,129},... | collective-permute-start | bytes 1105928 | tf_op jit(solution)/shard_map/ppermute | solution.py:552
  88.5 21.3 %all-to-all-start.2 = ((bf16[16,8,1280]{2,1,0:T(8,128)(2,1)}), bf16[16,8,1280]{2,1,0:T(8,128)(2,1)S(1)}, u32[]{:S(2)}, u32[]{:S(2)}) async-start(bf16[16,8,1280]{2,1,0:T(8,128)(2,1)} %bitcast.9), calls=%async_computation.2 | async-start | bytes 655360 | tf_op jit(solution)/shard_map/all_to_all | solution.py:429
  96.1 13.7 %copy-start = (bf16[8,1152]{1,0:T(8,128)(2,1)S(1)}, bf16[8,1152]{1,0:T(8,128)(2,1)}, u32[]{:S(2)}) copy-start(bf16[8,1152]{1,0:T(8,128)(2,1)} %text_ref.1) | copy-start | bytes 55300
  99.5 7.7 %collective-permute-start.1 = (bf16[80,1152]{1,0:T(8,128)(2,1)S(1)}, bf16[80,1152]{1,0:T(8,128)(2,1)S(1)}, u32[]{:S(2)}, u32[]{:S(2)}) collective-permute-start(bf16[80,1152]{1,0:T(8,128)(2,1)S(1)} %add_convert_fusion), channel_id=1, source_target_pairs={{0,3},{1,2},{2,1},{3,0},{64,65},{65,64},{66,67},{67,66},{128,131},... | collective-permute-start | bytes 552968 | tf_op jit(solution)/shard_map/ppermute | solution.py:563
